TPU v7x, 256 devices: a whole 4x4x8 slice. The times are simulated.
256 devices in a mesh: freq: 64 (over x, z, y_lo), rec: 4 (over y_hi, core).
Axes of the slice: x: 4, y: 4 (y_hi: 2, y_lo: 2; y = y_hi * 2 + y_lo), z: 8, core: 2. Of those that a mesh axis runs over, the one named last changes fastest.
Arguments:
- response: bfloat16 [2, 256, 768, 3072], P(None, 'freq', None, 'rec'), may hold values from -0.078125 to 0.078125
- focus_init: bfloat16 [3072, 256, 128], P('rec', 'freq'), may hold values from -6 to 6
- onset_src: int32 [768, 64], replicated, may hold values from 80 to 639
- onset_rec: int32 [3072, 64], P('rec'), may hold values from 80 to 639
Outputs:
- focus_minus: float32 [768, 256, 128], P('rec', 'freq')
- focus_plus: float32 [3072, 256, 128], P('rec', 'freq')
All inputs are finite; a program needn't handle non-finite values.
Results may differ from a plain program's by a relative error of at most 0.0022.
Values may be sent and summed in bfloat16 or wider, within the bound.
No kernel may reach another device: no remote copies, remote signals or barrier semaphores. Data moves between devices by JAX's collectives and lax.ppermute only.
A program may use at most 64 MiB of HBM per device.

v0:
```python
import math

import jax
import jax.numpy as jnp
from jax import lax
from jax.sharding import PartitionSpec as P

NT = 640
ITERS = 2


def tables(nbins):
    bins = jnp.arange(nbins, dtype=jnp.int32) + 1
    samples = jnp.arange(NT, dtype=jnp.int32)
    phase_idx = bins[:, None] * samples[None, :] % NT
    angles = phase_idx.astype(jnp.float32) * (2.0 * math.pi / NT)
    cosine = jnp.cos(angles)
    sine = jnp.sin(angles)
    inverse = jnp.stack([cosine, -sine], axis=1) * (2.0 / NT)
    forward = jnp.stack([cosine, -sine], axis=1)
    return (inverse, forward)


def window(values, onsets, inverse, forward):
    rows, nbins, width = values.shape
    half = width // 2
    split = values.reshape(rows, nbins, 2, half)
    traces = jnp.einsum("rkcp,kcn->rpn", split, inverse, precision=lax.Precision.HIGHEST)
    keep = jnp.arange(NT, dtype=jnp.int32)[None, None, :] < onsets[:, :, None]
    traces = jnp.where(keep, traces, jnp.zeros_like(traces))
    back = jnp.einsum("rpn,kcn->rkcp", traces, forward, precision=lax.Precision.HIGHEST)
    return back.reshape(rows, nbins, width)


def to_time(values):
    return lax.all_to_all(values, "freq", split_axis=0, concat_axis=1, tiled=True)


def to_freq(values):
    return lax.all_to_all(values, "freq", split_axis=1, concat_axis=0, tiled=True)


def forward_terms(response, plus_bf):
    both = jnp.einsum("cksr,rkq->cskq", response, plus_bf, preferred_element_type=jnp.float32)
    half = plus_bf.shape[2] // 2
    real_part = both[0, :, :, :half] - both[1, :, :, half:]
    imag_part = both[0, :, :, half:] + both[1, :, :, :half]
    return jnp.concatenate([real_part, imag_part], axis=2)


def adjoint_terms(response, minus_full):
    both = jnp.einsum("cksr,skq->crkq", response, minus_full, preferred_element_type=jnp.float32)
    half = minus_full.shape[2] // 2
    real_part = both[0, :, :, :half] + both[1, :, :, half:]
    imag_part = both[0, :, :, half:] - both[1, :, :, :half]
    return jnp.concatenate([real_part, imag_part], axis=2)


def body(response, focus_init, onset_src, onset_rec):
    nfreq = lax.axis_size("freq")
    nrec = lax.axis_size("rec")
    freq_pos = lax.axis_index("freq")
    rec_pos = lax.axis_index("rec")
    sources = response.shape[2]
    rec_rows = response.shape[3]
    nbins = response.shape[1] * nfreq
    inverse, forward = tables(nbins)
    plus_bf = focus_init
    minus_out = None
    plus = None
    for step in range(ITERS):
        terms = forward_terms(response, plus_bf)
        ahead = lax.psum(terms, "rec")
        exchanged = to_time(ahead)
        count = sources // nfreq
        onsets = lax.dynamic_slice_in_dim(onset_src, freq_pos * count, count, 0)
        minus_full_f = to_freq(window(exchanged, onsets, inverse, forward))
        block = sources // nrec
        minus_out = lax.dynamic_slice_in_dim(minus_full_f, rec_pos * block, block, 0)
        minus_full = minus_full_f.astype(jnp.bfloat16)
        behind = adjoint_terms(response, minus_full)
        exchanged_rec = to_time(behind)
        rec_count = rec_rows // nfreq
        rec_onsets = lax.dynamic_slice_in_dim(onset_rec, freq_pos * rec_count, rec_count, 0)
        windowed = to_freq(window(exchanged_rec, rec_onsets, inverse, forward))
        plus = focus_init.astype(jnp.float32) + windowed
        plus_bf = plus.astype(jnp.bfloat16)
    return (minus_out, plus)


def solution(mesh):
    return jax.shard_map(
        body,
        mesh=mesh,
        in_specs=(P(None, "freq", None, "rec"), P("rec", "freq", None), P(), P("rec", None)),
        out_specs=(P("rec", "freq", None), P("rec", "freq", None)),
        check_vma=False,
    )
```

profile of v0, /device:TPU:16, one launch (start us, length us, event | category | flops | bytes accessed | tf_op | source)
XLA Modules:
  0.0 641.1 jit_solution(490339716919458848)
XLA Ops:
  7.2 6.0 fusion.24
  13.4 1.3 pad_maximum_fusion
  14.8 57.3 %all-reduce.3.cloned.1.call-done = f32[768,4,128]{0,2,1:T(8,128)} async-done(((f32[768,4,128]{0,2,1:T(8,128)}), f32[768,4,128]{0,2,1:T(8,128)}) %all-reduce.3.cloned.1.call-update) | async-done | bytes 1572880 | tf_op jit(solution)/shard_map/psum | solution.py:73
  72.1 2.6 copy.107
  74.6 11.2 %all-to-all-start = ((f32[768,4,128]{2,1,0:T(4,128)}), f32[768,4,128]{2,1,0:T(4,128)S(1)}, u32[]{:S(2)}, u32[]{:S(2)}) async-start(f32[768,4,128]{2,1,0:T(4,128)} %copy.107), calls=%async_computation | async-start | bytes 3145728 | tf_op jit(solution)/shard_map/all_to_all | solution.py:36
  85.9 1.0 constant_dynamic-slice_fusion.1
  86.9 2.8 fusion.94
  89.7 37.0 %all-to-all-done = f32[768,4,128]{2,1,0:T(4,128)S(1)} async-done(((f32[768,4,128]{2,1,0:T(4,128)}), f32[768,4,128]{2,1,0:T(4,128)S(1)}, u32[]{:S(2)}, u32[]{:S(2)}) %all-to-all-start) | async-done | bytes 1572896 | tf_op jit(solution)/shard_map/all_to_all | solution.py:36
  126.7 1.5 copy.108
  128.2 4.5 reshape.129
  132.8 8.0 %fusion.14 = f32[12,64,640,1]{2,1,3,0:T(8,128)S(1)} fusion(f32[12,256,2,64]{3,2,1,0:T(2,128)} %reshape.129, f32[256,1,640]{2,0,1:T(8,128)S(1)} %get-tuple-element.5, f32[256,1,640]{2,0,1:T(8,128)S(1)} %get-tuple-element.4), kind=kOutput, calls=%fused_computation.14 | convolution fusion | flops 3020554240 | bytes 4849664 | tf_op jit(solution)/shard_map/rkcp,kcn->rpn/dot_general | solution.py:28
  140.8 4.0 fusion.37
  144.8 1.0 copy.111
  145.9 34.0 %all_to_all.123 = bf16[12,256,128]{2,0,1:T(8,128)(2,1)S(1)} all-to-all(bf16[12,256,128]{2,0,1:T(8,128)(2,1)S(1)} %copy.111), channel_id=1, replica_groups=mesh['freq'=64,'rec'=4] {'freq'}, dimensions={1} | all-to-all | bytes 1572864 | tf_op jit(solution)/shard_map/all_to_all | solution.py:40
  179.8 0.2 copy.201
  180.1 0.3 copy.113
  180.3 5.2 fusion.27
  185.7 0.1 pad_maximum_fusion.1
  185.9 1.6 copy.118
  187.4 6.0 all-to-all-start.2
  193.6 39.3 %all-to-all-done.2 = f32[768,4,128]{2,1,0:T(4,128)S(1)} async-done(((f32[768,4,128]{2,1,0:T(4,128)}), f32[768,4,128]{2,1,0:T(4,128)S(1)}, u32[]{:S(2)}, u32[]{:S(2)}) %all-to-all-start.2) | async-done | bytes 1572896 | tf_op jit(solution)/shard_map/all_to_all | solution.py:36
  232.9 1.5 copy.119
  234.4 4.7 reshape.131
  239.1 8.0 %fusion.12 = f32[12,64,640,1]{2,1,3,0:T(8,128)S(1)} fusion(f32[12,256,2,64]{3,2,1,0:T(2,128)} %reshape.131, f32[256,1,640]{2,0,1:T(8,128)S(1)} %get-tuple-element.5, f32[256,1,640]{2,0,1:T(8,128)S(1)} %get-tuple-element.4), kind=kOutput, calls=%fused_computation.12 | convolution fusion | flops 3020554240 | bytes 4849664 | tf_op jit(solution)/shard_map/rkcp,kcn->rpn/dot_general | solution.py:28
  247.1 4.0 fusion.40
  251.1 1.2 copy.121
  252.4 2.1 copy.122
  254.5 56.8 %all_to_all.124 = f32[12,256,128]{2,0,1:T(8,128)S(1)} all-to-all(f32[12,256,128]{2,0,1:T(8,128)S(1)} %copy.122), channel_id=1, replica_groups=mesh['freq'=64,'rec'=4] {'freq'}, dimensions={1} | all-to-all | bytes 3145728 | tf_op jit(solution)/shard_map/all_to_all | solution.py:40
  311.4 0.5 copy.123
  311.9 0.3 copy.124
  312.2 0.8 copy-done.1
  313.0 0.6 fusion.36
  313.6 5.7 fusion.30
  319.5 1.3 pad_maximum_fusion.2
  320.8 50.9 %all-reduce.5.cloned.1.call-done = f32[768,4,128]{0,2,1:T(8,128)} async-done(((f32[768,4,128]{0,2,1:T(8,128)}), f32[768,4,128]{0,2,1:T(8,128)}) %all-reduce.5.cloned.1.call-update) | async-done | bytes 1572880 | tf_op jit(solution)/shard_map/psum | solution.py:73
  371.7 1.8 copy.129
  373.5 52.0 %all_to_all.125 = f32[768,4,128]{2,1,0:T(4,128)S(1)} all-to-all(f32[768,4,128]{2,1,0:T(4,128)S(1)} %copy.129), channel_id=1, replica_groups=mesh['freq'=64,'rec'=4] {'freq'}, dimensions={0} | all-to-all | bytes 3145728 | tf_op jit(solution)/shard_map/all_to_all | solution.py:36
  425.5 0.4 copy.130
  425.8 3.2 reshape.133
  429.1 8.0 %fusion.10 = f32[12,64,640,1]{2,1,3,0:T(8,128)S(1)} fusion(f32[12,256,2,64]{3,2,1,0:T(2,128)} %reshape.133, f32[256,1,640]{2,0,1:T(8,128)S(1)} %get-tuple-element.5, f32[256,1,640]{2,0,1:T(8,128)S(1)} %get-tuple-element.4), kind=kOutput, calls=%fused_computation.10 | convolution fusion | flops 3020554240 | bytes 4849664 | tf_op jit(solution)/shard_map/rkcp,kcn->rpn/dot_general | solution.py:28
  437.1 4.0 fusion.43
  441.1 1.2 copy.132
  442.3 2.1 copy.133
  444.5 56.8 %all_to_all.126 = f32[12,256,128]{2,0,1:T(8,128)S(1)} all-to-all(f32[12,256,128]{2,0,1:T(8,128)S(1)} %copy.133), channel_id=1, replica_groups=mesh['freq'=64,'rec'=4] {'freq'}, dimensions={1} | all-to-all | bytes 3145728 | tf_op jit(solution)/shard_map/all_to_all | solution.py:40
  501.3 0.5 copy.134
  501.8 0.3 copy.135
  502.1 1.4 copy.136
  503.5 5.3 fusion.33
  509.0 0.1 pad_maximum_fusion.3
  509.2 1.6 copy.140
  510.7 45.2 %all_to_all.127 = f32[768,4,128]{2,1,0:T(4,128)S(1)} all-to-all(f32[768,4,128]{2,1,0:T(4,128)} %copy.140), channel_id=1, replica_groups=mesh['freq'=64,'rec'=4] {'freq'}, dimensions={0} | all-to-all | bytes 3145728 | tf_op jit(solution)/shard_map/all_to_all | solution.py:36
  556.0 0.4 copy.141
  556.4 3.2 reshape.135
  559.6 8.0 %fusion.8 = f32[12,64,640,1]{2,1,3,0:T(8,128)S(1)} fusion(f32[12,256,2,64]{3,2,1,0:T(2,128)} %reshape.135, f32[256,1,640]{2,0,1:T(8,128)S(1)} %get-tuple-element.5, f32[256,1,640]{2,0,1:T(8,128)S(1)} %get-tuple-element.4), kind=kOutput, calls=%fused_computation.8 | convolution fusion | flops 3020554240 | bytes 4849664 | tf_op jit(solution)/shard_map/rkcp,kcn->rpn/dot_general | solution.py:28
  567.6 4.0 fusion.46
  571.6 0.1 copy.143
  571.7 1.9 copy.144
  573.6 6.1 all-to-all-start.7
  579.7 1.8 constant_dynamic-slice_fusion
  581.5 49.0 %all-to-all-done.7 = f32[12,256,128]{2,0,1:T(8,128)S(1)} async-done(((f32[12,256,128]{2,0,1:T(8,128)}), f32[12,256,128]{2,0,1:T(8,128)S(1)}, u32[]{:S(2)}, u32[]{:S(2)}) %all-to-all-start.7) | async-done | bytes 1572896 | tf_op jit(solution)/shard_map/all_to_all | solution.py:40
  630.5 0.5 copy.145
  631.0 0.3 copy.146
  631.3 0.8 copy-done.2
  632.1 1.6 convert_add_fusion
  (20 shorter events, 1.0 us)
Async XLA Ops:
  7.2 64.9 %all-reduce.3.cloned.1.call-start = ((), (), s32[]{:S(2)}) async-start(), calls=%async_computation.8 | async-start | bytes 3145728 | tf_op jit(solution)/shard_map/psum | solution.py:73
  74.6 52.1 %all-to-all-start = ((f32[768,4,128]{2,1,0:T(4,128)}), f32[768,4,128]{2,1,0:T(4,128)S(1)}, u32[]{:S(2)}, u32[]{:S(2)}) async-start(f32[768,4,128]{2,1,0:T(4,128)} %copy.107), calls=%async_computation | async-start | bytes 3145728 | tf_op jit(solution)/shard_map/all_to_all | solution.py:36
  187.4 45.5 %all-to-all-start.2 = ((f32[768,4,128]{2,1,0:T(4,128)}), f32[768,4,128]{2,1,0:T(4,128)S(1)}, u32[]{:S(2)}, u32[]{:S(2)}) async-start(f32[768,4,128]{2,1,0:T(4,128)} %copy.118), calls=%async_computation.2 | async-start | bytes 3145728 | tf_op jit(solution)/shard_map/all_to_all | solution.py:36
  193.5 178.2 %all-reduce.5.cloned.1.call-start = ((), (), s32[]{:S(2)}) async-start(), calls=%async_computation.9 | async-start | bytes 3145728 | tf_op jit(solution)/shard_map/psum | solution.py:73
  311.9 1.1 copy-start.1
  502.1 6.8 %copy-start = (f32[64,12,4,128]{3,2,1,0:T(4,128)}, f32[64,12,4,128]{3,2,1,0:T(4,128)S(1)}, u32[]{:S(2)}) copy-start(f32[64,12,4,128]{3,2,1,0:T(4,128)S(1)} %copy.135) | copy-start | bytes 4718596
  573.6 56.8 %all-to-all-start.7 = ((f32[12,256,128]{2,0,1:T(8,128)}), f32[12,256,128]{2,0,1:T(8,128)S(1)}, u32[]{:S(2)}, u32[]{:S(2)}) async-start(f32[12,256,128]{2,0,1:T(8,128)} %copy.144), calls=%async_computation.7 | async-start | bytes 4194304 | tf_op jit(solution)/shard_map/all_to_all | solution.py:40
  631.0 1.1 copy-start.2
Sparse Core Ops, SparseCore 0:
  14.9 57.1 all-reduce.2
  320.9 50.7 all-reduce.4
where the time goes:
time: 648 us; the launch traced here: 641 us
  blocking collectives  245 us (38%)
  waiting for transfers between devices  234 us (36%)
  matrix products  70.2 us (11%)
  local copies, waits for them, and re-layouts  45.7 us (7%)
  starting transfers between devices  23.4 us (4%)
  between operations  14.8 us (2%)
  other arithmetic  8.46 us (1%)
    all_to_all x3, blocking collectives, to_freq(): lax.all_to_all(values, 'freq', split_axis=1, concat_axis=0, tiled=True)  148 us
    psum x2, waiting for transfers between devices, body(): ahead = lax.psum(terms, 'rec')  108 us
    all_to_all x2, blocking collectives, to_time(): lax.all_to_all(values, 'freq', split_axis=0, concat_axis=1, tiled=True)  97.3 us
    all_to_all x2, waiting for transfers between devices, to_time(): lax.all_to_all(values, 'freq', split_axis=0, concat_axis=1, tiled=True)  76.3 us
    all_to_all x1, waiting for transfers between devices, to_freq(): lax.all_to_all(values, 'freq', split_axis=1, concat_axis=0, tiled=True)  49 us
    dot_general x4, matrix products, window(): jnp.einsum('rkcp,kcn->rpn', split, inverse, precision=lax.Precision.HIGHEST)  32 us
    all_to_all x2, starting transfers between devices, to_time(): lax.all_to_all(values, 'freq', split_axis=0, concat_axis=1, tiled=True)  17.3 us
    dot_general x4, matrix products, window(): jnp.einsum('rpn,kcn->rkcp', traces, forward, precision=lax.Precision.HIGH...  15.9 us
  transfers between devices with their start and end apart: 5, of which 5 were waited for; matrix products, arithmetic and copies ran while one was open for 1% of the time, Pallas kernels for 0%

commit v1 on v0

v1 whole, which is shorter than its diff:
```python
import math

import jax
import jax.numpy as jnp
import numpy as np
from jax import lax
from jax.experimental import pallas as pl
from jax.experimental.pallas import tpu as pltpu
from jax.sharding import PartitionSpec as P

NT = 640
ITERS = 2
HALF = 64
FOLD = 336
R_ABS = 0.078125 * math.sqrt(2.0) * 1.001
INIT_ABS = 6.0
TOP = 16384.0
FLOOR = 2.0 ** -14
VMEM_LIMIT = 24 * 1024 * 1024
F32 = jnp.float32
BF16 = jnp.bfloat16
F16 = jnp.float16

CORE_SWAP = [(0, 1), (1, 0), (2, 3), (3, 2)]
HIGH_SWAP = [(0, 2), (2, 0), (1, 3), (3, 1)]


def vmem():
    return pl.BlockSpec(memory_space=pltpu.VMEM)


def smem():
    return pl.BlockSpec(memory_space=pltpu.SMEM)


def call(kernel, out_shape, specs, flops, moved):
    return pl.pallas_call(
        kernel,
        in_specs=specs,
        out_specs=jax.tree.map(lambda _: vmem(), out_shape),
        out_shape=out_shape,
        compiler_params=pltpu.CompilerParams(vmem_limit_bytes=VMEM_LIMIT),
        cost_estimate=pl.CostEstimate(flops=flops, bytes_accessed=moved, transcendentals=0),
    )


def high_low(values):
    values = np.asarray(values, np.float32)
    high = values.astype(jnp.bfloat16)
    return [high, (values - high.astype(np.float32)).astype(jnp.bfloat16)]


def fold_tables(nbins):
    bins = np.arange(nbins, dtype=np.int64) + 1
    samples = np.arange(FOLD, dtype=np.int64)
    angles = ((bins[:, None] * samples[None, :]) % NT).astype(np.float64) * (2.0 * math.pi / NT)
    used = samples[None, :] <= NT // 2
    cosine = np.where(used, np.cos(angles), 0.0)
    sine = np.where(used, np.sin(angles), 0.0)
    forward = np.stack(high_low(cosine) + high_low(sine))
    inverse = np.stack(high_low(cosine.T * (2.0 / NT)) + high_low(sine.T * (2.0 / NT)))
    return forward, inverse


def split_dot(high, low, x):
    x_high = x.astype(BF16)
    x_low = (x - x_high.astype(F32)).astype(BF16)
    total = jnp.dot(high, x_high, preferred_element_type=F32)
    total = total + jnp.dot(high, x_low, preferred_element_type=F32)
    return total + jnp.dot(low, x_high, preferred_element_type=F32)


def window_kernel(with_norm, x_ref, onset_ref, forward_ref, inverse_ref, o_ref):
    blocks, _, lanes = x_ref.shape
    x = x_ref[...].reshape(blocks // 2, 2, 8, lanes)
    even, odd = x[:, 0], x[:, 1]
    first = lax.broadcasted_iota(jnp.int32, even.shape, 1) < 4
    real = jnp.where(first, even, pltpu.roll(odd, 4, 1)).reshape(blocks * 4, lanes)
    imag = jnp.where(first, pltpu.roll(even, 4, 1), odd).reshape(blocks * 4, lanes)
    a = split_dot(inverse_ref[0], inverse_ref[1], real)
    b = split_dot(inverse_ref[2], inverse_ref[3], imag)
    n = lax.broadcasted_iota(jnp.int32, a.shape, 0)
    onset = onset_ref[...]
    near = jnp.where(n < onset, a - b, 0.0)
    far = jnp.where((NT - n < onset) & (n > 0) & (n < NT // 2), a + b, 0.0)
    real = split_dot(forward_ref[0], forward_ref[1], near + far)
    imag = split_dot(forward_ref[2], forward_ref[3], far - near)
    norm = None
    if with_norm:
        norm = jnp.sqrt(jnp.max(jnp.sum(real * real + imag * imag, axis=0, keepdims=True))) * 1.01
    real = real.reshape(blocks // 2, 8, lanes)
    imag = imag.reshape(blocks // 2, 8, lanes)
    even = jnp.where(first, real, pltpu.roll(imag, 4, 1))
    odd = jnp.where(first, pltpu.roll(real, 4, 1), imag)
    if with_norm:
        spare = lax.broadcasted_iota(jnp.int32, even.shape, 2) >= 3 * HALF
        even = jnp.where(spare, norm, even)
        odd = jnp.where(spare, norm, odd)
    o_ref[...] = jnp.concatenate([even[:, None], odd[:, None]], axis=1).reshape(blocks, 8, lanes)


def window_call(x, onsets, tables, with_norm):
    lanes = x.shape[2]
    return call(
        lambda *refs: window_kernel(with_norm, *refs),
        jax.ShapeDtypeStruct(x.shape, F32),
        [vmem()] * 4,
        12 * FOLD * 512 * lanes,
        2 * 4 * x.size,
    )(x, onsets, *tables)


def forward_kernel(picks, order_ref, r_ref, x_ref, o_ref):
    _, bins, block, _ = o_ref.shape
    dims = (((1,), (1,)), ((), ()))
    for k in range(bins):
        x = x_ref[k]
        y = jnp.concatenate([-x[HALF:], x[:HALF]], axis=0)
        starts = [pl.multiple_of(order_ref[pick] * block, HALF) for pick in picks]
        real = jnp.concatenate([r_ref[0, k, pl.ds(at, block), :] for at in starts], axis=0)
        imag = jnp.concatenate([r_ref[1, k, pl.ds(at, block), :] for at in starts], axis=0)
        both = lax.dot_general(real, x, dims, preferred_element_type=F32)
        both = both + lax.dot_general(imag, y, dims, preferred_element_type=F32)
        for i in range(len(picks)):
            o_ref[i, k] = both[i * block : (i + 1) * block]


def forward_call(order, response, plus, picks):
    _, bins, sources, recs = response.shape
    width = plus.shape[1]
    block = sources // 4
    return call(
        lambda *refs: forward_kernel(picks, *refs),
        jax.ShapeDtypeStruct((len(picks), bins, block, width), F32),
        [smem(), vmem(), vmem()],
        4 * bins * len(picks) * block * recs * width,
        4 * bins * len(picks) * block * recs,
    )(order, response, plus)


def adjoint_sum(order_ref, picks, r_ref, parts, k):
    block = r_ref.shape[2] // 4
    m = jnp.concatenate([part[k, :block, :] for part in parts], axis=0).T
    n = jnp.concatenate([m[HALF:], -m[:HALF]], axis=0)
    starts = [pl.multiple_of(order_ref[pick] * block, HALF) for pick in picks]
    real = jnp.concatenate([r_ref[0, k, pl.ds(at, block), :] for at in starts], axis=0)
    imag = jnp.concatenate([r_ref[1, k, pl.ds(at, block), :] for at in starts], axis=0)
    return jnp.dot(m, real, preferred_element_type=F32) + jnp.dot(n, imag, preferred_element_type=F32)


def adjoint_first_kernel(order_ref, r_ref, a_ref, b_ref, o_ref):
    for k in range(r_ref.shape[1]):
        o_ref[k] = adjoint_sum(order_ref, (3, 2), r_ref, (a_ref, b_ref), k)


def adjoint_first(order, response, mine, beside):
    _, bins, sources, recs = response.shape
    width = mine.shape[2]
    return call(
        adjoint_first_kernel,
        jax.ShapeDtypeStruct((bins, width, recs), F32),
        [smem()] + [vmem()] * 3,
        2 * bins * sources * recs * width,
        2 * bins * sources * recs,
    )(order, response, mine, beside)


def adjoint_last_kernel(gain, order_ref, r_ref, total_ref, unit_ref, a_ref, b_ref, c_ref, d_ref, o_ref, bound_ref):
    bins = r_ref.shape[1]
    block = r_ref.shape[2] // 4
    recs = r_ref.shape[3]
    peak = a_ref[0, block:, :]
    for part in (b_ref, c_ref, d_ref):
        peak = jnp.maximum(peak, part[0, block:, :])
    norm = jnp.maximum(jnp.max(peak.astype(F32), axis=0, keepdims=True), FLOOR)
    norm = jnp.broadcast_to(norm * (1.01 * 1.01 * gain), unit_ref.shape) * unit_ref[...]
    bound_ref[...] = norm
    scale = jnp.max(TOP / norm)
    real, imag = [], []
    for k in range(bins):
        both = total_ref[k] + adjoint_sum(order_ref, (1, 0), r_ref, (c_ref, d_ref), k)
        both = both * scale
        real.append(both[:HALF][None])
        imag.append(both[HALF:][None])
    both = jnp.concatenate(real + imag, axis=0)
    o_ref[...] = jnp.transpose(both, (1, 0, 2))


def adjoint_last(order, response, total, unit, parts):
    _, bins, sources, recs = response.shape
    width = total.shape[1]
    gain = sources * R_ABS
    return call(
        lambda *refs: adjoint_last_kernel(gain, *refs),
        (jax.ShapeDtypeStruct((HALF, 2 * bins, recs), F32), jax.ShapeDtypeStruct(unit.shape, F32)),
        [smem()] + [vmem()] * 7,
        2 * bins * sources * recs * width,
        2 * bins * sources * recs,
    )(order, response, total, unit, *parts)


def source_pack_kernel(kept_ref, other_ref, far_ref, scale_ref, o_ref):
    bins, block, width = kept_ref.shape
    scale = scale_ref[0:1, :]
    pieces = {}
    for k in range(bins):
        total = (kept_ref[k] + other_ref[k]) * scale + far_ref[k]
        rows = [total[i * HALF : (i + 1) * HALF] for i in range(3)]
        for c in range(2):
            cut = [row[:, c * HALF : (c + 1) * HALF] for row in rows]
            cut.append(jnp.zeros_like(cut[0]))
            pieces[c, k] = jnp.concatenate(cut, axis=1)[None]
    both = jnp.concatenate([pieces[c, k] for c in range(2) for k in range(bins)], axis=0)
    o_ref[...] = jnp.transpose(both, (1, 0, 2))


def source_pack(kept, other, far, scale):
    bins = kept.shape[0]
    return call(
        source_pack_kernel,
        jax.ShapeDtypeStruct((HALF, 2 * bins, 4 * HALF), F32),
        [vmem()] * 4,
        0,
        16 * kept.size,
    )(kept, other, far, scale)


def source_unpack_kernel(x_ref, unit_ref, o_ref, m_ref):
    bins, block, width = o_ref.shape
    unit = unit_ref[0:1, :]
    both = jnp.transpose(x_ref[...], (1, 0, 2))
    norm = jnp.max(jnp.max(x_ref[:, 0, 3 * HALF :], axis=0, keepdims=True))
    for k in range(bins):
        for i in range(3):
            cut = slice(i * HALF, (i + 1) * HALF)
            rows = jnp.concatenate([both[k][:, cut], both[bins + k][:, cut]], axis=1) * unit
            o_ref[k, cut, :] = rows
            m_ref[k, cut, :] = rows.astype(BF16)
        m_ref[k, block:, :] = jnp.full((16, width), norm, F32).astype(BF16)


def source_unpack(x, unit, bins):
    block, width = 3 * HALF, 2 * HALF
    return call(
        source_unpack_kernel,
        (
            jax.ShapeDtypeStruct((bins, block, width), F32),
            jax.ShapeDtypeStruct((bins, block + 16, width), BF16),
        ),
        [vmem()] * 2,
        0,
        16 * bins * block * width,
    )(x, unit)


def plus_kernel(x_ref, init_ref, unit_ref, o_ref):
    bins, _, recs = init_ref.shape
    unit = jnp.max(unit_ref[...])
    both = jnp.transpose(x_ref[...], (1, 0, 2))
    for k in range(bins):
        rows = jnp.concatenate([both[k], both[bins + k]], axis=0) * unit
        o_ref[k] = (init_ref[k].astype(F32) + rows).astype(BF16)


def plus_call(x, init, unit):
    return call(plus_kernel, jax.ShapeDtypeStruct(init.shape, BF16), [vmem()] * 3, 0, 8 * x.size)(x, init, unit)


def body(response, focus_init, onset_src, onset_rec):
    nfreq = lax.axis_size("freq")
    freq_pos = lax.axis_index("freq")
    rec_pos = lax.axis_index("rec")
    _, bins, sources, recs = response.shape
    width = focus_init.shape[2]
    block = sources // 4
    core, high = rec_pos % 2, rec_pos // 2
    tables = [jnp.asarray(t) for t in fold_tables(bins * nfreq)]

    def place(h, c):
        return h * 2 + c

    order = jnp.stack([place(1 - high, 1 - core), place(1 - high, core), place(high, 1 - core), place(high, core)])
    order = order.astype(jnp.int32)

    rec_onsets = lax.dynamic_slice_in_dim(onset_rec.T, freq_pos, 1, 0)
    rows = rec_pos * block + jnp.arange(3) * HALF + freq_pos
    src_onsets = jnp.concatenate([onset_src[rows].reshape(1, -1), jnp.zeros((1, HALF), jnp.int32)], axis=1)

    def swap(values):
        return lax.all_to_all(values.astype(F16), "freq", split_axis=0, concat_axis=0, tiled=True).astype(F32)

    def step_to(values, pairs):
        return lax.ppermute(values, "rec", pairs)

    init_t = jnp.transpose(focus_init, (1, 2, 0))
    init_norm = math.sqrt(2.0 * bins * nfreq) * INIT_ABS
    rec_gain = 4 * recs * R_ABS

    plus = init_t
    bound = jnp.full((8, 128), rec_gain * init_norm, F32)
    minus_out = None
    plus_out = None
    for step in range(ITERS):
        last = step == ITERS - 1
        scale = TOP / bound
        unit = bound * (1.0 / TOP)
        away = forward_call(order, response, plus, (0,))
        away_other = step_to(away, CORE_SWAP)
        away_mine = forward_call(order, response, plus, (1,))
        coded = ((away_mine + away_other)[0] * scale[0, 0]).astype(F16)
        far = step_to(coded, HIGH_SWAP)
        near = forward_call(order, response, plus, (2, 3))
        near_other = step_to(near[0], CORE_SWAP)
        field = source_pack(near[1], near_other, far.astype(F32), scale)
        field = swap(field)
        field = window_call(field, src_onsets, tables, True)
        minus, mine = source_unpack(swap(field), unit, bins)
        if last:
            minus_out = jnp.transpose(minus, (1, 0, 2))
        beside = step_to(mine, CORE_SWAP)
        across = step_to(mine, HIGH_SWAP)
        total = adjoint_first(order, response, mine, beside)
        corner = step_to(across, CORE_SWAP)
        behind, behind_bound = adjoint_last(order, response, total, unit, (mine, beside, across, corner))
        field = window_call(swap(behind), rec_onsets, tables, False)
        back = swap(field)
        back_unit = behind_bound * (1.0 / TOP)
        if last:
            back = back.reshape(HALF, 2, bins, recs) * back_unit[0, 0]
            back = jnp.transpose(back, (3, 2, 1, 0)).reshape(recs, bins, width)
            plus_out = focus_init.astype(F32) + back
        else:
            plus = plus_call(back, init_t, back_unit)
            bound = rec_gain * (init_norm + behind_bound)
    return (minus_out, plus_out)


def solution(mesh):
    return jax.shard_map(
        body,
        mesh=mesh,
        in_specs=(P(None, "freq", None, "rec"), P("rec", "freq", None), P(), P("rec", None)),
        out_specs=(P("rec", "freq", None), P("rec", "freq", None)),
        check_vma=False,
    )
```

time: 648 us -> 284 us (0.44)
  blocking collectives: 245 us -> 81.7 us
  waiting for transfers between devices: 234 us -> 107 us
  matrix products: 70.2 us -> 0 us
  Pallas kernels: 0 us -> 25.7 us
  local copies, waits for them, and re-layouts: 45.7 us -> 20.7 us
  between operations: 14.8 us -> 1.22 us
  starting transfers between devices: 23.4 us -> 36 us
    all_to_all x5 -> x4, blocking collectives: 245 us -> 81.7 us  [swap(): lax.all_to_all(values.astype(F16), 'freq', split_axis=0, concat_axis=0, t...]
    psum x2 -> x0, waiting for transfers between devices: 108 us -> none  [body(): ahead = lax.psum(terms, 'rec')]
    dot_general x12 -> x0, matrix products: 70.2 us -> none  [the longest x4 32 us: window(): jnp.einsum('rkcp,kcn->rpn', split, inverse, precision=lax.Precision.HIGHEST)]
    all_to_all x3 -> x4, waiting for transfers between devices: 125 us -> 79.8 us  [swap(): lax.all_to_all(values.astype(F16), 'freq', split_axis=0, concat_axis=0, t...]
    ppermute x0 -> x12, waiting for transfers between devices: none -> 27.6 us  [step_to(): return lax.ppermute(values, 'rec', pairs)]
    pallas_call x0 -> x19, Pallas kernels: none -> 25.7 us  [the longest x6 9.03 us: forward_call(): call(lambda *refs: forward_kernel(picks, *refs), jax.ShapeDtypeStruct((le...]
    reshape x8 -> x1, local copies, waits for them, and re-layouts: 23 us -> 0.08 us  [body(): onset_src[rows].reshape(1, -1)]
    unnamed x6 -> x24, local copies, waits for them, and re-layouts: 1.7 us -> 15.4 us
  transfers between devices with their start and end apart: 5 -> 16, of which waited for: 5 -> 8; matrix products, arithmetic and copies ran while one was open for 1% -> 2% of each run, Pallas kernels for 0% -> 3%
where the time goes in v1:
time: 284 us; the launch traced here: 283 us
  waiting for transfers between devices  107 us (38%)
  blocking collectives  81.7 us (29%)
  starting transfers between devices  36 us (13%)
  Pallas kernels  25.7 us (9%)
  local copies, waits for them, and re-layouts  20.7 us (7%)
  other arithmetic  10.1 us (4%)
    all_to_all x4, blocking collectives, swap(): lax.all_to_all(values.astype(F16), 'freq', split_axis=0, concat_axis=0, t...  81.7 us
    all_to_all x4, waiting for transfers between devices, swap(): lax.all_to_all(values.astype(F16), 'freq', split_axis=0, concat_axis=0, t...  79.8 us
    all_to_all x4, starting transfers between devices, swap(): lax.all_to_all(values.astype(F16), 'freq', split_axis=0, concat_axis=0, t...  30.4 us
    ppermute x12, waiting for transfers between devices, step_to(): return lax.ppermute(values, 'rec', pairs)  27.6 us
    unnamed x24, local copies, waits for them, and re-layouts  15.4 us
    pallas_call x6, Pallas kernels, forward_call(): call(lambda *refs: forward_kernel(picks, *refs), jax.ShapeDtypeStruct((le...  9.03 us
    pallas_call x4, Pallas kernels, window_call(): call(lambda *refs: window_kernel(with_norm, *refs), jax.ShapeDtypeStruct(...  7.36 us
  transfers between devices with their start and end apart: 16, of which 8 were waited for; matrix products, arithmetic and copies ran while one was open for 2% of the time, Pallas kernels for 3%

profile of v1, /device:TPU:16, one launch (start us, length us, event | category | flops | bytes accessed | tf_op | source)
XLA Modules:
  0.0 282.8 jit_solution(13019799755686589391)
XLA Ops:
  0.7 1.6 copy.12
  2.4 3.7 %copy-done.1 = bf16[2,4,768,768]{3,2,1,0:T(8,128)(2,1)S(1)} copy-done((bf16[2,4,768,768]{3,2,1,0:T(8,128)(2,1)S(1)}, bf16[2,4,768,768]{3,2,1,0:T(8,128)(2,1)}, u32[]{:S(2)}) %copy-start.1) | copy-done | bytes 9437208
  6.0 1.3 shard_map.79
  7.4 1.9 shard_map.77
  9.4 0.6 collective-permute-start
  10.0 1.3 shard_map.78
  11.4 2.2 collective-permute-start.2
  13.6 6.3 %collective-permute-done.2 = f16[4,192,128]{2,1,0:T(8,128)(2,1)S(1)} collective-permute-done((f16[4,192,128]{2,1,0:T(8,128)(2,1)S(1)}, f16[4,192,128]{2,1,0:T(8,128)(2,1)S(1)}, u32[]{:S(2)}, u32[]{:S(2)}) %collective-permute-start.2) | collective-permute-done | bytes 196640 | tf_op jit(solution)/shard_map/ppermute | solution.py:293
  19.9 0.2 shard_map.80
  20.2 0.7 convert_element_type.72
  20.9 12.7 %all-to-all-start = ((f16[64,8,256]{2,1,0:T(8,128)(2,1)}), f16[64,8,256]{2,1,0:T(8,128)(2,1)S(1)}, u32[]{:S(2)}, u32[]{:S(2)}) async-start(f16[64,8,256]{2,1,0:T(8,128)(2,1)} %convert_element_type.72), calls=%async_computation | async-start | bytes 524288 | tf_op jit(solution)/shard_map/all_to_all | solution.py:290
  33.6 0.2 copy.13
  33.8 0.6 gather_fusion
  34.4 11.0 %all-to-all-done = f16[64,8,256]{2,1,0:T(8,128)(2,1)S(1)} async-done(((f16[64,8,256]{2,1,0:T(8,128)(2,1)}), f16[64,8,256]{2,1,0:T(8,128)(2,1)S(1)}, u32[]{:S(2)}, u32[]{:S(2)}) %all-to-all-start) | async-done | bytes 262176 | tf_op jit(solution)/shard_map/all_to_all | solution.py:290
  45.5 1.3 shard_map.81
  46.8 17.1 %all_to_all.40 = f16[64,8,256]{2,1,0:T(8,128)(2,1)S(1)} all-to-all(f16[64,8,256]{2,1,0:T(8,128)(2,1)S(1)} %convert_element_type.74), channel_id=1, replica_groups=mesh['freq'=64,'rec'=4] {'freq'}, dimensions={0} | all-to-all | bytes 524288 | tf_op jit(solution)/shard_map/all_to_all | solution.py:290
  64.0 1.0 shard_map.82
  65.0 0.6 collective-permute-start.4
  65.6 6.7 %collective-permute-done.4.refs_6_ = bf16[4,208,128]{2,1,0:T(8,128)(2,1)S(1)} collective-permute-done((bf16[4,208,128]{2,1,0:T(8,128)(2,1)S(1)}, bf16[4,208,128]{2,1,0:T(8,128)(2,1)S(1)}, u32[]{:S(2)}, u32[]{:S(2)}) %collective-permute-start.4) | collective-permute-done | bytes 213024 | tf_op jit(solution)/shard_map/ppermute | solution.py:293
  72.3 3.7 %copy-done.2 = bf16[2,4,768,768]{3,2,1,0:T(8,128)(2,1)S(1)} copy-done((bf16[2,4,768,768]{3,2,1,0:T(8,128)(2,1)S(1)}, bf16[2,4,768,768]{3,2,1,0:T(8,128)(2,1)}, u32[]{:S(2)}) %copy-start.2) | copy-done | bytes 9437208
  76.0 1.5 shard_map.83.refs_2_
  77.6 1.8 shard_map.84
  79.4 1.0 convert_element_type.76
  80.4 5.7 %all-to-all-start.2 = ((f16[64,8,768]{2,1,0:T(8,128)(2,1)}), f16[64,8,768]{2,1,0:T(8,128)(2,1)}, u32[]{:S(2)}, u32[]{:S(2)}) async-start(f16[64,8,768]{2,1,0:T(8,128)(2,1)} %convert_element_type.76), calls=%async_computation.2 | async-start | bytes 1572864 | tf_op jit(solution)/shard_map/all_to_all | solution.py:290
  86.1 24.2 %all-to-all-done.2 = f16[64,8,768]{2,1,0:T(8,128)(2,1)} async-done(((f16[64,8,768]{2,1,0:T(8,128)(2,1)}), f16[64,8,768]{2,1,0:T(8,128)(2,1)}, u32[]{:S(2)}, u32[]{:S(2)}) %all-to-all-start.2) | async-done | bytes 786464 | tf_op jit(solution)/shard_map/all_to_all | solution.py:290
  110.3 1.2 convert_element_type.77.refs_0_
  111.6 2.4 shard_map.85
  114.0 1.0 convert_element_type.78
  115.0 6.1 %all-to-all-start.3 = ((f16[64,8,768]{2,1,0:T(8,128)(2,1)}), f16[64,8,768]{2,1,0:T(8,128)(2,1)}, u32[]{:S(2)}, u32[]{:S(2)}) async-start(f16[64,8,768]{2,1,0:T(8,128)(2,1)} %convert_element_type.78), calls=%async_computation.3 | async-start | bytes 1572864 | tf_op jit(solution)/shard_map/all_to_all | solution.py:290
  121.1 23.1 %all-to-all-done.3 = f16[64,8,768]{2,1,0:T(8,128)(2,1)} async-done(((f16[64,8,768]{2,1,0:T(8,128)(2,1)}), f16[64,8,768]{2,1,0:T(8,128)(2,1)}, u32[]{:S(2)}, u32[]{:S(2)}) %all-to-all-start.3) | async-done | bytes 786464 | tf_op jit(solution)/shard_map/all_to_all | solution.py:290
  144.2 1.2 convert_element_type.79.x_ref
  145.4 0.8 shard_map.86.refs_2_
  146.3 3.7 %copy-done.3 = bf16[2,4,768,768]{3,2,1,0:T(8,128)(2,1)S(1)} copy-done((bf16[2,4,768,768]{3,2,1,0:T(8,128)(2,1)S(1)}, bf16[2,4,768,768]{3,2,1,0:T(8,128)(2,1)}, u32[]{:S(2)}) %copy-start.3) | copy-done | bytes 9437208
  149.9 1.3 shard_map.89
  151.3 0.5 slice.22
  151.8 1.9 shard_map.87
  153.9 0.6 collective-permute-start.6
  154.4 1.3 shard_map.88
  155.8 1.2 fusion.1
  156.9 0.7 collective-permute-start.8
  157.6 7.9 %collective-permute-done.8 = f16[4,192,128]{2,1,0:T(8,128)(2,1)S(1)} collective-permute-done((f16[4,192,128]{2,1,0:T(8,128)(2,1)S(1)}, f16[4,192,128]{2,1,0:T(8,128)(2,1)S(1)}, u32[]{:S(2)}, u32[]{:S(2)}) %collective-permute-start.8) | collective-permute-done | bytes 196640 | tf_op jit(solution)/shard_map/ppermute | solution.py:293
  165.6 0.2 shard_map.90
  165.9 17.6 %all_to_all.41 = f16[64,8,256]{2,1,0:T(8,128)(2,1)S(1)} all-to-all(f16[64,8,256]{2,1,0:T(8,128)(2,1)S(1)} %convert_element_type.83), channel_id=1, replica_groups=mesh['freq'=64,'rec'=4] {'freq'}, dimensions={0} | all-to-all | bytes 524288 | tf_op jit(solution)/shard_map/all_to_all | solution.py:290
  183.5 1.3 shard_map.91
  184.9 17.2 %all_to_all.42 = f16[64,8,256]{2,1,0:T(8,128)(2,1)S(1)} all-to-all(f16[64,8,256]{2,1,0:T(8,128)(2,1)S(1)} %convert_element_type.85), channel_id=1, replica_groups=mesh['freq'=64,'rec'=4] {'freq'}, dimensions={0} | all-to-all | bytes 524288 | tf_op jit(solution)/shard_map/all_to_all | solution.py:290
  202.1 0.2 shard_map.92
  202.3 0.7 collective-permute-start.10
  203.1 6.7 %collective-permute-done.10.refs_6_ = bf16[4,208,128]{2,1,0:T(8,128)(2,1)S(1)} collective-permute-done((bf16[4,208,128]{2,1,0:T(8,128)(2,1)S(1)}, bf16[4,208,128]{2,1,0:T(8,128)(2,1)S(1)}, u32[]{:S(2)}, u32[]{:S(2)}) %collective-permute-start.10) | collective-permute-done | bytes 213024 | tf_op jit(solution)/shard_map/ppermute | solution.py:293
  209.8 1.6 shard_map.93.refs_2_
  211.4 1.9 shard_map.94
  213.2 0.1 convert_element_type.88
  213.3 29.7 %all_to_all.43 = f16[64,8,768]{2,1,0:T(8,128)(2,1)S(1)} all-to-all(f16[64,8,768]{2,1,0:T(8,128)(2,1)S(1)} %convert_element_type.88), channel_id=1, replica_groups=mesh['freq'=64,'rec'=4] {'freq'}, dimensions={0} | all-to-all | bytes 1572864 | tf_op jit(solution)/shard_map/all_to_all | solution.py:290
  243.1 0.1 convert_element_type.89.refs_0_
  243.2 2.4 shard_map.95
  245.7 1.0 convert_element_type.90
  246.6 6.0 %all-to-all-start.7 = ((f16[64,8,768]{2,1,0:T(8,128)(2,1)}), f16[64,8,768]{2,1,0:T(8,128)(2,1)}, u32[]{:S(2)}, u32[]{:S(2)}) async-start(f16[64,8,768]{2,1,0:T(8,128)(2,1)} %convert_element_type.90), calls=%async_computation.7 | async-start | bytes 1572864 | tf_op jit(solution)/shard_map/all_to_all | solution.py:290
  252.7 1.0 copy.16
  253.7 0.5 slice.23
  254.2 21.5 %all-to-all-done.7 = f16[64,8,768]{2,1,0:T(8,128)(2,1)} async-done(((f16[64,8,768]{2,1,0:T(8,128)(2,1)}), f16[64,8,768]{2,1,0:T(8,128)(2,1)}, u32[]{:S(2)}, u32[]{:S(2)}) %all-to-all-start.7) | async-done | bytes 786464 | tf_op jit(solution)/shard_map/all_to_all | solution.py:290
  275.7 1.9 convert_multiply_fusion
  277.6 1.6 mul.81
  279.2 1.9 copy.15
  281.1 0.2 bitcast_add_fusion
  281.3 1.6 copy.17
  (54 shorter events, 1.0 us)
Async XLA Ops:
  0.6 85.4 %copy-start = (s32[768,64]{0,1:T(8,128)S(1)}, s32[768,64]{0,1:T(8,128)}, u32[]{:S(2)}) copy-start(s32[768,64]{0,1:T(8,128)} %param.9) | copy-start | bytes 589828
  2.4 3.7 %copy-start.1 = (bf16[2,4,768,768]{3,2,1,0:T(8,128)(2,1)S(1)}, bf16[2,4,768,768]{3,2,1,0:T(8,128)(2,1)}, u32[]{:S(2)}) copy-start(bf16[2,4,768,768]{3,2,1,0:T(8,128)(2,1)} %refs_1_.15) | copy-start | bytes 28311556
  7.3 4.0 %collective-permute-start.1 = (f32[1,4,192,128]{3,2,1,0:T(8,128)S(1)}, f32[1,4,192,128]{3,2,1,0:T(8,128)S(1)}, u32[]{:S(2)}, u32[]{:S(2)}) collective-permute-start(f32[1,4,192,128]{3,2,1,0:T(8,128)S(1)} %shard_map.79), channel_id=1, source_target_pairs={{0,1},{1,0},{2,3},{3,2},{4,5},{5,4},{6,7},{7,6},{8,9},{9,8},{10,11... | collective-permute-start | bytes 1179656 | tf_op jit(solution)/shard_map/ppermute | solution.py:293
  9.4 10.4 %collective-permute-start = (f32[4,192,128]{2,1,0:T(8,128)S(1)}, f32[4,192,128]{2,1,0:T(8,128)S(1)}, u32[]{:S(2)}, u32[]{:S(2)}) collective-permute-start(f32[4,192,128]{2,1,0:T(8,128)S(1)} %get-tuple-element.22), channel_id=1, source_target_pairs={{0,1},{1,0},{2,3},{3,2},{4,5},{5,4},{6,7},{7,6},{8,9},{9,8},{10,11... | collective-permute-start | bytes 1179656 | tf_op jit(solution)/shard_map/ppermute | solution.py:293
  11.4 8.4 %collective-permute-start.2 = (f16[4,192,128]{2,1,0:T(8,128)(2,1)S(1)}, f16[4,192,128]{2,1,0:T(8,128)(2,1)S(1)}, u32[]{:S(2)}, u32[]{:S(2)}) collective-permute-start(f16[4,192,128]{2,1,0:T(8,128)(2,1)S(1)} %fusion), channel_id=1, source_target_pairs={{0,2},{2,0},{1,3},{3,1},{4,6},{6,4},{5,7},{7,5},{8,10},{10,8},{9,1... | collective-permute-start | bytes 589832 | tf_op jit(solution)/shard_map/ppermute | solution.py:293
  19.9 13.7 %copy-start.6 = (s32[768,64]{0,1:T(8,128)S(1)}, s32[768,64]{0,1:T(8,128)}, u32[]{:S(2)}) copy-start(s32[768,64]{0,1:T(8,128)} %param.8) | copy-start | bytes 589828
  20.1 25.3 %copy-start.4 = (bf16[4,256,336]{2,1,0:T(8,128)(2,1)S(1)}, bf16[4,256,336]{2,1,0:T(8,128)(2,1)}, u32[]{:S(2)}) copy-start(bf16[4,256,336]{2,1,0:T(8,128)(2,1)} %constant.63.clone.refs_2_) | copy-start | bytes 2064388
  20.1 25.3 %copy-start.5 = (bf16[4,336,256]{2,1,0:T(8,128)(2,1)S(1)}, bf16[4,336,256]{2,1,0:T(8,128)(2,1)}, u32[]{:S(2)}) copy-start(bf16[4,336,256]{2,1,0:T(8,128)(2,1)} %constant.64.clone.refs_3_) | copy-start | bytes 2064388
  20.9 24.5 %all-to-all-start = ((f16[64,8,256]{2,1,0:T(8,128)(2,1)}), f16[64,8,256]{2,1,0:T(8,128)(2,1)S(1)}, u32[]{:S(2)}, u32[]{:S(2)}) async-start(f16[64,8,256]{2,1,0:T(8,128)(2,1)} %convert_element_type.72), calls=%async_computation | async-start | bytes 524288 | tf_op jit(solution)/shard_map/all_to_all | solution.py:290
  65.0 7.3 %collective-permute-start.4 = (bf16[4,208,128]{2,1,0:T(8,128)(2,1)S(1)}, bf16[4,208,128]{2,1,0:T(8,128)(2,1)S(1)}, u32[]{:S(2)}, u32[]{:S(2)}) collective-permute-start(bf16[4,208,128]{2,1,0:T(8,128)(2,1)S(1)} %get-tuple-element.9.a_ref.refs_4_), channel_id=1, source_target_pairs={{0,2},{2,0},{1,3},{3,1},{4,6},{6,4},{5,7},{7,5},{8,10},{10,8},{9,1... | collective-permute-start | bytes 638984 | tf_op jit(solution)/shard_map/ppermute | solution.py:293
  65.6 6.7 %collective-permute-start.3 = (bf16[4,208,128]{2,1,0:T(8,128)(2,1)S(1)}, bf16[4,208,128]{2,1,0:T(8,128)(2,1)S(1)}, u32[]{:S(2)}, u32[]{:S(2)}) collective-permute-start(bf16[4,208,128]{2,1,0:T(8,128)(2,1)S(1)} %get-tuple-element.9.a_ref.refs_4_), channel_id=1, source_target_pairs={{0,1},{1,0},{2,3},{3,2},{4,5},{5,4},{6,7},{7,6},{8,9},{9,8},{10,11... | collective-permute-start | bytes 638984 | tf_op jit(solution)/shard_map/ppermute | solution.py:293
  72.3 5.2 %collective-permute-start.5 = (bf16[4,208,128]{2,1,0:T(8,128)(2,1)S(1)}, bf16[4,208,128]{2,1,0:T(8,128)(2,1)S(1)}, u32[]{:S(2)}, u32[]{:S(2)}) collective-permute-start(bf16[4,208,128]{2,1,0:T(8,128)(2,1)S(1)} %collective-permute-done.4.refs_6_), channel_id=1, source_target_pairs={{0,1},{1,0},{2,3},{3,2},{4,5},{5,4},{6,7},{7,6},{8,9},{9,8},{10,11... | collective-permute-start | bytes 638984 | tf_op jit(solution)/shard_map/ppermute | solution.py:293
  72.3 3.7 %copy-start.2 = (bf16[2,4,768,768]{3,2,1,0:T(8,128)(2,1)S(1)}, bf16[2,4,768,768]{3,2,1,0:T(8,128)(2,1)}, u32[]{:S(2)}) copy-start(bf16[2,4,768,768]{3,2,1,0:T(8,128)(2,1)} %refs_1_.15) | copy-start | bytes 28311556
  80.4 29.9 %all-to-all-start.2 = ((f16[64,8,768]{2,1,0:T(8,128)(2,1)}), f16[64,8,768]{2,1,0:T(8,128)(2,1)}, u32[]{:S(2)}, u32[]{:S(2)}) async-start(f16[64,8,768]{2,1,0:T(8,128)(2,1)} %convert_element_type.76), calls=%async_computation.2 | async-start | bytes 1572864 | tf_op jit(solution)/shard_map/all_to_all | solution.py:290
  115.0 29.2 %all-to-all-start.3 = ((f16[64,8,768]{2,1,0:T(8,128)(2,1)}), f16[64,8,768]{2,1,0:T(8,128)(2,1)}, u32[]{:S(2)}, u32[]{:S(2)}) async-start(f16[64,8,768]{2,1,0:T(8,128)(2,1)} %convert_element_type.78), calls=%async_computation.3 | async-start | bytes 1572864 | tf_op jit(solution)/shard_map/all_to_all | solution.py:290
  146.2 3.7 %copy-start.3 = (bf16[2,4,768,768]{3,2,1,0:T(8,128)(2,1)S(1)}, bf16[2,4,768,768]{3,2,1,0:T(8,128)(2,1)}, u32[]{:S(2)}) copy-start(bf16[2,4,768,768]{3,2,1,0:T(8,128)(2,1)} %refs_1_.15) | copy-start | bytes 28311556
  151.2 4.5 %collective-permute-start.7 = (f32[1,4,192,128]{3,2,1,0:T(8,128)S(1)}, f32[1,4,192,128]{3,2,1,0:T(8,128)S(1)}, u32[]{:S(2)}, u32[]{:S(2)}) collective-permute-start(f32[1,4,192,128]{3,2,1,0:T(8,128)S(1)} %shard_map.89), channel_id=1, source_target_pairs={{0,1},{1,0},{2,3},{3,2},{4,5},{5,4},{6,7},{7,6},{8,9},{9,8},{10,11... | collective-permute-start | bytes 1179656 | tf_op jit(solution)/shard_map/ppermute | solution.py:293
  153.8 56.0 %slice-start = ((s8[9437184]{0:T(1024)(128)(4,1)}), s8[4194304]{0:T(1024)(128)(4,1)S(1)}, s32[]{:S(2)}) async-start(s8[9437184]{0:T(1024)(128)(4,1)} %bitcast.28), calls=%async_computation.8 | async-start | bytes 8388608
  153.8 55.9 %slice-start.1 = ((s8[9437184]{0:T(1024)(128)(4,1)}), s8[4194304]{0:T(1024)(128)(4,1)S(1)}, s32[]{:S(2)}) async-start(s8[9437184]{0:T(1024)(128)(4,1)} %bitcast.28), calls=%async_computation.9 | async-start | bytes 8388608
  153.9 11.8 %collective-permute-start.6 = (f32[4,192,128]{2,1,0:T(8,128)S(1)}, f32[4,192,128]{2,1,0:T(8,128)S(1)}, u32[]{:S(2)}, u32[]{:S(2)}) collective-permute-start(f32[4,192,128]{2,1,0:T(8,128)S(1)} %get-tuple-element.20), channel_id=1, source_target_pairs={{0,1},{1,0},{2,3},{3,2},{4,5},{5,4},{6,7},{7,6},{8,9},{9,8},{10,11... | collective-permute-start | bytes 1179656 | tf_op jit(solution)/shard_map/ppermute | solution.py:293
  156.9 8.6 %collective-permute-start.8 = (f16[4,192,128]{2,1,0:T(8,128)(2,1)S(1)}, f16[4,192,128]{2,1,0:T(8,128)(2,1)S(1)}, u32[]{:S(2)}, u32[]{:S(2)}) collective-permute-start(f16[4,192,128]{2,1,0:T(8,128)(2,1)S(1)} %fusion.1), channel_id=1, source_target_pairs={{0,2},{2,0},{1,3},{3,1},{4,6},{6,4},{5,7},{7,5},{8,10},{10,8},{9,1... | collective-permute-start | bytes 589832 | tf_op jit(solution)/shard_map/ppermute | solution.py:293
  165.6 44.2 %slice-start.2 = ((s8[9437184]{0:T(1024)(128)(4,1)}), s8[1048576]{0:T(1024)(128)(4,1)S(1)}, s32[]{:S(2)}) async-start(s8[9437184]{0:T(1024)(128)(4,1)} %bitcast.28), calls=%async_computation.10 | async-start | bytes 2097152
  202.3 7.4 %collective-permute-start.10 = (bf16[4,208,128]{2,1,0:T(8,128)(2,1)S(1)}, bf16[4,208,128]{2,1,0:T(8,128)(2,1)S(1)}, u32[]{:S(2)}, u32[]{:S(2)}) collective-permute-start(bf16[4,208,128]{2,1,0:T(8,128)(2,1)S(1)} %get-tuple-element.13.a_ref.refs_4_), channel_id=1, source_target_pairs={{0,2},{2,0},{1,3},{3,1},{4,6},{6,4},{5,7},{7,5},{8,10},{10,8},{9,1... | collective-permute-start | bytes 638984 | tf_op jit(solution)/shard_map/ppermute | solution.py:293
  203.1 6.7 %collective-permute-start.9 = (bf16[4,208,128]{2,1,0:T(8,128)(2,1)S(1)}, bf16[4,208,128]{2,1,0:T(8,128)(2,1)S(1)}, u32[]{:S(2)}, u32[]{:S(2)}) collective-permute-start(bf16[4,208,128]{2,1,0:T(8,128)(2,1)S(1)} %get-tuple-element.13.a_ref.refs_4_), channel_id=1, source_target_pairs={{0,1},{1,0},{2,3},{3,2},{4,5},{5,4},{6,7},{7,6},{8,9},{9,8},{10,11... | collective-permute-start | bytes 638984 | tf_op jit(solution)/shard_map/ppermute | solution.py:293
  209.8 1.6 collective-permute-start.11
  246.6 29.1 %all-to-all-start.7 = ((f16[64,8,768]{2,1,0:T(8,128)(2,1)}), f16[64,8,768]{2,1,0:T(8,128)(2,1)}, u32[]{:S(2)}, u32[]{:S(2)}) async-start(f16[64,8,768]{2,1,0:T(8,128)(2,1)} %convert_element_type.90), calls=%async_computation.7 | async-start | bytes 1572864 | tf_op jit(solution)/shard_map/all_to_all | solution.py:290

commit v2 on v1

--- a/solution.py
+++ b/solution.py
@@ -16,7 +16,7 @@
 INIT_ABS = 6.0
 TOP = 16384.0
 FLOOR = 2.0 ** -14
-VMEM_LIMIT = 24 * 1024 * 1024
+MIB = 1024 * 1024
 F32 = jnp.float32
 BF16 = jnp.bfloat16
 F16 = jnp.float16
@@ -33,13 +33,13 @@
     return pl.BlockSpec(memory_space=pltpu.SMEM)
 
 
-def call(kernel, out_shape, specs, flops, moved):
+def call(kernel, out_shape, specs, flops, moved, limit=8):
     return pl.pallas_call(
         kernel,
         in_specs=specs,
         out_specs=jax.tree.map(lambda _: vmem(), out_shape),
         out_shape=out_shape,
-        compiler_params=pltpu.CompilerParams(vmem_limit_bytes=VMEM_LIMIT),
+        compiler_params=pltpu.CompilerParams(vmem_limit_bytes=limit * MIB),
         cost_estimate=pl.CostEstimate(flops=flops, bytes_accessed=moved, transcendentals=0),
     )
 
@@ -107,22 +107,27 @@
         [vmem()] * 4,
         12 * FOLD * 512 * lanes,
         2 * 4 * x.size,
+        16,
     )(x, onsets, *tables)
 
 
+def forward_bin(picks, order_ref, r_ref, x_ref, o_ref, k):
+    block = o_ref.shape[2]
+    dims = (((1,), (1,)), ((), ()))
+    x = x_ref[k]
+    y = jnp.concatenate([-x[HALF:], x[:HALF]], axis=0)
+    starts = [pl.multiple_of(order_ref[pick] * block, HALF) for pick in picks]
+    real = jnp.concatenate([r_ref[0, k, pl.ds(at, block), :] for at in starts], axis=0)
+    imag = jnp.concatenate([r_ref[1, k, pl.ds(at, block), :] for at in starts], axis=0)
+    both = lax.dot_general(real, x, dims, preferred_element_type=F32)
+    both = both + lax.dot_general(imag, y, dims, preferred_element_type=F32)
+    for i in range(len(picks)):
+        o_ref[i, k] = both[i * block : (i + 1) * block]
+
+
 def forward_kernel(picks, order_ref, r_ref, x_ref, o_ref):
-    _, bins, block, _ = o_ref.shape
-    dims = (((1,), (1,)), ((), ()))
-    for k in range(bins):
-        x = x_ref[k]
-        y = jnp.concatenate([-x[HALF:], x[:HALF]], axis=0)
-        starts = [pl.multiple_of(order_ref[pick] * block, HALF) for pick in picks]
-        real = jnp.concatenate([r_ref[0, k, pl.ds(at, block), :] for at in starts], axis=0)
-        imag = jnp.concatenate([r_ref[1, k, pl.ds(at, block), :] for at in starts], axis=0)
-        both = lax.dot_general(real, x, dims, preferred_element_type=F32)
-        both = both + lax.dot_general(imag, y, dims, preferred_element_type=F32)
-        for i in range(len(picks)):
-            o_ref[i, k] = both[i * block : (i + 1) * block]
+    for k in range(o_ref.shape[1]):
+        forward_bin(picks, order_ref, r_ref, x_ref, o_ref, k)
 
 
 def forward_call(order, response, plus, picks):
@@ -140,7 +145,7 @@
 
 def adjoint_sum(order_ref, picks, r_ref, parts, k):
     block = r_ref.shape[2] // 4
-    m = jnp.concatenate([part[k, :block, :] for part in parts], axis=0).T
+    m = jnp.concatenate([part[k * block : (k + 1) * block, :] for part in parts], axis=0).T
     n = jnp.concatenate([m[HALF:], -m[:HALF]], axis=0)
     starts = [pl.multiple_of(order_ref[pick] * block, HALF) for pick in picks]
     real = jnp.concatenate([r_ref[0, k, pl.ds(at, block), :] for at in starts], axis=0)
@@ -155,7 +160,7 @@
 
 def adjoint_first(order, response, mine, beside):
     _, bins, sources, recs = response.shape
-    width = mine.shape[2]
+    width = mine.shape[1]
     return call(
         adjoint_first_kernel,
         jax.ShapeDtypeStruct((bins, width, recs), F32),
@@ -165,16 +170,35 @@
     )(order, response, mine, beside)
 
 
-def adjoint_last_kernel(gain, order_ref, r_ref, total_ref, unit_ref, a_ref, b_ref, c_ref, d_ref, o_ref, bound_ref):
+def adjoint_last_kernel(
+    gain,
+    rec_gain,
+    init_norm,
+    order_ref,
+    r_ref,
+    total_ref,
+    unit_ref,
+    a_ref,
+    b_ref,
+    c_ref,
+    d_ref,
+    o_ref,
+    back_ref,
+    next_scale_ref,
+    next_unit_ref,
+):
     bins = r_ref.shape[1]
     block = r_ref.shape[2] // 4
     recs = r_ref.shape[3]
-    peak = a_ref[0, block:, :]
+    peak = a_ref[bins * block :, :]
     for part in (b_ref, c_ref, d_ref):
-        peak = jnp.maximum(peak, part[0, block:, :])
+        peak = jnp.maximum(peak, part[bins * block :, :])
     norm = jnp.maximum(jnp.max(peak.astype(F32), axis=0, keepdims=True), FLOOR)
     norm = jnp.broadcast_to(norm * (1.01 * 1.01 * gain), unit_ref.shape) * unit_ref[...]
-    bound_ref[...] = norm
+    back_ref[...] = norm * (1.0 / TOP)
+    after = rec_gain * (init_norm + norm)
+    next_scale_ref[...] = TOP / after
+    next_unit_ref[...] = after * (1.0 / TOP)
     scale = jnp.max(TOP / norm)
     real, imag = [], []
     for k in range(bins):
@@ -186,13 +210,14 @@
     o_ref[...] = jnp.transpose(both, (1, 0, 2))
 
 
-def adjoint_last(order, response, total, unit, parts):
+def adjoint_last(order, response, total, unit, parts, rec_gain, init_norm):
     _, bins, sources, recs = response.shape
     width = total.shape[1]
     gain = sources * R_ABS
-    return call(
-        lambda *refs: adjoint_last_kernel(gain, *refs),
-        (jax.ShapeDtypeStruct((HALF, 2 * bins, recs), F32), jax.ShapeDtypeStruct(unit.shape, F32)),
+    stat = jax.ShapeDtypeStruct(unit.shape, F32)
+    return call(
+        lambda *refs: adjoint_last_kernel(gain, rec_gain, init_norm, *refs),
+        (jax.ShapeDtypeStruct((HALF, 2 * bins, recs), F32), stat, stat, stat),
         [smem()] + [vmem()] * 7,
         2 * bins * sources * recs * width,
         2 * bins * sources * recs,
@@ -200,11 +225,11 @@
 
 
 def source_pack_kernel(kept_ref, other_ref, far_ref, scale_ref, o_ref):
-    bins, block, width = kept_ref.shape
+    _, bins, block, width = kept_ref.shape
     scale = scale_ref[0:1, :]
     pieces = {}
     for k in range(bins):
-        total = (kept_ref[k] + other_ref[k]) * scale + far_ref[k]
+        total = (kept_ref[0, k] + other_ref[1, k]) * scale + far_ref[k]
         rows = [total[i * HALF : (i + 1) * HALF] for i in range(3)]
         for c in range(2):
             cut = [row[:, c * HALF : (c + 1) * HALF] for row in rows]
@@ -215,7 +240,7 @@
 
 
 def source_pack(kept, other, far, scale):
-    bins = kept.shape[0]
+    bins = kept.shape[1]
     return call(
         source_pack_kernel,
         jax.ShapeDtypeStruct((HALF, 2 * bins, 4 * HALF), F32),
@@ -225,8 +250,10 @@
     )(kept, other, far, scale)
 
 
-def source_unpack_kernel(x_ref, unit_ref, o_ref, m_ref):
-    bins, block, width = o_ref.shape
+def source_unpack_kernel(x_ref, unit_ref, m_ref, *outs):
+    bins = x_ref.shape[1] // 2
+    width = m_ref.shape[1]
+    block = 3 * HALF
     unit = unit_ref[0:1, :]
     both = jnp.transpose(x_ref[...], (1, 0, 2))
     norm = jnp.max(jnp.max(x_ref[:, 0, 3 * HALF :], axis=0, keepdims=True))
@@ -234,23 +261,18 @@
         for i in range(3):
             cut = slice(i * HALF, (i + 1) * HALF)
             rows = jnp.concatenate([both[k][:, cut], both[bins + k][:, cut]], axis=1) * unit
-            o_ref[k, cut, :] = rows
-            m_ref[k, cut, :] = rows.astype(BF16)
-        m_ref[k, block:, :] = jnp.full((16, width), norm, F32).astype(BF16)
-
-
-def source_unpack(x, unit, bins):
+            for o_ref in outs:
+                o_ref[cut, k, :] = rows
+            m_ref[k * block + i * HALF : k * block + (i + 1) * HALF, :] = rows.astype(BF16)
+    m_ref[bins * block :, :] = jnp.full((16, width), norm, F32).astype(BF16)
+
+
+def source_unpack(x, unit, bins, full):
     block, width = 3 * HALF, 2 * HALF
-    return call(
-        source_unpack_kernel,
-        (
-            jax.ShapeDtypeStruct((bins, block, width), F32),
-            jax.ShapeDtypeStruct((bins, block + 16, width), BF16),
-        ),
-        [vmem()] * 2,
-        0,
-        16 * bins * block * width,
-    )(x, unit)
+    out = [jax.ShapeDtypeStruct((bins * block + 16, width), BF16)]
+    if full:
+        out.append(jax.ShapeDtypeStruct((block, bins, width), F32))
+    return call(source_unpack_kernel, out, [vmem()] * 2, 0, 16 * bins * block * width)(x, unit)
 
 
 def plus_kernel(x_ref, init_ref, unit_ref, o_ref):
@@ -264,6 +286,21 @@
 
 def plus_call(x, init, unit):
     return call(plus_kernel, jax.ShapeDtypeStruct(init.shape, BF16), [vmem()] * 3, 0, 8 * x.size)(x, init, unit)
+
+
+def final_kernel(x_ref, init_ref, unit_ref, o_ref):
+    bins = init_ref.shape[0]
+    unit = jnp.max(unit_ref[...])
+    both = jnp.transpose(x_ref[...], (1, 0, 2))
+    for k in range(bins):
+        rows = jnp.concatenate([both[k], both[bins + k]], axis=0) * unit
+        o_ref[:, k, :] = (init_ref[k].astype(F32) + rows).T
+
+
+def final_call(x, init, unit):
+    bins, width, recs = init.shape
+    out = jax.ShapeDtypeStruct((recs, bins, width), F32)
+    return call(final_kernel, out, [vmem()] * 3, 0, 8 * x.size)(x, init, unit)
 
 
 def body(response, focus_init, onset_src, onset_rec):
@@ -283,8 +320,8 @@
     order = order.astype(jnp.int32)
 
     rec_onsets = lax.dynamic_slice_in_dim(onset_rec.T, freq_pos, 1, 0)
-    rows = rec_pos * block + jnp.arange(3) * HALF + freq_pos
-    src_onsets = jnp.concatenate([onset_src[rows].reshape(1, -1), jnp.zeros((1, HALF), jnp.int32)], axis=1)
+    mine = lax.dynamic_slice(onset_src.reshape(4, 3, HALF, HALF), (rec_pos, 0, freq_pos, 0), (1, 3, 1, HALF))
+    src_onsets = jnp.concatenate([mine.reshape(1, 3 * HALF), jnp.zeros((1, HALF), jnp.int32)], axis=1)
 
     def swap(values):
         return lax.all_to_all(values.astype(F16), "freq", split_axis=0, concat_axis=0, tiled=True).astype(F32)
@@ -292,46 +329,44 @@
     def step_to(values, pairs):
         return lax.ppermute(values, "rec", pairs)
 
-    init_t = jnp.transpose(focus_init, (1, 2, 0))
     init_norm = math.sqrt(2.0 * bins * nfreq) * INIT_ABS
     rec_gain = 4 * recs * R_ABS
 
+    init_t = jnp.transpose(focus_init, (1, 2, 0))
+    init_t, order, src_onsets, rec_onsets = lax.optimization_barrier((init_t, order, src_onsets, rec_onsets))
     plus = init_t
     bound = jnp.full((8, 128), rec_gain * init_norm, F32)
+    scale, unit = TOP / bound, bound * (1.0 / TOP)
     minus_out = None
     plus_out = None
     for step in range(ITERS):
         last = step == ITERS - 1
-        scale = TOP / bound
-        unit = bound * (1.0 / TOP)
-        away = forward_call(order, response, plus, (0,))
+        away = forward_call(order, response, plus, (0, 2))
         away_other = step_to(away, CORE_SWAP)
         away_mine = forward_call(order, response, plus, (1,))
-        coded = ((away_mine + away_other)[0] * scale[0, 0]).astype(F16)
+        coded = ((away_mine[0] + away_other[0]) * scale[0, 0]).astype(F16)
+        coded, plus = lax.optimization_barrier((coded, plus))
         far = step_to(coded, HIGH_SWAP)
-        near = forward_call(order, response, plus, (2, 3))
-        near_other = step_to(near[0], CORE_SWAP)
-        field = source_pack(near[1], near_other, far.astype(F32), scale)
+        near = forward_call(order, response, plus, (3,))
+        field = source_pack(near, away_other, far.astype(F32), scale)
         field = swap(field)
         field = window_call(field, src_onsets, tables, True)
-        minus, mine = source_unpack(swap(field), unit, bins)
+        mine, *full = source_unpack(swap(field), unit, bins, last)
         if last:
-            minus_out = jnp.transpose(minus, (1, 0, 2))
+            minus_out = full[0]
+        across = step_to(mine, HIGH_SWAP)
         beside = step_to(mine, CORE_SWAP)
-        across = step_to(mine, HIGH_SWAP)
         total = adjoint_first(order, response, mine, beside)
+        across, total = lax.optimization_barrier((across, total))
         corner = step_to(across, CORE_SWAP)
-        behind, behind_bound = adjoint_last(order, response, total, unit, (mine, beside, across, corner))
+        parts = (mine, beside, across, corner)
+        behind, back_unit, scale, unit = adjoint_last(order, response, total, unit, parts, rec_gain, init_norm)
         field = window_call(swap(behind), rec_onsets, tables, False)
         back = swap(field)
-        back_unit = behind_bound * (1.0 / TOP)
         if last:
-            back = back.reshape(HALF, 2, bins, recs) * back_unit[0, 0]
-            back = jnp.transpose(back, (3, 2, 1, 0)).reshape(recs, bins, width)
-            plus_out = focus_init.astype(F32) + back
+            plus_out = final_call(back, init_t, back_unit)
         else:
             plus = plus_call(back, init_t, back_unit)
-            bound = rec_gain * (init_norm + behind_bound)
     return (minus_out, plus_out)
 
 

time: 284 us -> 265 us (0.933)
  blocking collectives: 81.7 us -> 192 us
  waiting for transfers between devices: 107 us -> 29.1 us
  starting transfers between devices: 36 us -> 4.57 us
  local copies, waits for them, and re-layouts: 20.7 us -> 6.49 us
  other arithmetic: 10.1 us -> 2 us
  Pallas kernels: 25.7 us -> 28.9 us
    all_to_all x4 -> x8, blocking collectives: 81.7 us -> 192 us  [swap(): lax.all_to_all(values.astype(F16), 'freq', split_axis=0, concat_axis=0, t...]
    all_to_all x4 -> x0, waiting for transfers between devices: 79.8 us -> none  [swap(): lax.all_to_all(values.astype(F16), 'freq', split_axis=0, concat_axis=0, t...]
    all_to_all x4 -> x0, starting transfers between devices: 30.4 us -> none  [swap(): lax.all_to_all(values.astype(F16), 'freq', split_axis=0, concat_axis=0, t...]
    unnamed x24 -> x17, local copies, waits for them, and re-layouts: 15.4 us -> 4.35 us
    mul x3 -> x1, local copies, waits for them, and re-layouts: 3.52 us -> 0.01 us  [body(): scale, unit = (TOP / bound, bound * (1.0 / TOP))]
    convert_element_type x8, other arithmetic: 3.87 us -> 0.54 us  [swap(): values.astype(F16)]
    pallas_call x4 -> x5, Pallas kernels: 4.93 us -> 8.05 us  [the longest x2 4.24 us: adjoint_last(): call(lambda *refs: adjoint_last_kernel(gain, rec_gain, init_norm, *refs),...]
    ppermute x12 -> x10, waiting for transfers between devices: 27.6 us -> 29.1 us  [step_to(): return lax.ppermute(values, 'rec', pairs)]
  transfers between devices with their start and end apart: 16 -> 10, of which waited for: 8 -> 10; matrix products, arithmetic and copies ran while one was open for 2% -> 0% of each run, Pallas kernels for 3% -> 3%
where the time goes in v2:
time: 265 us; the launch traced here: 264 us
  blocking collectives  192 us (72%)
  waiting for transfers between devices  29.1 us (11%)
  Pallas kernels  28.9 us (11%)
  local copies, waits for them, and re-layouts  6.49 us (2%)
  starting transfers between devices  4.57 us (2%)
    all_to_all x8, blocking collectives, swap(): lax.all_to_all(values.astype(F16), 'freq', split_axis=0, concat_axis=0, t...  192 us
    ppermute x10, waiting for transfers between devices, step_to(): return lax.ppermute(values, 'rec', pairs)  29.1 us
    pallas_call x6, Pallas kernels, forward_call(): call(lambda *refs: forward_kernel(picks, *refs), jax.ShapeDtypeStruct((le...  9.03 us
    pallas_call x4, Pallas kernels, window_call(): call(lambda *refs: window_kernel(with_norm, *refs), jax.ShapeDtypeStruct(...  7.46 us
  transfers between devices with their start and end apart: 10, of which 10 were waited for; matrix products, arithmetic and copies ran while one was open for 0% of the time, Pallas kernels for 3%

profile of v2, /device:TPU:16, one launch (start us, length us, event | category | flops | bytes accessed | tf_op | source)
XLA Modules:
  0.0 264.4 jit_solution(9246373911631248477)
XLA Ops:
  0.6 0.0 copy-start
  0.7 1.3 reshape.19
  2.0 0.1 constant_dynamic-slice_fusion
  2.2 0.1 copy.11
  2.2 0.1 reshape.20
  2.4 0.6 copy.10
  3.0 0.1 pad_add_fusion.refs_0_.order_ref
  3.1 3.7 %copy-done.1 = bf16[2,4,768,768]{3,2,1,0:T(8,128)(2,1)S(1)} copy-done((bf16[2,4,768,768]{3,2,1,0:T(8,128)(2,1)S(1)}, bf16[2,4,768,768]{3,2,1,0:T(8,128)(2,1)}, u32[]{:S(2)}) %copy-start.1) | copy-done | bytes 9437208
  6.8 1.9 shard_map.78
  8.7 0.1 collective-permute-start
  8.8 1.3 shard_map.77
  10.1 1.0 collective-permute-done.other_ref
  11.1 0.1 fusion.4
  11.1 2.2 collective-permute-start.1
  13.3 1.3 shard_map.79.kept_ref
  14.6 5.0 %collective-permute-done.1 = f16[4,192,128]{2,1,0:T(8,128)(2,1)S(1)} collective-permute-done((f16[4,192,128]{2,1,0:T(8,128)(2,1)S(1)}, f16[4,192,128]{2,1,0:T(8,128)(2,1)S(1)}, u32[]{:S(2)}, u32[]{:S(2)}) %collective-permute-start.1) | collective-permute-done | bytes 196640 | tf_op jit(solution)/shard_map/ppermute | solution.py:330
  19.7 0.2 shard_map.80
  20.0 24.4 %all_to_all.40 = f16[64,8,256]{2,1,0:T(8,128)(2,1)S(1)} all-to-all(f16[64,8,256]{2,1,0:T(8,128)(2,1)S(1)} %convert_element_type.69), channel_id=1, replica_groups=mesh['freq'=64,'rec'=4] {'freq'}, dimensions={0} | all-to-all | bytes 524288 | tf_op jit(solution)/shard_map/all_to_all | solution.py:327
  44.5 1.3 shard_map.81
  45.8 17.2 %all_to_all.41 = f16[64,8,256]{2,1,0:T(8,128)(2,1)S(1)} all-to-all(f16[64,8,256]{2,1,0:T(8,128)(2,1)S(1)} %convert_element_type.71), channel_id=1, replica_groups=mesh['freq'=64,'rec'=4] {'freq'}, dimensions={0} | all-to-all | bytes 524288 | tf_op jit(solution)/shard_map/all_to_all | solution.py:327
  63.1 0.2 shard_map.82.a_ref.refs_4_
  63.3 0.1 collective-permute-start.3
  63.4 0.8 collective-permute-start.2
  64.2 0.7 collective-permute-done.3.b_ref.refs_5_
  64.8 1.6 shard_map.83.refs_2_
  66.4 5.9 %collective-permute-done.2.refs_6_ = bf16[784,128]{1,0:T(8,128)(2,1)S(1)} collective-permute-done((bf16[784,128]{1,0:T(8,128)(2,1)S(1)}, bf16[784,128]{1,0:T(8,128)(2,1)S(1)}, u32[]{:S(2)}, u32[]{:S(2)}) %collective-permute-start.2) | collective-permute-done | bytes 200736 | tf_op jit(solution)/shard_map/ppermute | solution.py:330
  72.3 1.4 collective-permute-done.4.refs_7_
  73.8 1.8 shard_map.84
  75.6 0.1 convert_element_type.73
  75.7 29.2 %all_to_all.42 = f16[64,8,768]{2,1,0:T(8,128)(2,1)S(1)} all-to-all(f16[64,8,768]{2,1,0:T(8,128)(2,1)S(1)} %convert_element_type.73), channel_id=1, replica_groups=mesh['freq'=64,'rec'=4] {'freq'}, dimensions={0} | all-to-all | bytes 1572864 | tf_op jit(solution)/shard_map/all_to_all | solution.py:327
  104.9 0.1 convert_element_type.74.refs_0_
  105.0 2.5 shard_map.85
  107.5 0.1 convert_element_type.75
  107.6 28.8 %all_to_all.43 = f16[64,8,768]{2,1,0:T(8,128)(2,1)S(1)} all-to-all(f16[64,8,768]{2,1,0:T(8,128)(2,1)S(1)} %convert_element_type.75), channel_id=1, replica_groups=mesh['freq'=64,'rec'=4] {'freq'}, dimensions={0} | all-to-all | bytes 1572864 | tf_op jit(solution)/shard_map/all_to_all | solution.py:327
  136.3 0.1 convert_element_type.76.x_ref
  136.5 0.8 shard_map.86.refs_2_
  137.3 1.9 shard_map.88
  139.2 0.1 collective-permute-start.5
  139.3 0.5 slice.11
  139.8 1.3 shard_map.87
  141.1 0.4 collective-permute-done.5.other_ref
  141.6 0.7 fusion.5
  142.3 0.7 collective-permute-start.6
  143.0 1.3 shard_map.89.kept_ref
  144.3 6.5 %collective-permute-done.6 = f16[4,192,128]{2,1,0:T(8,128)(2,1)S(1)} collective-permute-done((f16[4,192,128]{2,1,0:T(8,128)(2,1)S(1)}, f16[4,192,128]{2,1,0:T(8,128)(2,1)S(1)}, u32[]{:S(2)}, u32[]{:S(2)}) %collective-permute-start.6) | collective-permute-done | bytes 196640 | tf_op jit(solution)/shard_map/ppermute | solution.py:330
  150.9 0.2 shard_map.90
  151.1 17.5 %all_to_all.44 = f16[64,8,256]{2,1,0:T(8,128)(2,1)S(1)} all-to-all(f16[64,8,256]{2,1,0:T(8,128)(2,1)S(1)} %convert_element_type.80), channel_id=1, replica_groups=mesh['freq'=64,'rec'=4] {'freq'}, dimensions={0} | all-to-all | bytes 524288 | tf_op jit(solution)/shard_map/all_to_all | solution.py:327
  168.6 1.3 shard_map.91
  170.0 17.3 %all_to_all.45 = f16[64,8,256]{2,1,0:T(8,128)(2,1)S(1)} all-to-all(f16[64,8,256]{2,1,0:T(8,128)(2,1)S(1)} %convert_element_type.82), channel_id=1, replica_groups=mesh['freq'=64,'rec'=4] {'freq'}, dimensions={0} | all-to-all | bytes 524288 | tf_op jit(solution)/shard_map/all_to_all | solution.py:327
  187.3 1.1 shard_map.92
  188.4 0.6 collective-permute-start.7
  189.0 0.8 collective-permute-done.8.b_ref.refs_5_
  189.9 1.6 shard_map.93.refs_2_
  191.4 5.9 %collective-permute-done.7.refs_6_ = bf16[784,128]{1,0:T(8,128)(2,1)S(1)} collective-permute-done((bf16[784,128]{1,0:T(8,128)(2,1)S(1)}, bf16[784,128]{1,0:T(8,128)(2,1)S(1)}, u32[]{:S(2)}, u32[]{:S(2)}) %collective-permute-start.7) | collective-permute-done | bytes 200736 | tf_op jit(solution)/shard_map/ppermute | solution.py:330
  197.3 1.4 collective-permute-done.9.refs_7_
  198.8 2.4 shard_map.94
  201.2 0.1 convert_element_type.84
  201.3 29.1 %all_to_all.46 = f16[64,8,768]{2,1,0:T(8,128)(2,1)S(1)} all-to-all(f16[64,8,768]{2,1,0:T(8,128)(2,1)S(1)} %convert_element_type.84), channel_id=1, replica_groups=mesh['freq'=64,'rec'=4] {'freq'}, dimensions={0} | all-to-all | bytes 1572864 | tf_op jit(solution)/shard_map/all_to_all | solution.py:327
  230.4 0.1 convert_element_type.85.refs_0_
  230.5 2.5 shard_map.95
  233.0 0.1 convert_element_type.86
  233.1 28.8 %all_to_all.47 = f16[64,8,768]{2,1,0:T(8,128)(2,1)S(1)} all-to-all(f16[64,8,768]{2,1,0:T(8,128)(2,1)S(1)} %convert_element_type.86), channel_id=1, replica_groups=mesh['freq'=64,'rec'=4] {'freq'}, dimensions={0} | all-to-all | bytes 1572864 | tf_op jit(solution)/shard_map/all_to_all | solution.py:327
  261.9 0.1 convert_element_type.87.x_ref
  262.0 2.4 shard_map.96
  (32 shorter events, 0.4 us)
Async XLA Ops:
  0.6 1.3 copy-start
  0.6 1.7 copy-start.4
  3.1 3.7 %copy-start.1 = (bf16[2,4,768,768]{3,2,1,0:T(8,128)(2,1)S(1)}, bf16[2,4,768,768]{3,2,1,0:T(8,128)(2,1)}, u32[]{:S(2)}) copy-start(bf16[2,4,768,768]{3,2,1,0:T(8,128)(2,1)} %refs_1_.15) | copy-start | bytes 28311556
  6.8 6.5 %slice-start = ((s8[9437184]{0:T(1024)(128)(4,1)}), s8[4194304]{0:T(1024)(128)(4,1)S(1)}, s32[]{:S(2)}) async-start(s8[9437184]{0:T(1024)(128)(4,1)} %bitcast.16), calls=%async_computation.8 | async-start | bytes 8388608
  6.8 6.5 %slice-start.1 = ((s8[9437184]{0:T(1024)(128)(4,1)}), s8[4194304]{0:T(1024)(128)(4,1)S(1)}, s32[]{:S(2)}) async-start(s8[9437184]{0:T(1024)(128)(4,1)} %bitcast.16), calls=%async_computation.9 | async-start | bytes 8388608
  8.7 4.6 %slice-start.2 = ((s8[9437184]{0:T(1024)(128)(4,1)}), s8[1048576]{0:T(1024)(128)(4,1)S(1)}, s32[]{:S(2)}) async-start(s8[9437184]{0:T(1024)(128)(4,1)} %bitcast.16), calls=%async_computation.10 | async-start | bytes 2097152
  8.7 2.4 collective-permute-start
  11.1 8.5 %collective-permute-start.1 = (f16[4,192,128]{2,1,0:T(8,128)(2,1)S(1)}, f16[4,192,128]{2,1,0:T(8,128)(2,1)S(1)}, u32[]{:S(2)}, u32[]{:S(2)}) collective-permute-start(f16[4,192,128]{2,1,0:T(8,128)(2,1)S(1)} %fusion.4), channel_id=1, source_target_pairs={{0,2},{2,0},{1,3},{3,1},{4,6},{6,4},{5,7},{7,5},{8,10},{10,8},{9,1... | collective-permute-start | bytes 589832 | tf_op jit(solution)/shard_map/ppermute | solution.py:330
  19.9 24.5 %copy-start.2 = (bf16[4,256,336]{2,1,0:T(8,128)(2,1)S(1)}, bf16[4,256,336]{2,1,0:T(8,128)(2,1)}, u32[]{:S(2)}) copy-start(bf16[4,256,336]{2,1,0:T(8,128)(2,1)} %constant.49.clone.refs_2_) | copy-start | bytes 2064388
  19.9 24.5 %copy-start.3 = (bf16[4,336,256]{2,1,0:T(8,128)(2,1)S(1)}, bf16[4,336,256]{2,1,0:T(8,128)(2,1)}, u32[]{:S(2)}) copy-start(bf16[4,336,256]{2,1,0:T(8,128)(2,1)} %constant.50.clone.refs_3_) | copy-start | bytes 2064388
  63.3 1.5 collective-permute-start.3
  63.4 8.9 %collective-permute-start.2 = (bf16[784,128]{1,0:T(8,128)(2,1)S(1)}, bf16[784,128]{1,0:T(8,128)(2,1)S(1)}, u32[]{:S(2)}, u32[]{:S(2)}) collective-permute-start(bf16[784,128]{1,0:T(8,128)(2,1)S(1)} %shard_map.82.a_ref.refs_4_), channel_id=1, source_target_pairs={{0,2},{2,0},{1,3},{3,1},{4,6},{6,4},{5,7},{7,5},{8,10},{10,8},{9,1... | collective-permute-start | bytes 602120 | tf_op jit(solution)/shard_map/ppermute | solution.py:330
  72.3 1.4 collective-permute-start.4
  139.2 2.4 collective-permute-start.5
  142.3 8.5 %collective-permute-start.6 = (f16[4,192,128]{2,1,0:T(8,128)(2,1)S(1)}, f16[4,192,128]{2,1,0:T(8,128)(2,1)S(1)}, u32[]{:S(2)}, u32[]{:S(2)}) collective-permute-start(f16[4,192,128]{2,1,0:T(8,128)(2,1)S(1)} %fusion.5), channel_id=1, source_target_pairs={{0,2},{2,0},{1,3},{3,1},{4,6},{6,4},{5,7},{7,5},{8,10},{10,8},{9,1... | collective-permute-start | bytes 589832 | tf_op jit(solution)/shard_map/ppermute | solution.py:330
  188.4 1.4 collective-permute-start.8
  188.4 8.9 %collective-permute-start.7 = (bf16[784,128]{1,0:T(8,128)(2,1)S(1)}, bf16[784,128]{1,0:T(8,128)(2,1)S(1)}, u32[]{:S(2)}, u32[]{:S(2)}) collective-permute-start(bf16[784,128]{1,0:T(8,128)(2,1)S(1)} %get-tuple-element.37.a_ref.refs_4_), channel_id=1, source_target_pairs={{0,2},{2,0},{1,3},{3,1},{4,6},{6,4},{5,7},{7,5},{8,10},{10,8},{9,1... | collective-permute-start | bytes 602120 | tf_op jit(solution)/shard_map/ppermute | solution.py:330
  197.3 1.4 collective-permute-start.9

commit v3 on v2

--- a/solution.py
+++ b/solution.py
@@ -70,13 +70,30 @@
     return total + jnp.dot(low, x_high, preferred_element_type=F32)
 
 
-def window_kernel(with_norm, x_ref, onset_ref, forward_ref, inverse_ref, o_ref):
+def pair_halves(x_ref, first):
     blocks, _, lanes = x_ref.shape
     x = x_ref[...].reshape(blocks // 2, 2, 8, lanes)
     even, odd = x[:, 0], x[:, 1]
-    first = lax.broadcasted_iota(jnp.int32, even.shape, 1) < 4
-    real = jnp.where(first, even, pltpu.roll(odd, 4, 1)).reshape(blocks * 4, lanes)
-    imag = jnp.where(first, pltpu.roll(even, 4, 1), odd).reshape(blocks * 4, lanes)
+    real = jnp.where(first, even, pltpu.roll(odd, 4, 1))
+    imag = jnp.where(first, pltpu.roll(even, 4, 1), odd)
+    return real.reshape(blocks * 4, lanes), imag.reshape(blocks * 4, lanes)
+
+
+def triple_halves(x_ref, first):
+    groups = x_ref.shape[0] // 24
+    x = x_ref[...].reshape(groups, 3, 8, 2 * HALF)
+    a, b, c = x[:, 0], x[:, 1], x[:, 2]
+    first = first[:, :, : 2 * HALF]
+    real = jnp.where(first, a, b).reshape(groups * 8, 2 * HALF)
+    imag = pltpu.roll(jnp.where(first, c, a), 4, 1).reshape(groups * 8, 2 * HALF)
+    rest = jnp.where(first, b, c).reshape(groups * 8, 2 * HALF)
+    return jnp.concatenate([real, rest], axis=1), jnp.concatenate([imag, pltpu.roll(rest, HALF, 1)], axis=1)
+
+
+def window_kernel(from_source, x_ref, onset_ref, forward_ref, inverse_ref, o_ref):
+    blocks, _, lanes = o_ref.shape
+    first = lax.broadcasted_iota(jnp.int32, (blocks // 2, 8, lanes), 1) < 4
+    real, imag = triple_halves(x_ref, first) if from_source else pair_halves(x_ref, first)
     a = split_dot(inverse_ref[0], inverse_ref[1], real)
     b = split_dot(inverse_ref[2], inverse_ref[3], imag)
     n = lax.broadcasted_iota(jnp.int32, a.shape, 0)
@@ -86,24 +103,25 @@
     real = split_dot(forward_ref[0], forward_ref[1], near + far)
     imag = split_dot(forward_ref[2], forward_ref[3], far - near)
     norm = None
-    if with_norm:
+    if from_source:
         norm = jnp.sqrt(jnp.max(jnp.sum(real * real + imag * imag, axis=0, keepdims=True))) * 1.01
     real = real.reshape(blocks // 2, 8, lanes)
     imag = imag.reshape(blocks // 2, 8, lanes)
     even = jnp.where(first, real, pltpu.roll(imag, 4, 1))
     odd = jnp.where(first, pltpu.roll(real, 4, 1), imag)
-    if with_norm:
+    if from_source:
         spare = lax.broadcasted_iota(jnp.int32, even.shape, 2) >= 3 * HALF
         even = jnp.where(spare, norm, even)
         odd = jnp.where(spare, norm, odd)
     o_ref[...] = jnp.concatenate([even[:, None], odd[:, None]], axis=1).reshape(blocks, 8, lanes)
 
 
-def window_call(x, onsets, tables, with_norm):
-    lanes = x.shape[2]
-    return call(
-        lambda *refs: window_kernel(with_norm, *refs),
-        jax.ShapeDtypeStruct(x.shape, F32),
+def window_call(x, onsets, tables, from_source):
+    lanes = onsets.shape[1]
+    blocks = x.shape[0] // 12 if from_source else x.shape[0]
+    return call(
+        lambda *refs: window_kernel(from_source, *refs),
+        jax.ShapeDtypeStruct((blocks, 8, lanes), F32),
         [vmem()] * 4,
         12 * FOLD * 512 * lanes,
         2 * 4 * x.size,
@@ -227,23 +245,19 @@
 def source_pack_kernel(kept_ref, other_ref, far_ref, scale_ref, o_ref):
     _, bins, block, width = kept_ref.shape
     scale = scale_ref[0:1, :]
-    pieces = {}
     for k in range(bins):
         total = (kept_ref[0, k] + other_ref[1, k]) * scale + far_ref[k]
-        rows = [total[i * HALF : (i + 1) * HALF] for i in range(3)]
-        for c in range(2):
-            cut = [row[:, c * HALF : (c + 1) * HALF] for row in rows]
-            cut.append(jnp.zeros_like(cut[0]))
-            pieces[c, k] = jnp.concatenate(cut, axis=1)[None]
-    both = jnp.concatenate([pieces[c, k] for c in range(2) for k in range(bins)], axis=0)
-    o_ref[...] = jnp.transpose(both, (1, 0, 2))
+        a, b = total[:HALF], total[HALF : 2 * HALF]
+        o_ref[:, 0, k, :] = jnp.concatenate([a[:, :HALF], b[:, :HALF]], axis=1)
+        o_ref[:, 1, k, :] = jnp.concatenate([a[:, HALF:], b[:, HALF:]], axis=1)
+        o_ref[:, 2, k, :] = total[2 * HALF :]
 
 
 def source_pack(kept, other, far, scale):
     bins = kept.shape[1]
     return call(
         source_pack_kernel,
-        jax.ShapeDtypeStruct((HALF, 2 * bins, 4 * HALF), F32),
+        jax.ShapeDtypeStruct((HALF, 3, bins, 2 * HALF), F32),
         [vmem()] * 4,
         0,
         16 * kept.size,
@@ -275,17 +289,29 @@
     return call(source_unpack_kernel, out, [vmem()] * 2, 0, 16 * bins * block * width)(x, unit)
 
 
-def plus_kernel(x_ref, init_ref, unit_ref, o_ref):
+def plus_forward_kernel(picks, order_ref, r_ref, back_ref, init_ref, unit_ref, x_ref, o_ref):
     bins, _, recs = init_ref.shape
     unit = jnp.max(unit_ref[...])
-    both = jnp.transpose(x_ref[...], (1, 0, 2))
+    both = jnp.transpose(back_ref[...], (1, 0, 2))
     for k in range(bins):
         rows = jnp.concatenate([both[k], both[bins + k]], axis=0) * unit
-        o_ref[k] = (init_ref[k].astype(F32) + rows).astype(BF16)
-
-
-def plus_call(x, init, unit):
-    return call(plus_kernel, jax.ShapeDtypeStruct(init.shape, BF16), [vmem()] * 3, 0, 8 * x.size)(x, init, unit)
+        x_ref[k] = (init_ref[k].astype(F32) + rows).astype(BF16)
+        forward_bin(picks, order_ref, r_ref, x_ref, o_ref, k)
+
+
+def plus_forward(order, response, back, init, unit, picks):
+    bins, width, recs = init.shape
+    block = response.shape[2] // 4
+    return call(
+        lambda *refs: plus_forward_kernel(picks, *refs),
+        [
+            jax.ShapeDtypeStruct(init.shape, BF16),
+            jax.ShapeDtypeStruct((len(picks), bins, block, width), F32),
+        ],
+        [smem()] + [vmem()] * 4,
+        4 * bins * len(picks) * block * recs * width,
+        4 * bins * len(picks) * block * recs,
+    )(order, response, back, init, unit)
 
 
 def final_kernel(x_ref, init_ref, unit_ref, o_ref):
@@ -335,21 +361,24 @@
     init_t = jnp.transpose(focus_init, (1, 2, 0))
     init_t, order, src_onsets, rec_onsets = lax.optimization_barrier((init_t, order, src_onsets, rec_onsets))
     plus = init_t
-    bound = jnp.full((8, 128), rec_gain * init_norm, F32)
+    bound = jnp.full((1, 128), rec_gain * init_norm, F32)
     scale, unit = TOP / bound, bound * (1.0 / TOP)
     minus_out = None
     plus_out = None
     for step in range(ITERS):
         last = step == ITERS - 1
-        away = forward_call(order, response, plus, (0, 2))
+        if step == 0:
+            away = forward_call(order, response, plus, (0, 2))
+        else:
+            plus, away = plus_forward(order, response, back, init_t, back_unit, (0, 2))
         away_other = step_to(away, CORE_SWAP)
         away_mine = forward_call(order, response, plus, (1,))
-        coded = ((away_mine[0] + away_other[0]) * scale[0, 0]).astype(F16)
+        coded = ((away_mine[0] + away_other[0]) * scale).astype(F16)
         coded, plus = lax.optimization_barrier((coded, plus))
         far = step_to(coded, HIGH_SWAP)
         near = forward_call(order, response, plus, (3,))
         field = source_pack(near, away_other, far.astype(F32), scale)
-        field = swap(field)
+        field = swap(field).reshape(3 * HALF * bins, width)
         field = window_call(field, src_onsets, tables, True)
         mine, *full = source_unpack(swap(field), unit, bins, last)
         if last:
@@ -365,8 +394,6 @@
         back = swap(field)
         if last:
             plus_out = final_call(back, init_t, back_unit)
-        else:
-            plus = plus_call(back, init_t, back_unit)
     return (minus_out, plus_out)
 
 

time: 265 us -> 260 us (0.981)
  blocking collectives: 192 us -> 188 us
    all_to_all x8, blocking collectives: 192 us -> 188 us  [swap(): lax.all_to_all(values.astype(F16), 'freq', split_axis=0, concat_axis=0, t...]
    pallas_call x6 -> x5, Pallas kernels: 9.03 us -> 7.13 us  [forward_call(): call(lambda *refs: forward_kernel(picks, *refs), jax.ShapeDtypeStruct((le...]
where the time goes in v3:
time: 260 us; the launch traced here: 259 us
  blocking collectives  188 us (72%)
  waiting for transfers between devices  29.7 us (11%)
  Pallas kernels  28.4 us (11%)
  local copies, waits for them, and re-layouts  5.98 us (2%)
  starting transfers between devices  4.51 us (2%)
    all_to_all x8, blocking collectives, swap(): lax.all_to_all(values.astype(F16), 'freq', split_axis=0, concat_axis=0, t...  188 us
    ppermute x10, waiting for transfers between devices, step_to(): return lax.ppermute(values, 'rec', pairs)  29.7 us
    pallas_call x4, Pallas kernels, window_call(): call(lambda *refs: window_kernel(from_source, *refs), jax.ShapeDtypeStruc...  7.47 us
    pallas_call x5, Pallas kernels, forward_call(): call(lambda *refs: forward_kernel(picks, *refs), jax.ShapeDtypeStruct((le...  7.13 us
  transfers between devices with their start and end apart: 10, of which 10 were waited for; matrix products, arithmetic and copies ran while one was open for 0% of the time, Pallas kernels for 3%

profile of v3, /device:TPU:16, one launch (start us, length us, event | category | flops | bytes accessed | tf_op | source)
XLA Modules:
  0.0 259.2 jit_solution(167785812598762364)
XLA Ops:
  0.6 0.0 copy-start
  0.7 1.3 reshape.27
  2.0 0.1 constant_dynamic-slice_fusion
  2.2 0.1 copy.11
  2.2 0.1 reshape.28
  2.4 0.6 copy.10
  3.0 0.1 pad_add_fusion.refs_0_.order_ref
  3.1 3.7 %copy-done.1 = bf16[2,4,768,768]{3,2,1,0:T(8,128)(2,1)S(1)} copy-done((bf16[2,4,768,768]{3,2,1,0:T(8,128)(2,1)S(1)}, bf16[2,4,768,768]{3,2,1,0:T(8,128)(2,1)}, u32[]{:S(2)}) %copy-start.1) | copy-done | bytes 9437208
  6.8 1.9 shard_map.78
  8.7 0.1 collective-permute-start
  8.8 1.3 shard_map.77
  10.1 1.0 collective-permute-done.other_ref
  11.1 0.1 fusion.5
  11.1 2.2 collective-permute-start.1
  13.3 1.3 shard_map.79.kept_ref
  14.6 5.0 %collective-permute-done.1 = f16[4,192,128]{2,1,0:T(8,128)(2,1)S(1)} collective-permute-done((f16[4,192,128]{2,1,0:T(8,128)(2,1)S(1)}, f16[4,192,128]{2,1,0:T(8,128)(2,1)S(1)}, u32[]{:S(2)}, u32[]{:S(2)}) %collective-permute-start.1) | collective-permute-done | bytes 196640 | tf_op jit(solution)/shard_map/ppermute | solution.py:356
  19.7 0.3 shard_map.80
  20.0 0.1 convert_element_type.62
  20.1 23.7 %all_to_all.40 = f16[64,3,4,128]{3,2,1,0:T(4,128)(2,1)S(1)} all-to-all(f16[64,3,4,128]{3,2,1,0:T(4,128)(2,1)S(1)} %convert_element_type.62), channel_id=1, replica_groups=mesh['freq'=64,'rec'=4] {'freq'}, dimensions={0} | all-to-all | bytes 393216 | tf_op jit(solution)/shard_map/all_to_all | solution.py:353
  43.9 1.3 shard_map.81
  45.2 16.3 %all_to_all.41 = f16[64,8,256]{2,1,0:T(8,128)(2,1)S(1)} all-to-all(f16[64,8,256]{2,1,0:T(8,128)(2,1)S(1)} %convert_element_type.63), channel_id=1, replica_groups=mesh['freq'=64,'rec'=4] {'freq'}, dimensions={0} | all-to-all | bytes 524288 | tf_op jit(solution)/shard_map/all_to_all | solution.py:353
  61.6 0.2 shard_map.82.a_ref.refs_4_
  61.8 0.1 collective-permute-start.3
  61.9 0.7 collective-permute-start.2
  62.6 0.7 collective-permute-done.3.b_ref.refs_5_
  63.4 1.5 shard_map.83.refs_2_
  64.9 5.9 %collective-permute-done.2.refs_6_ = bf16[784,128]{1,0:T(8,128)(2,1)S(1)} collective-permute-done((bf16[784,128]{1,0:T(8,128)(2,1)S(1)}, bf16[784,128]{1,0:T(8,128)(2,1)S(1)}, u32[]{:S(2)}, u32[]{:S(2)}) %collective-permute-start.2) | collective-permute-done | bytes 200736 | tf_op jit(solution)/shard_map/ppermute | solution.py:356
  70.8 1.4 collective-permute-done.4.refs_7_
  72.3 1.8 shard_map.84
  74.1 0.1 convert_element_type.65
  74.2 28.7 %all_to_all.42 = f16[64,8,768]{2,1,0:T(8,128)(2,1)S(1)} all-to-all(f16[64,8,768]{2,1,0:T(8,128)(2,1)S(1)} %convert_element_type.65), channel_id=1, replica_groups=mesh['freq'=64,'rec'=4] {'freq'}, dimensions={0} | all-to-all | bytes 1572864 | tf_op jit(solution)/shard_map/all_to_all | solution.py:353
  102.9 0.1 convert_element_type.66.refs_0_
  103.0 2.5 shard_map.85
  105.5 0.1 convert_element_type.67
  105.6 28.8 %all_to_all.43 = f16[64,8,768]{2,1,0:T(8,128)(2,1)S(1)} all-to-all(f16[64,8,768]{2,1,0:T(8,128)(2,1)S(1)} %convert_element_type.67), channel_id=1, replica_groups=mesh['freq'=64,'rec'=4] {'freq'}, dimensions={0} | all-to-all | bytes 1572864 | tf_op jit(solution)/shard_map/all_to_all | solution.py:353
  134.4 0.1 convert_element_type.68.refs_2_
  134.5 2.1 shard_map.86
  136.6 0.1 collective-permute-start.5
  136.7 1.3 shard_map.87
  138.1 1.0 collective-permute-done.5.other_ref
  139.0 0.1 fusion.2
  139.1 0.7 collective-permute-start.6
  139.8 1.3 shard_map.88.kept_ref
  141.1 6.5 %collective-permute-done.6 = f16[4,192,128]{2,1,0:T(8,128)(2,1)S(1)} collective-permute-done((f16[4,192,128]{2,1,0:T(8,128)(2,1)S(1)}, f16[4,192,128]{2,1,0:T(8,128)(2,1)S(1)}, u32[]{:S(2)}, u32[]{:S(2)}) %collective-permute-start.6) | collective-permute-done | bytes 196640 | tf_op jit(solution)/shard_map/ppermute | solution.py:356
  147.7 0.3 shard_map.89
  148.0 0.1 convert_element_type.71
  148.1 16.8 %all_to_all.44 = f16[64,3,4,128]{3,2,1,0:T(4,128)(2,1)S(1)} all-to-all(f16[64,3,4,128]{3,2,1,0:T(4,128)(2,1)S(1)} %convert_element_type.71), channel_id=1, replica_groups=mesh['freq'=64,'rec'=4] {'freq'}, dimensions={0} | all-to-all | bytes 393216 | tf_op jit(solution)/shard_map/all_to_all | solution.py:353
  164.8 1.3 shard_map.90
  166.2 16.3 %all_to_all.45 = f16[64,8,256]{2,1,0:T(8,128)(2,1)S(1)} all-to-all(f16[64,8,256]{2,1,0:T(8,128)(2,1)S(1)} %convert_element_type.72), channel_id=1, replica_groups=mesh['freq'=64,'rec'=4] {'freq'}, dimensions={0} | all-to-all | bytes 524288 | tf_op jit(solution)/shard_map/all_to_all | solution.py:353
  182.5 1.1 shard_map.91
  183.7 0.6 collective-permute-start.7
  184.3 0.8 collective-permute-done.8.b_ref.refs_5_
  185.1 1.6 shard_map.92.refs_2_
  186.7 5.9 %collective-permute-done.7.refs_6_ = bf16[784,128]{1,0:T(8,128)(2,1)S(1)} collective-permute-done((bf16[784,128]{1,0:T(8,128)(2,1)S(1)}, bf16[784,128]{1,0:T(8,128)(2,1)S(1)}, u32[]{:S(2)}, u32[]{:S(2)}) %collective-permute-start.7) | collective-permute-done | bytes 200736 | tf_op jit(solution)/shard_map/ppermute | solution.py:356
  192.6 1.4 collective-permute-done.9.refs_7_
  194.0 2.4 shard_map.93
  196.4 0.1 convert_element_type.74
  196.5 28.7 %all_to_all.46 = f16[64,8,768]{2,1,0:T(8,128)(2,1)S(1)} all-to-all(f16[64,8,768]{2,1,0:T(8,128)(2,1)S(1)} %convert_element_type.74), channel_id=1, replica_groups=mesh['freq'=64,'rec'=4] {'freq'}, dimensions={0} | all-to-all | bytes 1572864 | tf_op jit(solution)/shard_map/all_to_all | solution.py:353
  225.2 0.1 convert_element_type.75.refs_0_
  225.3 2.5 shard_map.94
  227.8 0.1 convert_element_type.76
  227.9 28.8 %all_to_all.47 = f16[64,8,768]{2,1,0:T(8,128)(2,1)S(1)} all-to-all(f16[64,8,768]{2,1,0:T(8,128)(2,1)S(1)} %convert_element_type.76), channel_id=1, replica_groups=mesh['freq'=64,'rec'=4] {'freq'}, dimensions={0} | all-to-all | bytes 1572864 | tf_op jit(solution)/shard_map/all_to_all | solution.py:353
  256.6 0.1 convert_element_type.77.x_ref
  256.8 2.4 shard_map.95
  (30 shorter events, 0.3 us)
Async XLA Ops:
  0.6 1.3 copy-start
  0.6 1.7 copy-start.4
  3.1 3.7 %copy-start.1 = (bf16[2,4,768,768]{3,2,1,0:T(8,128)(2,1)S(1)}, bf16[2,4,768,768]{3,2,1,0:T(8,128)(2,1)}, u32[]{:S(2)}) copy-start(bf16[2,4,768,768]{3,2,1,0:T(8,128)(2,1)} %refs_1_.15) | copy-start | bytes 28311556
  6.8 6.5 %slice-start = ((s8[9437184]{0:T(1024)(128)(4,1)}), s8[4194304]{0:T(1024)(128)(4,1)S(1)}, s32[]{:S(2)}) async-start(s8[9437184]{0:T(1024)(128)(4,1)} %bitcast.24), calls=%async_computation.8 | async-start | bytes 8388608
  6.8 6.5 %slice-start.1 = ((s8[9437184]{0:T(1024)(128)(4,1)}), s8[4194304]{0:T(1024)(128)(4,1)S(1)}, s32[]{:S(2)}) async-start(s8[9437184]{0:T(1024)(128)(4,1)} %bitcast.24), calls=%async_computation.9 | async-start | bytes 8388608
  8.7 4.6 %slice-start.2 = ((s8[9437184]{0:T(1024)(128)(4,1)}), s8[1048576]{0:T(1024)(128)(4,1)S(1)}, s32[]{:S(2)}) async-start(s8[9437184]{0:T(1024)(128)(4,1)} %bitcast.24), calls=%async_computation.10 | async-start | bytes 2097152
  8.7 2.4 collective-permute-start
  11.1 8.5 %collective-permute-start.1 = (f16[4,192,128]{2,1,0:T(8,128)(2,1)S(1)}, f16[4,192,128]{2,1,0:T(8,128)(2,1)S(1)}, u32[]{:S(2)}, u32[]{:S(2)}) collective-permute-start(f16[4,192,128]{2,1,0:T(8,128)(2,1)S(1)} %fusion.5), channel_id=1, source_target_pairs={{0,2},{2,0},{1,3},{3,1},{4,6},{6,4},{5,7},{7,5},{8,10},{10,8},{9,1... | collective-permute-start | bytes 589832 | tf_op jit(solution)/shard_map/ppermute | solution.py:356
  19.7 24.1 %copy-start.2 = (bf16[4,256,336]{2,1,0:T(8,128)(2,1)S(1)}, bf16[4,256,336]{2,1,0:T(8,128)(2,1)}, u32[]{:S(2)}) copy-start(bf16[4,256,336]{2,1,0:T(8,128)(2,1)} %constant.49.clone.refs_2_) | copy-start | bytes 2064388
  19.7 24.1 %copy-start.3 = (bf16[4,336,256]{2,1,0:T(8,128)(2,1)S(1)}, bf16[4,336,256]{2,1,0:T(8,128)(2,1)}, u32[]{:S(2)}) copy-start(bf16[4,336,256]{2,1,0:T(8,128)(2,1)} %constant.50.clone.refs_3_) | copy-start | bytes 2064388
  61.8 1.5 collective-permute-start.3
  61.9 8.9 %collective-permute-start.2 = (bf16[784,128]{1,0:T(8,128)(2,1)S(1)}, bf16[784,128]{1,0:T(8,128)(2,1)S(1)}, u32[]{:S(2)}, u32[]{:S(2)}) collective-permute-start(bf16[784,128]{1,0:T(8,128)(2,1)S(1)} %shard_map.82.a_ref.refs_4_), channel_id=1, source_target_pairs={{0,2},{2,0},{1,3},{3,1},{4,6},{6,4},{5,7},{7,5},{8,10},{10,8},{9,1... | collective-permute-start | bytes 602120 | tf_op jit(solution)/shard_map/ppermute | solution.py:356
  70.8 1.4 collective-permute-start.4
  136.6 2.4 collective-permute-start.5
  139.1 8.5 %collective-permute-start.6 = (f16[4,192,128]{2,1,0:T(8,128)(2,1)S(1)}, f16[4,192,128]{2,1,0:T(8,128)(2,1)S(1)}, u32[]{:S(2)}, u32[]{:S(2)}) collective-permute-start(f16[4,192,128]{2,1,0:T(8,128)(2,1)S(1)} %fusion.2), channel_id=1, source_target_pairs={{0,2},{2,0},{1,3},{3,1},{4,6},{6,4},{5,7},{7,5},{8,10},{10,8},{9,1... | collective-permute-start | bytes 589832 | tf_op jit(solution)/shard_map/ppermute | solution.py:356
  183.7 1.4 collective-permute-start.8
  183.7 8.9 %collective-permute-start.7 = (bf16[784,128]{1,0:T(8,128)(2,1)S(1)}, bf16[784,128]{1,0:T(8,128)(2,1)S(1)}, u32[]{:S(2)}, u32[]{:S(2)}) collective-permute-start(bf16[784,128]{1,0:T(8,128)(2,1)S(1)} %get-tuple-element.41.a_ref.refs_4_), channel_id=1, source_target_pairs={{0,2},{2,0},{1,3},{3,1},{4,6},{6,4},{5,7},{7,5},{8,10},{10,8},{9,1... | collective-permute-start | bytes 602120 | tf_op jit(solution)/shard_map/ppermute | solution.py:356
  192.6 1.4 collective-permute-start.9

commit v4 on v3

--- a/solution.py
+++ b/solution.py
@@ -186,6 +186,22 @@
         2 * bins * sources * recs * width,
         2 * bins * sources * recs,
     )(order, response, mine, beside)
+
+
+def adjoint_middle_kernel(order_ref, r_ref, total_ref, part_ref, o_ref):
+    for k in range(r_ref.shape[1]):
+        o_ref[k] = total_ref[k] + adjoint_sum(order_ref, (1,), r_ref, (part_ref,), k)
+
+
+def adjoint_middle(order, response, total, part):
+    _, bins, sources, recs = response.shape
+    return call(
+        adjoint_middle_kernel,
+        jax.ShapeDtypeStruct(total.shape, F32),
+        [smem()] + [vmem()] * 3,
+        bins * sources * recs * total.shape[1],
+        bins * sources * recs,
+    )(order, response, total, part)
 
 
 def adjoint_last_kernel(
@@ -220,7 +236,7 @@
     scale = jnp.max(TOP / norm)
     real, imag = [], []
     for k in range(bins):
-        both = total_ref[k] + adjoint_sum(order_ref, (1, 0), r_ref, (c_ref, d_ref), k)
+        both = total_ref[k] + adjoint_sum(order_ref, (0,), r_ref, (d_ref,), k)
         both = both * scale
         real.append(both[:HALF][None])
         imag.append(both[HALF:][None])
@@ -264,29 +280,60 @@
     )(kept, other, far, scale)
 
 
-def source_unpack_kernel(x_ref, unit_ref, m_ref, *outs):
-    bins = x_ref.shape[1] // 2
-    width = m_ref.shape[1]
-    block = 3 * HALF
+def source_rows(both, bins, k, i, unit):
+    cut = slice(i * HALF, (i + 1) * HALF)
+    return jnp.concatenate([both[k][:, cut], both[bins + k][:, cut]], axis=1) * unit
+
+
+def source_unpack_kernel(x_ref, unit_ref, m_ref):
+    bins, width = x_ref.shape[1] // 2, m_ref.shape[1]
     unit = unit_ref[0:1, :]
     both = jnp.transpose(x_ref[...], (1, 0, 2))
     norm = jnp.max(jnp.max(x_ref[:, 0, 3 * HALF :], axis=0, keepdims=True))
+    at = 0
     for k in range(bins):
         for i in range(3):
-            cut = slice(i * HALF, (i + 1) * HALF)
-            rows = jnp.concatenate([both[k][:, cut], both[bins + k][:, cut]], axis=1) * unit
-            for o_ref in outs:
-                o_ref[cut, k, :] = rows
-            m_ref[k * block + i * HALF : k * block + (i + 1) * HALF, :] = rows.astype(BF16)
-    m_ref[bins * block :, :] = jnp.full((16, width), norm, F32).astype(BF16)
-
-
-def source_unpack(x, unit, bins, full):
-    block, width = 3 * HALF, 2 * HALF
-    out = [jax.ShapeDtypeStruct((bins * block + 16, width), BF16)]
-    if full:
-        out.append(jax.ShapeDtypeStruct((block, bins, width), F32))
-    return call(source_unpack_kernel, out, [vmem()] * 2, 0, 16 * bins * block * width)(x, unit)
+            m_ref[at : at + HALF, :] = source_rows(both, bins, k, i, unit).astype(BF16)
+            at += HALF
+    m_ref[at:, :] = jnp.full((16, width), norm, F32).astype(BF16)
+
+
+def source_unpack(x, unit):
+    out = jax.ShapeDtypeStruct((x.shape[1] // 2 * 3 * HALF + 16, 2 * HALF), BF16)
+    return call(source_unpack_kernel, out, [vmem()] * 2, 0, 6 * x.size)(x, unit)
+
+
+def source_output_kernel(x_ref, unit_ref, o_ref):
+    bins = x_ref.shape[1] // 2
+    unit = unit_ref[0:1, :]
+    both = jnp.transpose(x_ref[...], (1, 0, 2))
+    for k in range(bins):
+        for i in range(3):
+            o_ref[i * HALF : (i + 1) * HALF, k, :] = source_rows(both, bins, k, i, unit)
+
+
+def source_output(x, unit):
+    out = jax.ShapeDtypeStruct((3 * HALF, x.shape[1] // 2, 2 * HALF), F32)
+    return call(source_output_kernel, out, [vmem(), vmem()], 0, 8 * x.size)(x, unit)
+
+
+def onset_kernel(order_ref, src_ref, rec_ref, src_row_ref, rec_row_ref):
+    freq, first = order_ref[4], order_ref[5]
+    lane = lax.broadcasted_iota(jnp.int32, src_ref.shape, 1)
+    src = src_ref[...].astype(F32)
+    rows = []
+    for i in range(3):
+        picked = jnp.where(lane == first + i * HALF + freq, src, 0.0)
+        picked = jnp.sum(picked, axis=1, keepdims=True)
+        rows.append(jnp.broadcast_to(picked, (HALF, 2 * HALF)).T[0:1, :])
+    rows.append(jnp.zeros_like(rows[0]))
+    src_row_ref[...] = jnp.concatenate(rows, axis=1).astype(jnp.int32)
+    rec_row_ref[...] = rec_ref[pl.ds(freq, 1), :]
+
+
+def onset_rows(order, src, rec):
+    out = [jax.ShapeDtypeStruct((1, 4 * HALF), jnp.int32), jax.ShapeDtypeStruct((1, rec.shape[1]), jnp.int32)]
+    return call(onset_kernel, out, [smem(), vmem(), vmem()], 0, 4 * (src.size + rec.size))(order, src, rec)
 
 
 def plus_forward_kernel(picks, order_ref, r_ref, back_ref, init_ref, unit_ref, x_ref, o_ref):
@@ -342,12 +389,16 @@
     def place(h, c):
         return h * 2 + c
 
-    order = jnp.stack([place(1 - high, 1 - core), place(1 - high, core), place(high, 1 - core), place(high, core)])
-    order = order.astype(jnp.int32)
-
-    rec_onsets = lax.dynamic_slice_in_dim(onset_rec.T, freq_pos, 1, 0)
-    mine = lax.dynamic_slice(onset_src.reshape(4, 3, HALF, HALF), (rec_pos, 0, freq_pos, 0), (1, 3, 1, HALF))
-    src_onsets = jnp.concatenate([mine.reshape(1, 3 * HALF), jnp.zeros((1, HALF), jnp.int32)], axis=1)
+    order = jnp.stack(
+        [
+            place(1 - high, 1 - core),
+            place(1 - high, core),
+            place(high, 1 - core),
+            place(high, core),
+            freq_pos,
+            rec_pos * block,
+        ]
+    ).astype(jnp.int32)
 
     def swap(values):
         return lax.all_to_all(values.astype(F16), "freq", split_axis=0, concat_axis=0, tiled=True).astype(F32)
@@ -359,7 +410,8 @@
     rec_gain = 4 * recs * R_ABS
 
     init_t = jnp.transpose(focus_init, (1, 2, 0))
-    init_t, order, src_onsets, rec_onsets = lax.optimization_barrier((init_t, order, src_onsets, rec_onsets))
+    init_t, order = lax.optimization_barrier((init_t, order))
+    src_onsets = rec_onsets = None
     plus = init_t
     bound = jnp.full((1, 128), rec_gain * init_norm, F32)
     scale, unit = TOP / bound, bound * (1.0 / TOP)
@@ -374,20 +426,27 @@
         away_other = step_to(away, CORE_SWAP)
         away_mine = forward_call(order, response, plus, (1,))
         coded = ((away_mine[0] + away_other[0]) * scale).astype(F16)
-        coded, plus = lax.optimization_barrier((coded, plus))
+        coded, plus, late = lax.optimization_barrier((coded, plus, order))
         far = step_to(coded, HIGH_SWAP)
         near = forward_call(order, response, plus, (3,))
+        if step == 0:
+            src_onsets, rec_onsets = onset_rows(late, onset_src.T, onset_rec.T)
+        far, src_onsets, rec_onsets = lax.optimization_barrier((far, src_onsets, rec_onsets))
         field = source_pack(near, away_other, far.astype(F32), scale)
         field = swap(field).reshape(3 * HALF * bins, width)
         field = window_call(field, src_onsets, tables, True)
-        mine, *full = source_unpack(swap(field), unit, bins, last)
-        if last:
-            minus_out = full[0]
+        field = swap(field)
+        mine = source_unpack(field, unit)
         across = step_to(mine, HIGH_SWAP)
         beside = step_to(mine, CORE_SWAP)
         total = adjoint_first(order, response, mine, beside)
-        across, total = lax.optimization_barrier((across, total))
+        if last:
+            minus_out = source_output(field, unit)
+            across, total, minus_out = lax.optimization_barrier((across, total, minus_out))
+        else:
+            across, total = lax.optimization_barrier((across, total))
         corner = step_to(across, CORE_SWAP)
+        total = adjoint_middle(order, response, total, across)
         parts = (mine, beside, across, corner)
         behind, back_unit, scale, unit = adjoint_last(order, response, total, unit, parts, rec_gain, init_norm)
         field = window_call(swap(behind), rec_onsets, tables, False)

time: 260 us -> 258 us (level)
  waiting for transfers between devices: 29.7 us -> 25.2 us
  Pallas kernels: 28.4 us -> 31 us
    ppermute x10, waiting for transfers between devices: 29.7 us -> 25.2 us  [step_to(): return lax.ppermute(values, 'rec', pairs)]
    pallas_call x2 -> x6, Pallas kernels: 1.37 us -> 4.65 us  [the longest x2 2.33 us: adjoint_middle(): call(adjoint_middle_kernel, jax.ShapeDtypeStruct(total.shape, F32), [smem...]
  transfers between devices with their start and end apart: 10 -> 10, of which waited for: 10 -> 9; matrix products, arithmetic and copies ran while one was open for 0% -> 0% of each run, Pallas kernels for 3% -> 5%
where the time goes in v4:
time: 258 us; the launch traced here: 257 us
  blocking collectives  188 us (73%)
  Pallas kernels  31 us (12%)
  waiting for transfers between devices  25.2 us (10%)
  local copies, waits for them, and re-layouts  5.39 us (2%)
  starting transfers between devices  4.91 us (2%)
    all_to_all x8, blocking collectives, swap(): lax.all_to_all(values.astype(F16), 'freq', split_axis=0, concat_axis=0, t...  188 us
    ppermute x10, waiting for transfers between devices, step_to(): return lax.ppermute(values, 'rec', pairs)  25.2 us
    pallas_call x4, Pallas kernels, window_call(): call(lambda *refs: window_kernel(from_source, *refs), jax.ShapeDtypeStruc...  7.47 us
    pallas_call x5, Pallas kernels, forward_call(): call(lambda *refs: forward_kernel(picks, *refs), jax.ShapeDtypeStruct((le...  7.14 us
    unnamed x17, local copies, waits for them, and re-layouts  5.29 us
  transfers between devices with their start and end apart: 10, of which 9 were waited for; matrix products, arithmetic and copies ran while one was open for 0% of the time, Pallas kernels for 5%

profile of v4, /device:TPU:16, one launch (start us, length us, event | category | flops | bytes accessed | tf_op | source)
XLA Modules:
  0.0 257.1 jit_solution(9484339854607844948)
XLA Ops:
  0.7 1.5 copy.8
  2.2 0.1 stack.27.refs_0_.order_ref
  2.3 3.7 %copy-done = bf16[2,4,768,768]{3,2,1,0:T(8,128)(2,1)S(1)} copy-done((bf16[2,4,768,768]{3,2,1,0:T(8,128)(2,1)S(1)}, bf16[2,4,768,768]{3,2,1,0:T(8,128)(2,1)}, u32[]{:S(2)}) %copy-start) | copy-done | bytes 9437208
  6.0 1.9 shard_map.78
  7.9 0.1 collective-permute-start
  8.0 1.3 shard_map.77
  9.4 1.0 collective-permute-done.other_ref
  10.3 0.1 fusion.5
  10.4 2.2 collective-permute-start.1
  12.5 0.7 shard_map.80
  13.3 0.0 slice-done.1
  13.3 1.3 shard_map.79.kept_ref
  14.7 4.3 %collective-permute-done.1 = f16[4,192,128]{2,1,0:T(8,128)(2,1)S(1)} collective-permute-done((f16[4,192,128]{2,1,0:T(8,128)(2,1)S(1)}, f16[4,192,128]{2,1,0:T(8,128)(2,1)S(1)}, u32[]{:S(2)}, u32[]{:S(2)}) %collective-permute-start.1) | collective-permute-done | bytes 196640 | tf_op jit(solution)/shard_map/ppermute | solution.py:407
  19.0 0.3 shard_map.81
  19.3 0.1 convert_element_type.62
  19.4 23.7 %all_to_all.40 = f16[64,3,4,128]{3,2,1,0:T(4,128)(2,1)S(1)} all-to-all(f16[64,3,4,128]{3,2,1,0:T(4,128)(2,1)S(1)} %convert_element_type.62), channel_id=1, replica_groups=mesh['freq'=64,'rec'=4] {'freq'}, dimensions={0} | all-to-all | bytes 393216 | tf_op jit(solution)/shard_map/all_to_all | solution.py:404
  43.1 1.3 shard_map.82
  44.4 16.3 %all_to_all.41 = f16[64,8,256]{2,1,0:T(8,128)(2,1)S(1)} all-to-all(f16[64,8,256]{2,1,0:T(8,128)(2,1)S(1)} %convert_element_type.63), channel_id=1, replica_groups=mesh['freq'=64,'rec'=4] {'freq'}, dimensions={0} | all-to-all | bytes 524288 | tf_op jit(solution)/shard_map/all_to_all | solution.py:404
  60.8 0.2 shard_map.83.a_ref.refs_4_
  61.1 0.1 collective-permute-start.3
  61.2 0.7 collective-permute-start.2
  61.9 0.7 collective-permute-done.3.b_ref.refs_5_
  62.6 1.5 shard_map.84.total_ref
  64.2 5.9 %collective-permute-done.2.part_ref.refs_6_ = bf16[784,128]{1,0:T(8,128)(2,1)S(1)} collective-permute-done((bf16[784,128]{1,0:T(8,128)(2,1)S(1)}, bf16[784,128]{1,0:T(8,128)(2,1)S(1)}, u32[]{:S(2)}, u32[]{:S(2)}) %collective-permute-start.2) | collective-permute-done | bytes 200736 | tf_op jit(solution)/shard_map/ppermute | solution.py:407
  70.1 1.2 shard_map.85.refs_2_
  71.3 0.3 collective-permute-done.4.refs_7_
  71.5 1.5 shard_map.86
  73.0 0.1 convert_element_type.65
  73.1 28.7 %all_to_all.42 = f16[64,8,768]{2,1,0:T(8,128)(2,1)S(1)} all-to-all(f16[64,8,768]{2,1,0:T(8,128)(2,1)S(1)} %convert_element_type.65), channel_id=1, replica_groups=mesh['freq'=64,'rec'=4] {'freq'}, dimensions={0} | all-to-all | bytes 1572864 | tf_op jit(solution)/shard_map/all_to_all | solution.py:404
  101.8 0.1 convert_element_type.66.refs_0_
  102.0 2.5 shard_map.87
  104.4 0.1 convert_element_type.67
  104.5 28.8 %all_to_all.43 = f16[64,8,768]{2,1,0:T(8,128)(2,1)S(1)} all-to-all(f16[64,8,768]{2,1,0:T(8,128)(2,1)S(1)} %convert_element_type.67), channel_id=1, replica_groups=mesh['freq'=64,'rec'=4] {'freq'}, dimensions={0} | all-to-all | bytes 1572864 | tf_op jit(solution)/shard_map/all_to_all | solution.py:404
  133.4 0.1 convert_element_type.68.refs_2_
  133.5 2.1 shard_map.88
  135.6 0.1 collective-permute-start.5
  135.7 1.3 shard_map.89
  137.1 1.0 collective-permute-done.5.other_ref
  138.0 0.1 fusion.2
  138.1 0.7 collective-permute-start.6
  138.8 1.3 shard_map.90.kept_ref
  140.1 6.5 %collective-permute-done.6 = f16[4,192,128]{2,1,0:T(8,128)(2,1)S(1)} collective-permute-done((f16[4,192,128]{2,1,0:T(8,128)(2,1)S(1)}, f16[4,192,128]{2,1,0:T(8,128)(2,1)S(1)}, u32[]{:S(2)}, u32[]{:S(2)}) %collective-permute-start.6) | collective-permute-done | bytes 196640 | tf_op jit(solution)/shard_map/ppermute | solution.py:407
  146.7 0.3 shard_map.91
  147.0 0.1 convert_element_type.71
  147.1 16.8 %all_to_all.44 = f16[64,3,4,128]{3,2,1,0:T(4,128)(2,1)S(1)} all-to-all(f16[64,3,4,128]{3,2,1,0:T(4,128)(2,1)S(1)} %convert_element_type.71), channel_id=1, replica_groups=mesh['freq'=64,'rec'=4] {'freq'}, dimensions={0} | all-to-all | bytes 393216 | tf_op jit(solution)/shard_map/all_to_all | solution.py:404
  163.8 1.3 shard_map.92
  165.2 16.3 %all_to_all.45 = f16[64,8,256]{2,1,0:T(8,128)(2,1)S(1)} all-to-all(f16[64,8,256]{2,1,0:T(8,128)(2,1)S(1)} %convert_element_type.72), channel_id=1, replica_groups=mesh['freq'=64,'rec'=4] {'freq'}, dimensions={0} | all-to-all | bytes 524288 | tf_op jit(solution)/shard_map/all_to_all | solution.py:404
  181.5 0.2 shard_map.93.a_ref.refs_4_
  181.8 0.1 collective-permute-start.8
  181.9 0.9 collective-permute-start.7
  182.8 1.1 shard_map.95
  183.9 1.5 shard_map.94.total_ref
  185.5 5.3 %collective-permute-done.7.part_ref.refs_6_ = bf16[784,128]{1,0:T(8,128)(2,1)S(1)} collective-permute-done((bf16[784,128]{1,0:T(8,128)(2,1)S(1)}, bf16[784,128]{1,0:T(8,128)(2,1)S(1)}, u32[]{:S(2)}, u32[]{:S(2)}) %collective-permute-start.7) | collective-permute-done | bytes 200736 | tf_op jit(solution)/shard_map/ppermute | solution.py:407
  190.8 1.2 shard_map.96.refs_2_
  192.0 0.3 collective-permute-done.9.refs_7_
  192.2 2.0 shard_map.97
  194.2 0.1 convert_element_type.74
  194.3 28.7 %all_to_all.46 = f16[64,8,768]{2,1,0:T(8,128)(2,1)S(1)} all-to-all(f16[64,8,768]{2,1,0:T(8,128)(2,1)S(1)} %convert_element_type.74), channel_id=1, replica_groups=mesh['freq'=64,'rec'=4] {'freq'}, dimensions={0} | all-to-all | bytes 1572864 | tf_op jit(solution)/shard_map/all_to_all | solution.py:404
  223.0 0.1 convert_element_type.75.refs_0_
  223.2 2.5 shard_map.98
  225.6 0.1 convert_element_type.76
  225.7 28.8 %all_to_all.47 = f16[64,8,768]{2,1,0:T(8,128)(2,1)S(1)} all-to-all(f16[64,8,768]{2,1,0:T(8,128)(2,1)S(1)} %convert_element_type.76), channel_id=1, replica_groups=mesh['freq'=64,'rec'=4] {'freq'}, dimensions={0} | all-to-all | bytes 1572864 | tf_op jit(solution)/shard_map/all_to_all | solution.py:404
  254.6 0.1 convert_element_type.77.x_ref
  254.7 2.4 shard_map.99
  (28 shorter events, 0.3 us)
Async XLA Ops:
  2.3 3.7 %copy-start = (bf16[2,4,768,768]{3,2,1,0:T(8,128)(2,1)S(1)}, bf16[2,4,768,768]{3,2,1,0:T(8,128)(2,1)}, u32[]{:S(2)}) copy-start(bf16[2,4,768,768]{3,2,1,0:T(8,128)(2,1)} %refs_1_.15) | copy-start | bytes 28311556
  6.0 7.3 %slice-start = ((s8[9437184]{0:T(1024)(128)(4,1)}), s8[4194304]{0:T(1024)(128)(4,1)S(1)}, s32[]{:S(2)}) async-start(s8[9437184]{0:T(1024)(128)(4,1)} %bitcast.22), calls=%async_computation.8 | async-start | bytes 8388608
  6.0 7.3 %slice-start.1 = ((s8[9437184]{0:T(1024)(128)(4,1)}), s8[4194304]{0:T(1024)(128)(4,1)S(1)}, s32[]{:S(2)}) async-start(s8[9437184]{0:T(1024)(128)(4,1)} %bitcast.22), calls=%async_computation.9 | async-start | bytes 8388608
  7.9 4.6 %copy-start.3 = (s32[768,64]{0,1:T(8,128)S(1)}, s32[768,64]{0,1:T(8,128)}, u32[]{:S(2)}) copy-start(s32[768,64]{0,1:T(8,128)} %param.8) | copy-start | bytes 589828
  7.9 4.6 %copy-start.4 = (s32[768,64]{0,1:T(8,128)S(1)}, s32[768,64]{0,1:T(8,128)}, u32[]{:S(2)}) copy-start(s32[768,64]{0,1:T(8,128)} %param.9) | copy-start | bytes 589828
  7.9 5.4 %slice-start.2 = ((s8[9437184]{0:T(1024)(128)(4,1)}), s8[1048576]{0:T(1024)(128)(4,1)S(1)}, s32[]{:S(2)}) async-start(s8[9437184]{0:T(1024)(128)(4,1)} %bitcast.22), calls=%async_computation.10 | async-start | bytes 2097152
  7.9 2.4 collective-permute-start
  10.4 8.5 %collective-permute-start.1 = (f16[4,192,128]{2,1,0:T(8,128)(2,1)S(1)}, f16[4,192,128]{2,1,0:T(8,128)(2,1)S(1)}, u32[]{:S(2)}, u32[]{:S(2)}) collective-permute-start(f16[4,192,128]{2,1,0:T(8,128)(2,1)S(1)} %fusion.5), channel_id=1, source_target_pairs={{0,2},{2,0},{1,3},{3,1},{4,6},{6,4},{5,7},{7,5},{8,10},{10,8},{9,1... | collective-permute-start | bytes 589832 | tf_op jit(solution)/shard_map/ppermute | solution.py:407
  19.0 24.1 %copy-start.1 = (bf16[4,256,336]{2,1,0:T(8,128)(2,1)S(1)}, bf16[4,256,336]{2,1,0:T(8,128)(2,1)}, u32[]{:S(2)}) copy-start(bf16[4,256,336]{2,1,0:T(8,128)(2,1)} %constant.45.clone.refs_2_) | copy-start | bytes 2064388
  19.0 24.1 %copy-start.2 = (bf16[4,336,256]{2,1,0:T(8,128)(2,1)S(1)}, bf16[4,336,256]{2,1,0:T(8,128)(2,1)}, u32[]{:S(2)}) copy-start(bf16[4,336,256]{2,1,0:T(8,128)(2,1)} %constant.46.clone.refs_3_) | copy-start | bytes 2064388
  61.1 1.5 collective-permute-start.3
  61.2 8.9 %collective-permute-start.2 = (bf16[784,128]{1,0:T(8,128)(2,1)S(1)}, bf16[784,128]{1,0:T(8,128)(2,1)S(1)}, u32[]{:S(2)}, u32[]{:S(2)}) collective-permute-start(bf16[784,128]{1,0:T(8,128)(2,1)S(1)} %shard_map.83.a_ref.refs_4_), channel_id=1, source_target_pairs={{0,2},{2,0},{1,3},{3,1},{4,6},{6,4},{5,7},{7,5},{8,10},{10,8},{9,1... | collective-permute-start | bytes 602120 | tf_op jit(solution)/shard_map/ppermute | solution.py:407
  70.1 1.4 collective-permute-start.4
  135.6 2.4 collective-permute-start.5
  138.1 8.5 %collective-permute-start.6 = (f16[4,192,128]{2,1,0:T(8,128)(2,1)S(1)}, f16[4,192,128]{2,1,0:T(8,128)(2,1)S(1)}, u32[]{:S(2)}, u32[]{:S(2)}) collective-permute-start(f16[4,192,128]{2,1,0:T(8,128)(2,1)S(1)} %fusion.2), channel_id=1, source_target_pairs={{0,2},{2,0},{1,3},{3,1},{4,6},{6,4},{5,7},{7,5},{8,10},{10,8},{9,1... | collective-permute-start | bytes 589832 | tf_op jit(solution)/shard_map/ppermute | solution.py:407
  181.8 2.1 collective-permute-start.8
  181.9 8.9 %collective-permute-start.7 = (bf16[784,128]{1,0:T(8,128)(2,1)S(1)}, bf16[784,128]{1,0:T(8,128)(2,1)S(1)}, u32[]{:S(2)}, u32[]{:S(2)}) collective-permute-start(bf16[784,128]{1,0:T(8,128)(2,1)S(1)} %shard_map.93.a_ref.refs_4_), channel_id=1, source_target_pairs={{0,2},{2,0},{1,3},{3,1},{4,6},{6,4},{5,7},{7,5},{8,10},{10,8},{9,1... | collective-permute-start | bytes 602120 | tf_op jit(solution)/shard_map/ppermute | solution.py:407
  190.8 1.4 collective-permute-start.9

commit v5 on v4

--- a/solution.py
+++ b/solution.py
@@ -129,8 +129,8 @@
     )(x, onsets, *tables)
 
 
-def forward_bin(picks, order_ref, r_ref, x_ref, o_ref, k):
-    block = o_ref.shape[2]
+def forward_bin(picks, order_ref, r_ref, x_ref, outs, k):
+    block = outs[0].shape[1]
     dims = (((1,), (1,)), ((), ()))
     x = x_ref[k]
     y = jnp.concatenate([-x[HALF:], x[:HALF]], axis=0)
@@ -139,13 +139,13 @@
     imag = jnp.concatenate([r_ref[1, k, pl.ds(at, block), :] for at in starts], axis=0)
     both = lax.dot_general(real, x, dims, preferred_element_type=F32)
     both = both + lax.dot_general(imag, y, dims, preferred_element_type=F32)
-    for i in range(len(picks)):
-        o_ref[i, k] = both[i * block : (i + 1) * block]
-
-
-def forward_kernel(picks, order_ref, r_ref, x_ref, o_ref):
-    for k in range(o_ref.shape[1]):
-        forward_bin(picks, order_ref, r_ref, x_ref, o_ref, k)
+    for i, o_ref in enumerate(outs):
+        o_ref[k] = both[i * block : (i + 1) * block]
+
+
+def forward_kernel(picks, order_ref, r_ref, x_ref, *outs):
+    for k in range(x_ref.shape[0]):
+        forward_bin(picks, order_ref, r_ref, x_ref, outs, k)
 
 
 def forward_call(order, response, plus, picks):
@@ -154,7 +154,7 @@
     block = sources // 4
     return call(
         lambda *refs: forward_kernel(picks, *refs),
-        jax.ShapeDtypeStruct((len(picks), bins, block, width), F32),
+        [jax.ShapeDtypeStruct((bins, block, width), F32)] * len(picks),
         [smem(), vmem(), vmem()],
         4 * bins * len(picks) * block * recs * width,
         4 * bins * len(picks) * block * recs,
@@ -258,26 +258,27 @@
     )(order, response, total, unit, *parts)
 
 
-def source_pack_kernel(kept_ref, other_ref, far_ref, scale_ref, o_ref):
-    _, bins, block, width = kept_ref.shape
+def source_pack_kernel(kept_ref, far_ref, scale_ref, *refs):
+    others, o_ref = refs[:-1], refs[-1]
+    bins = kept_ref.shape[0]
     scale = scale_ref[0:1, :]
     for k in range(bins):
-        total = (kept_ref[0, k] + other_ref[1, k]) * scale + far_ref[k]
+        total = (kept_ref[k] + (others[0][k] if len(others) == 1 else others[k][...])) * scale + far_ref[k]
         a, b = total[:HALF], total[HALF : 2 * HALF]
         o_ref[:, 0, k, :] = jnp.concatenate([a[:, :HALF], b[:, :HALF]], axis=1)
         o_ref[:, 1, k, :] = jnp.concatenate([a[:, HALF:], b[:, HALF:]], axis=1)
         o_ref[:, 2, k, :] = total[2 * HALF :]
 
 
-def source_pack(kept, other, far, scale):
-    bins = kept.shape[1]
+def source_pack(kept, far, scale, others):
+    bins = kept.shape[0]
     return call(
         source_pack_kernel,
         jax.ShapeDtypeStruct((HALF, 3, bins, 2 * HALF), F32),
-        [vmem()] * 4,
+        [vmem()] * (3 + len(others)),
         0,
         16 * kept.size,
-    )(kept, other, far, scale)
+    )(kept, far, scale, *others)
 
 
 def source_rows(both, bins, k, i, unit):
@@ -336,14 +337,14 @@
     return call(onset_kernel, out, [smem(), vmem(), vmem()], 0, 4 * (src.size + rec.size))(order, src, rec)
 
 
-def plus_forward_kernel(picks, order_ref, r_ref, back_ref, init_ref, unit_ref, x_ref, o_ref):
+def plus_forward_kernel(picks, order_ref, r_ref, back_ref, init_ref, unit_ref, x_ref, *outs):
     bins, _, recs = init_ref.shape
     unit = jnp.max(unit_ref[...])
     both = jnp.transpose(back_ref[...], (1, 0, 2))
     for k in range(bins):
         rows = jnp.concatenate([both[k], both[bins + k]], axis=0) * unit
         x_ref[k] = (init_ref[k].astype(F32) + rows).astype(BF16)
-        forward_bin(picks, order_ref, r_ref, x_ref, o_ref, k)
+        forward_bin(picks, order_ref, r_ref, x_ref, outs, k)
 
 
 def plus_forward(order, response, back, init, unit, picks):
@@ -351,29 +352,43 @@
     block = response.shape[2] // 4
     return call(
         lambda *refs: plus_forward_kernel(picks, *refs),
-        [
-            jax.ShapeDtypeStruct(init.shape, BF16),
-            jax.ShapeDtypeStruct((len(picks), bins, block, width), F32),
-        ],
+        [jax.ShapeDtypeStruct(init.shape, BF16)] + [jax.ShapeDtypeStruct((bins, block, width), F32)] * len(picks),
         [smem()] + [vmem()] * 4,
         4 * bins * len(picks) * block * recs * width,
         4 * bins * len(picks) * block * recs,
     )(order, response, back, init, unit)
 
 
-def final_kernel(x_ref, init_ref, unit_ref, o_ref):
-    bins = init_ref.shape[0]
+def final_kernel(x_ref, init_ref, unit_ref, o_ref, held_ref, sems):
+    bins, _, recs = init_ref.shape
     unit = jnp.max(unit_ref[...])
-    both = jnp.transpose(x_ref[...], (1, 0, 2))
-    for k in range(bins):
-        rows = jnp.concatenate([both[k], both[bins + k]], axis=0) * unit
-        o_ref[:, k, :] = (init_ref[k].astype(F32) + rows).T
+    pieces = sems.shape[0]
+    size = recs // pieces
+    copies = []
+    for i in range(pieces):
+        cut = slice(i * size, (i + 1) * size)
+        both = jnp.transpose(x_ref[:, :, cut], (1, 0, 2))
+        for k in range(bins):
+            rows = jnp.concatenate([both[k], both[bins + k]], axis=0) * unit
+            held_ref[cut, k, :] = (init_ref[k][:, cut].astype(F32) + rows).T
+        copies.append(pltpu.make_async_copy(held_ref.at[cut], o_ref.at[cut], sems.at[i]))
+        copies[-1].start()
+    for copy in copies:
+        copy.wait()
 
 
 def final_call(x, init, unit):
     bins, width, recs = init.shape
     out = jax.ShapeDtypeStruct((recs, bins, width), F32)
-    return call(final_kernel, out, [vmem()] * 3, 0, 8 * x.size)(x, init, unit)
+    return pl.pallas_call(
+        final_kernel,
+        in_specs=[vmem()] * 3,
+        out_specs=pl.BlockSpec(memory_space=pl.ANY),
+        out_shape=out,
+        scratch_shapes=[pltpu.VMEM(out.shape, F32), pltpu.SemaphoreType.DMA((3,))],
+        compiler_params=pltpu.CompilerParams(vmem_limit_bytes=16 * MIB),
+        cost_estimate=pl.CostEstimate(flops=0, bytes_accessed=8 * x.size, transcendentals=0),
+    )(x, init, unit)
 
 
 def body(response, focus_init, onset_src, onset_rec):
@@ -419,20 +434,27 @@
     plus_out = None
     for step in range(ITERS):
         last = step == ITERS - 1
+        aside = None
         if step == 0:
-            away = forward_call(order, response, plus, (0, 2))
+            (away,) = forward_call(order, response, plus, (0,))
         else:
-            plus, away = plus_forward(order, response, back, init_t, back_unit, (0, 2))
-        away_other = step_to(away, CORE_SWAP)
-        away_mine = forward_call(order, response, plus, (1,))
-        coded = ((away_mine[0] + away_other[0]) * scale).astype(F16)
-        coded, plus, late = lax.optimization_barrier((coded, plus, order))
-        far = step_to(coded, HIGH_SWAP)
-        near = forward_call(order, response, plus, (3,))
+            plus, away, aside = plus_forward(order, response, back, init_t, back_unit, (0, 2))
+        away = step_to(away, CORE_SWAP)
+        (mine,) = forward_call(order, response, plus, (1,))
+        coded = ((mine + away) * scale).astype(F16)
         if step == 0:
+            coded, plus, late = lax.optimization_barrier((coded, plus, order))
+            far = step_to(coded, HIGH_SWAP)
+            aside, near = forward_call(order, response, plus, (2, 3))
+            aside = [step_to(aside[k], CORE_SWAP) for k in range(bins)]
             src_onsets, rec_onsets = onset_rows(late, onset_src.T, onset_rec.T)
+        else:
+            coded, plus, aside = lax.optimization_barrier((coded, plus, aside))
+            far = step_to(coded, HIGH_SWAP)
+            aside = [step_to(aside, CORE_SWAP)]
+            (near,) = forward_call(order, response, plus, (3,))
         far, src_onsets, rec_onsets = lax.optimization_barrier((far, src_onsets, rec_onsets))
-        field = source_pack(near, away_other, far.astype(F32), scale)
+        field = source_pack(near, far.astype(F32), scale, aside)
         field = swap(field).reshape(3 * HALF * bins, width)
         field = window_call(field, src_onsets, tables, True)
         field = swap(field)

time: 258 us -> 257 us (level)
    ppermute x10 -> x15, waiting for transfers between devices: 25.2 us -> 22.8 us  [step_to(): return lax.ppermute(values, 'rec', pairs)]
    ppermute x10 -> x15, starting transfers between devices: 4.91 us -> 5.95 us  [step_to(): return lax.ppermute(values, 'rec', pairs)]
  transfers between devices with their start and end apart: 10 -> 15, of which waited for: 9 -> 9; matrix products, arithmetic and copies ran while one was open for 0% -> 0% of each run, Pallas kernels for 5% -> 5%
where the time goes in v5:
time: 257 us
  blocking collectives  189 us (74%)
  Pallas kernels  30.7 us (12%)
  waiting for transfers between devices  22.8 us (9%)
  starting transfers between devices  5.95 us (2%)
  local copies, waits for them, and re-layouts  5.39 us (2%)
    all_to_all x8, blocking collectives, swap(): lax.all_to_all(values.astype(F16), 'freq', split_axis=0, concat_axis=0, t...  189 us
    ppermute x15, waiting for transfers between devices, step_to(): return lax.ppermute(values, 'rec', pairs)  22.8 us
    pallas_call x4, Pallas kernels, window_call(): call(lambda *refs: window_kernel(from_source, *refs), jax.ShapeDtypeStruc...  7.46 us
    pallas_call x5, Pallas kernels, forward_call(): call(lambda *refs: forward_kernel(picks, *refs), [jax.ShapeDtypeStruct((b...  7.13 us
    ppermute x15, starting transfers between devices, step_to(): return lax.ppermute(values, 'rec', pairs)  5.95 us
    unnamed x17, local copies, waits for them, and re-layouts  5.26 us
  transfers between devices with their start and end apart: 15, of which 9 were waited for; matrix products, arithmetic and copies ran while one was open for 0% of the time, Pallas kernels for 5%

profile of v5, /device:TPU:16, one launch (start us, length us, event | category | flops | bytes accessed | tf_op | source)
XLA Modules:
  0.0 256.8 jit_solution(15741813305433955747)
XLA Ops:
  0.7 1.5 copy.8
  2.2 0.1 stack.27.refs_0_.order_ref
  2.3 3.7 %copy-done = bf16[2,4,768,768]{3,2,1,0:T(8,128)(2,1)S(1)} copy-done((bf16[2,4,768,768]{3,2,1,0:T(8,128)(2,1)S(1)}, bf16[2,4,768,768]{3,2,1,0:T(8,128)(2,1)}, u32[]{:S(2)}) %copy-start) | copy-done | bytes 9437208
  6.0 1.3 shard_map.78
  7.3 0.1 collective-permute-start
  7.4 1.3 shard_map.77
  8.7 0.4 collective-permute-done
  9.2 2.2 collective-permute-start.1
  11.4 1.9 shard_map.79
  13.3 0.1 collective-permute-start.5
  13.4 0.5 collective-permute-start.4
  13.9 0.1 collective-permute-start.3
  14.0 0.4 collective-permute-start.2
  14.4 0.7 shard_map.80
  15.2 2.5 collective-permute-done.1
  17.9 0.3 shard_map.81
  18.2 23.7 %all_to_all.40 = f16[64,3,4,128]{3,2,1,0:T(4,128)(2,1)S(1)} all-to-all(f16[64,3,4,128]{3,2,1,0:T(4,128)(2,1)S(1)} %convert_element_type.58), channel_id=1, replica_groups=mesh['freq'=64,'rec'=4] {'freq'}, dimensions={0} | all-to-all | bytes 393216 | tf_op jit(solution)/shard_map/all_to_all | solution.py:419
  42.0 1.3 shard_map.82
  43.3 16.3 %all_to_all.41 = f16[64,8,256]{2,1,0:T(8,128)(2,1)S(1)} all-to-all(f16[64,8,256]{2,1,0:T(8,128)(2,1)S(1)} %convert_element_type.59), channel_id=1, replica_groups=mesh['freq'=64,'rec'=4] {'freq'}, dimensions={0} | all-to-all | bytes 524288 | tf_op jit(solution)/shard_map/all_to_all | solution.py:419
  59.7 0.2 shard_map.83.a_ref.refs_4_
  59.9 0.1 collective-permute-start.7
  60.0 0.7 collective-permute-start.6
  60.7 0.7 collective-permute-done.7.b_ref.refs_5_
  61.5 1.5 shard_map.84.total_ref
  63.0 5.9 %collective-permute-done.6.part_ref.refs_6_ = bf16[784,128]{1,0:T(8,128)(2,1)S(1)} collective-permute-done((bf16[784,128]{1,0:T(8,128)(2,1)S(1)}, bf16[784,128]{1,0:T(8,128)(2,1)S(1)}, u32[]{:S(2)}, u32[]{:S(2)}) %collective-permute-start.6) | collective-permute-done | bytes 200736 | tf_op jit(solution)/shard_map/ppermute | solution.py:422
  68.9 1.2 shard_map.85.refs_2_
  70.1 0.3 collective-permute-done.8.refs_7_
  70.4 1.5 shard_map.86
  71.9 0.1 convert_element_type.61
  72.0 28.7 %all_to_all.42 = f16[64,8,768]{2,1,0:T(8,128)(2,1)S(1)} all-to-all(f16[64,8,768]{2,1,0:T(8,128)(2,1)S(1)} %convert_element_type.61), channel_id=1, replica_groups=mesh['freq'=64,'rec'=4] {'freq'}, dimensions={0} | all-to-all | bytes 1572864 | tf_op jit(solution)/shard_map/all_to_all | solution.py:419
  100.7 0.1 convert_element_type.62.refs_0_
  100.8 2.5 shard_map.87
  103.3 0.1 convert_element_type.63
  103.4 28.9 %all_to_all.43 = f16[64,8,768]{2,1,0:T(8,128)(2,1)S(1)} all-to-all(f16[64,8,768]{2,1,0:T(8,128)(2,1)S(1)} %convert_element_type.63), channel_id=1, replica_groups=mesh['freq'=64,'rec'=4] {'freq'}, dimensions={0} | all-to-all | bytes 1572864 | tf_op jit(solution)/shard_map/all_to_all | solution.py:419
  132.2 0.1 convert_element_type.64.refs_2_
  132.3 2.1 shard_map.88
  134.5 0.1 collective-permute-start.9
  134.6 1.3 shard_map.89
  135.9 0.4 collective-permute-done.9
  136.4 0.2 collective-permute-start.11
  136.6 0.7 collective-permute-start.10
  137.2 1.3 shard_map.90.kept_ref
  138.6 6.7 %collective-permute-done.10 = f16[4,192,128]{2,1,0:T(8,128)(2,1)S(1)} collective-permute-done((f16[4,192,128]{2,1,0:T(8,128)(2,1)S(1)}, f16[4,192,128]{2,1,0:T(8,128)(2,1)S(1)}, u32[]{:S(2)}, u32[]{:S(2)}) %collective-permute-start.10) | collective-permute-done | bytes 196640 | tf_op jit(solution)/shard_map/ppermute | solution.py:422
  145.3 0.3 shard_map.91
  145.7 16.8 %all_to_all.44 = f16[64,3,4,128]{3,2,1,0:T(4,128)(2,1)S(1)} all-to-all(f16[64,3,4,128]{3,2,1,0:T(4,128)(2,1)S(1)} %convert_element_type.67), channel_id=1, replica_groups=mesh['freq'=64,'rec'=4] {'freq'}, dimensions={0} | all-to-all | bytes 393216 | tf_op jit(solution)/shard_map/all_to_all | solution.py:419
  162.6 1.3 shard_map.92
  163.9 17.0 %all_to_all.45 = f16[64,8,256]{2,1,0:T(8,128)(2,1)S(1)} all-to-all(f16[64,8,256]{2,1,0:T(8,128)(2,1)S(1)} %convert_element_type.68), channel_id=1, replica_groups=mesh['freq'=64,'rec'=4] {'freq'}, dimensions={0} | all-to-all | bytes 524288 | tf_op jit(solution)/shard_map/all_to_all | solution.py:419
  180.9 0.2 shard_map.93.a_ref.refs_4_
  181.2 0.1 collective-permute-start.13
  181.3 0.7 collective-permute-start.12
  182.0 1.1 shard_map.95
  183.1 1.6 shard_map.94.total_ref
  184.6 5.5 %collective-permute-done.12.part_ref.refs_6_ = bf16[784,128]{1,0:T(8,128)(2,1)S(1)} collective-permute-done((bf16[784,128]{1,0:T(8,128)(2,1)S(1)}, bf16[784,128]{1,0:T(8,128)(2,1)S(1)}, u32[]{:S(2)}, u32[]{:S(2)}) %collective-permute-start.12) | collective-permute-done | bytes 200736 | tf_op jit(solution)/shard_map/ppermute | solution.py:422
  190.2 1.2 shard_map.96.refs_2_
  191.4 0.3 collective-permute-done.14.refs_7_
  191.6 2.1 shard_map.97
  193.7 0.1 convert_element_type.70
  193.8 29.0 %all_to_all.46 = f16[64,8,768]{2,1,0:T(8,128)(2,1)S(1)} all-to-all(f16[64,8,768]{2,1,0:T(8,128)(2,1)S(1)} %convert_element_type.70), channel_id=1, replica_groups=mesh['freq'=64,'rec'=4] {'freq'}, dimensions={0} | all-to-all | bytes 1572864 | tf_op jit(solution)/shard_map/all_to_all | solution.py:419
  222.8 0.1 convert_element_type.71.refs_0_
  222.9 2.5 shard_map.98
  225.4 0.1 convert_element_type.72
  225.5 28.9 %all_to_all.47 = f16[64,8,768]{2,1,0:T(8,128)(2,1)S(1)} all-to-all(f16[64,8,768]{2,1,0:T(8,128)(2,1)S(1)} %convert_element_type.72), channel_id=1, replica_groups=mesh['freq'=64,'rec'=4] {'freq'}, dimensions={0} | all-to-all | bytes 1572864 | tf_op jit(solution)/shard_map/all_to_all | solution.py:419
  254.3 0.1 convert_element_type.73.x_ref
  254.4 2.1 shard_map.99
  (39 shorter events, 0.6 us)
Async XLA Ops:
  2.3 3.7 %copy-start = (bf16[2,4,768,768]{3,2,1,0:T(8,128)(2,1)S(1)}, bf16[2,4,768,768]{3,2,1,0:T(8,128)(2,1)}, u32[]{:S(2)}) copy-start(bf16[2,4,768,768]{3,2,1,0:T(8,128)(2,1)} %refs_1_.15) | copy-start | bytes 28311556
  6.0 5.4 %slice-start = ((s8[9437184]{0:T(1024)(128)(4,1)}), s8[4194304]{0:T(1024)(128)(4,1)S(1)}, s32[]{:S(2)}) async-start(s8[9437184]{0:T(1024)(128)(4,1)} %bitcast.22), calls=%async_computation.8 | async-start | bytes 8388608
  6.0 5.4 %slice-start.1 = ((s8[9437184]{0:T(1024)(128)(4,1)}), s8[4194304]{0:T(1024)(128)(4,1)S(1)}, s32[]{:S(2)}) async-start(s8[9437184]{0:T(1024)(128)(4,1)} %bitcast.22), calls=%async_computation.9 | async-start | bytes 8388608
  7.3 4.1 %slice-start.2 = ((s8[9437184]{0:T(1024)(128)(4,1)}), s8[1048576]{0:T(1024)(128)(4,1)S(1)}, s32[]{:S(2)}) async-start(s8[9437184]{0:T(1024)(128)(4,1)} %bitcast.22), calls=%async_computation.10 | async-start | bytes 2097152
  7.3 1.8 collective-permute-start
  9.2 5.3 %copy-start.3 = (s32[768,64]{0,1:T(8,128)S(1)}, s32[768,64]{0,1:T(8,128)}, u32[]{:S(2)}) copy-start(s32[768,64]{0,1:T(8,128)} %param.8) | copy-start | bytes 589828
  9.2 5.3 %copy-start.4 = (s32[768,64]{0,1:T(8,128)S(1)}, s32[768,64]{0,1:T(8,128)}, u32[]{:S(2)}) copy-start(s32[768,64]{0,1:T(8,128)} %param.9) | copy-start | bytes 589828
  9.2 8.5 %collective-permute-start.1 = (f16[4,192,128]{2,1,0:T(8,128)(2,1)S(1)}, f16[4,192,128]{2,1,0:T(8,128)(2,1)S(1)}, u32[]{:S(2)}, u32[]{:S(2)}) collective-permute-start(f16[4,192,128]{2,1,0:T(8,128)(2,1)S(1)} %multiply_convert_fusion.1), channel_id=1, source_target_pairs={{0,2},{2,0},{1,3},{3,1},{4,6},{6,4},{5,7},{7,5},{8,10},{10,8},{9,1... | collective-permute-start | bytes 589832 | tf_op jit(solution)/shard_map/ppermute | solution.py:422
  13.3 4.4 %collective-permute-start.5 = (f32[192,128]{1,0:T(8,128)S(1)}, f32[192,128]{1,0:T(8,128)S(1)}, u32[]{:S(2)}, u32[]{:S(2)}) collective-permute-start(f32[192,128]{1,0:T(8,128)S(1)} %get-tuple-element.66), channel_id=1, source_target_pairs={{0,1},{1,0},{2,3},{3,2},{4,5},{5,4},{6,7},{7,6},{8,9},{9,8},{10,11... | collective-permute-start | bytes 294920 | tf_op jit(solution)/shard_map/ppermute | solution.py:422
  13.4 4.4 %collective-permute-start.4 = (f32[192,128]{1,0:T(8,128)S(1)}, f32[192,128]{1,0:T(8,128)S(1)}, u32[]{:S(2)}, u32[]{:S(2)}) collective-permute-start(f32[192,128]{1,0:T(8,128)S(1)} %get-tuple-element.67), channel_id=1, source_target_pairs={{0,1},{1,0},{2,3},{3,2},{4,5},{5,4},{6,7},{7,6},{8,9},{9,8},{10,11... | collective-permute-start | bytes 294920 | tf_op jit(solution)/shard_map/ppermute | solution.py:422
  13.9 3.9 %collective-permute-start.3 = (f32[192,128]{1,0:T(8,128)S(1)}, f32[192,128]{1,0:T(8,128)S(1)}, u32[]{:S(2)}, u32[]{:S(2)}) collective-permute-start(f32[192,128]{1,0:T(8,128)S(1)} %get-tuple-element.68), channel_id=1, source_target_pairs={{0,1},{1,0},{2,3},{3,2},{4,5},{5,4},{6,7},{7,6},{8,9},{9,8},{10,11... | collective-permute-start | bytes 294920 | tf_op jit(solution)/shard_map/ppermute | solution.py:422
  14.0 3.8 %collective-permute-start.2 = (f32[192,128]{1,0:T(8,128)S(1)}, f32[192,128]{1,0:T(8,128)S(1)}, u32[]{:S(2)}, u32[]{:S(2)}) collective-permute-start(f32[192,128]{1,0:T(8,128)S(1)} %get-tuple-element.69), channel_id=1, source_target_pairs={{0,1},{1,0},{2,3},{3,2},{4,5},{5,4},{6,7},{7,6},{8,9},{9,8},{10,11... | collective-permute-start | bytes 294920 | tf_op jit(solution)/shard_map/ppermute | solution.py:422
  17.8 24.1 %copy-start.1 = (bf16[4,256,336]{2,1,0:T(8,128)(2,1)S(1)}, bf16[4,256,336]{2,1,0:T(8,128)(2,1)}, u32[]{:S(2)}) copy-start(bf16[4,256,336]{2,1,0:T(8,128)(2,1)} %constant.45.clone.refs_2_) | copy-start | bytes 2064388
  17.8 24.1 %copy-start.2 = (bf16[4,336,256]{2,1,0:T(8,128)(2,1)S(1)}, bf16[4,336,256]{2,1,0:T(8,128)(2,1)}, u32[]{:S(2)}) copy-start(bf16[4,336,256]{2,1,0:T(8,128)(2,1)} %constant.46.clone.refs_3_) | copy-start | bytes 2064388
  59.9 1.5 collective-permute-start.7
  60.0 8.9 %collective-permute-start.6 = (bf16[784,128]{1,0:T(8,128)(2,1)S(1)}, bf16[784,128]{1,0:T(8,128)(2,1)S(1)}, u32[]{:S(2)}, u32[]{:S(2)}) collective-permute-start(bf16[784,128]{1,0:T(8,128)(2,1)S(1)} %shard_map.83.a_ref.refs_4_), channel_id=1, source_target_pairs={{0,2},{2,0},{1,3},{3,1},{4,6},{6,4},{5,7},{7,5},{8,10},{10,8},{9,1... | collective-permute-start | bytes 602120 | tf_op jit(solution)/shard_map/ppermute | solution.py:422
  68.9 1.4 collective-permute-start.8
  134.5 1.8 collective-permute-start.9
  136.4 8.9 %collective-permute-start.11 = (f32[4,192,128]{2,1,0:T(8,128)S(1)}, f32[4,192,128]{2,1,0:T(8,128)S(1)}, u32[]{:S(2)}, u32[]{:S(2)}) collective-permute-start(f32[4,192,128]{2,1,0:T(8,128)S(1)} %get-tuple-element.57), channel_id=1, source_target_pairs={{0,1},{1,0},{2,3},{3,2},{4,5},{5,4},{6,7},{7,6},{8,9},{9,8},{10,11... | collective-permute-start | bytes 1179656 | tf_op jit(solution)/shard_map/ppermute | solution.py:422
  136.6 8.7 %collective-permute-start.10 = (f16[4,192,128]{2,1,0:T(8,128)(2,1)S(1)}, f16[4,192,128]{2,1,0:T(8,128)(2,1)S(1)}, u32[]{:S(2)}, u32[]{:S(2)}) collective-permute-start(f16[4,192,128]{2,1,0:T(8,128)(2,1)S(1)} %multiply_convert_fusion), channel_id=1, source_target_pairs={{0,2},{2,0},{1,3},{3,1},{4,6},{6,4},{5,7},{7,5},{8,10},{10,8},{9,1... | collective-permute-start | bytes 589832 | tf_op jit(solution)/shard_map/ppermute | solution.py:422
  181.2 1.9 collective-permute-start.13
  181.3 8.9 %collective-permute-start.12 = (bf16[784,128]{1,0:T(8,128)(2,1)S(1)}, bf16[784,128]{1,0:T(8,128)(2,1)S(1)}, u32[]{:S(2)}, u32[]{:S(2)}) collective-permute-start(bf16[784,128]{1,0:T(8,128)(2,1)S(1)} %shard_map.93.a_ref.refs_4_), channel_id=1, source_target_pairs={{0,2},{2,0},{1,3},{3,1},{4,6},{6,4},{5,7},{7,5},{8,10},{10,8},{9,1... | collective-permute-start | bytes 602120 | tf_op jit(solution)/shard_map/ppermute | solution.py:422
  190.2 1.4 collective-permute-start.14

commit v6 on v5

--- a/solution.py
+++ b/solution.py
@@ -50,6 +50,11 @@
     return [high, (values - high.astype(np.float32)).astype(jnp.bfloat16)]
 
 
+def three(values):
+    high, low = high_low(values)
+    return np.concatenate([high, high, low], axis=1)
+
+
 def fold_tables(nbins):
     bins = np.arange(nbins, dtype=np.int64) + 1
     samples = np.arange(FOLD, dtype=np.int64)
@@ -57,17 +62,15 @@
     used = samples[None, :] <= NT // 2
     cosine = np.where(used, np.cos(angles), 0.0)
     sine = np.where(used, np.sin(angles), 0.0)
-    forward = np.stack(high_low(cosine) + high_low(sine))
-    inverse = np.stack(high_low(cosine.T * (2.0 / NT)) + high_low(sine.T * (2.0 / NT)))
+    forward = np.stack([three(cosine), three(sine)])
+    inverse = np.stack([three(cosine.T * (2.0 / NT)), three(sine.T * (2.0 / NT))])
     return forward, inverse
 
 
-def split_dot(high, low, x):
-    x_high = x.astype(BF16)
-    x_low = (x - x_high.astype(F32)).astype(BF16)
-    total = jnp.dot(high, x_high, preferred_element_type=F32)
-    total = total + jnp.dot(high, x_low, preferred_element_type=F32)
-    return total + jnp.dot(low, x_high, preferred_element_type=F32)
+def split_dot(table, x):
+    high = x.astype(BF16)
+    low = (x - high.astype(F32)).astype(BF16)
+    return jnp.dot(table, jnp.concatenate([high, low, high], axis=0), preferred_element_type=F32)
 
 
 def pair_halves(x_ref, first):
@@ -94,14 +97,14 @@
     blocks, _, lanes = o_ref.shape
     first = lax.broadcasted_iota(jnp.int32, (blocks // 2, 8, lanes), 1) < 4
     real, imag = triple_halves(x_ref, first) if from_source else pair_halves(x_ref, first)
-    a = split_dot(inverse_ref[0], inverse_ref[1], real)
-    b = split_dot(inverse_ref[2], inverse_ref[3], imag)
+    a = split_dot(inverse_ref[0], real)
+    b = split_dot(inverse_ref[1], imag)
     n = lax.broadcasted_iota(jnp.int32, a.shape, 0)
     onset = onset_ref[...]
     near = jnp.where(n < onset, a - b, 0.0)
     far = jnp.where((NT - n < onset) & (n > 0) & (n < NT // 2), a + b, 0.0)
-    real = split_dot(forward_ref[0], forward_ref[1], near + far)
-    imag = split_dot(forward_ref[2], forward_ref[3], far - near)
+    real = split_dot(forward_ref[0], near + far)
+    imag = split_dot(forward_ref[1], far - near)
     norm = None
     if from_source:
         norm = jnp.sqrt(jnp.max(jnp.sum(real * real + imag * imag, axis=0, keepdims=True))) * 1.01

time: 257 us -> 256 us (level)
  no operation moved by 1% of the time
where the time goes in v6:
time: 256 us
  blocking collectives  189 us (74%)
  Pallas kernels  29.8 us (12%)
  waiting for transfers between devices  22.8 us (9%)
  starting transfers between devices  5.95 us (2%)
  local copies, waits for them, and re-layouts  5.39 us (2%)
    all_to_all x8, blocking collectives, swap(): lax.all_to_all(values.astype(F16), 'freq', split_axis=0, concat_axis=0, t...  189 us
    ppermute x15, waiting for transfers between devices, step_to(): return lax.ppermute(values, 'rec', pairs)  22.8 us
    pallas_call x5, Pallas kernels, forward_call(): call(lambda *refs: forward_kernel(picks, *refs), [jax.ShapeDtypeStruct((b...  7.13 us
    pallas_call x4, Pallas kernels, window_call(): call(lambda *refs: window_kernel(from_source, *refs), jax.ShapeDtypeStruc...  6.57 us
    ppermute x15, starting transfers between devices, step_to(): return lax.ppermute(values, 'rec', pairs)  5.95 us
    unnamed x17, local copies, waits for them, and re-layouts  5.26 us
  transfers between devices with their start and end apart: 15, of which 9 were waited for; matrix products, arithmetic and copies ran while one was open for 0% of the time, Pallas kernels for 5%

profile of v6, /device:TPU:16, one launch (start us, length us, event | category | flops | bytes accessed | tf_op | source)
XLA Modules:
  0.0 255.6 jit_solution(16953465741634699219)
XLA Ops:
  0.7 1.5 copy.8
  2.2 0.1 stack.27.refs_0_.order_ref
  2.3 3.7 %copy-done = bf16[2,4,768,768]{3,2,1,0:T(8,128)(2,1)S(1)} copy-done((bf16[2,4,768,768]{3,2,1,0:T(8,128)(2,1)S(1)}, bf16[2,4,768,768]{3,2,1,0:T(8,128)(2,1)}, u32[]{:S(2)}) %copy-start) | copy-done | bytes 9437208
  6.0 1.3 shard_map.78
  7.3 0.1 collective-permute-start
  7.4 1.3 shard_map.77
  8.7 0.4 collective-permute-done
  9.2 2.2 collective-permute-start.1
  11.4 1.9 shard_map.79
  13.3 0.1 collective-permute-start.5
  13.4 0.5 collective-permute-start.4
  13.9 0.1 collective-permute-start.3
  14.0 0.4 collective-permute-start.2
  14.4 0.7 shard_map.80
  15.2 2.5 collective-permute-done.1
  17.9 0.3 shard_map.81
  18.2 23.7 %all_to_all.40 = f16[64,3,4,128]{3,2,1,0:T(4,128)(2,1)S(1)} all-to-all(f16[64,3,4,128]{3,2,1,0:T(4,128)(2,1)S(1)} %convert_element_type.58), channel_id=1, replica_groups=mesh['freq'=64,'rec'=4] {'freq'}, dimensions={0} | all-to-all | bytes 393216 | tf_op jit(solution)/shard_map/all_to_all | solution.py:422
  42.0 1.1 shard_map.82
  43.1 16.3 %all_to_all.41 = f16[64,8,256]{2,1,0:T(8,128)(2,1)S(1)} all-to-all(f16[64,8,256]{2,1,0:T(8,128)(2,1)S(1)} %convert_element_type.59), channel_id=1, replica_groups=mesh['freq'=64,'rec'=4] {'freq'}, dimensions={0} | all-to-all | bytes 524288 | tf_op jit(solution)/shard_map/all_to_all | solution.py:422
  59.5 0.2 shard_map.83.a_ref.refs_4_
  59.8 0.1 collective-permute-start.7
  59.9 0.7 collective-permute-start.6
  60.6 0.7 collective-permute-done.7.b_ref.refs_5_
  61.3 1.5 shard_map.84.total_ref
  62.9 5.9 %collective-permute-done.6.part_ref.refs_6_ = bf16[784,128]{1,0:T(8,128)(2,1)S(1)} collective-permute-done((bf16[784,128]{1,0:T(8,128)(2,1)S(1)}, bf16[784,128]{1,0:T(8,128)(2,1)S(1)}, u32[]{:S(2)}, u32[]{:S(2)}) %collective-permute-start.6) | collective-permute-done | bytes 200736 | tf_op jit(solution)/shard_map/ppermute | solution.py:425
  68.8 1.2 shard_map.85.refs_2_
  70.0 0.3 collective-permute-done.8.refs_7_
  70.2 1.5 shard_map.86
  71.7 0.1 convert_element_type.61
  71.8 28.7 %all_to_all.42 = f16[64,8,768]{2,1,0:T(8,128)(2,1)S(1)} all-to-all(f16[64,8,768]{2,1,0:T(8,128)(2,1)S(1)} %convert_element_type.61), channel_id=1, replica_groups=mesh['freq'=64,'rec'=4] {'freq'}, dimensions={0} | all-to-all | bytes 1572864 | tf_op jit(solution)/shard_map/all_to_all | solution.py:422
  100.5 0.1 convert_element_type.62.refs_0_
  100.6 2.2 shard_map.87
  102.8 0.1 convert_element_type.63
  102.9 28.9 %all_to_all.43 = f16[64,8,768]{2,1,0:T(8,128)(2,1)S(1)} all-to-all(f16[64,8,768]{2,1,0:T(8,128)(2,1)S(1)} %convert_element_type.63), channel_id=1, replica_groups=mesh['freq'=64,'rec'=4] {'freq'}, dimensions={0} | all-to-all | bytes 1572864 | tf_op jit(solution)/shard_map/all_to_all | solution.py:422
  131.8 0.1 convert_element_type.64.refs_2_
  131.9 2.1 shard_map.88
  134.0 0.1 collective-permute-start.9
  134.1 1.3 shard_map.89
  135.4 0.4 collective-permute-done.9
  135.9 0.2 collective-permute-start.11
  136.1 0.7 collective-permute-start.10
  136.8 1.3 shard_map.90.kept_ref
  138.1 6.7 %collective-permute-done.10 = f16[4,192,128]{2,1,0:T(8,128)(2,1)S(1)} collective-permute-done((f16[4,192,128]{2,1,0:T(8,128)(2,1)S(1)}, f16[4,192,128]{2,1,0:T(8,128)(2,1)S(1)}, u32[]{:S(2)}, u32[]{:S(2)}) %collective-permute-start.10) | collective-permute-done | bytes 196640 | tf_op jit(solution)/shard_map/ppermute | solution.py:425
  144.9 0.3 shard_map.91
  145.3 16.8 %all_to_all.44 = f16[64,3,4,128]{3,2,1,0:T(4,128)(2,1)S(1)} all-to-all(f16[64,3,4,128]{3,2,1,0:T(4,128)(2,1)S(1)} %convert_element_type.67), channel_id=1, replica_groups=mesh['freq'=64,'rec'=4] {'freq'}, dimensions={0} | all-to-all | bytes 393216 | tf_op jit(solution)/shard_map/all_to_all | solution.py:422
  162.1 1.1 shard_map.92
  163.3 16.8 %all_to_all.45 = f16[64,8,256]{2,1,0:T(8,128)(2,1)S(1)} all-to-all(f16[64,8,256]{2,1,0:T(8,128)(2,1)S(1)} %convert_element_type.68), channel_id=1, replica_groups=mesh['freq'=64,'rec'=4] {'freq'}, dimensions={0} | all-to-all | bytes 524288 | tf_op jit(solution)/shard_map/all_to_all | solution.py:422
  180.1 0.2 shard_map.93.a_ref.refs_4_
  180.3 0.1 collective-permute-start.13
  180.4 0.7 collective-permute-start.12
  181.2 1.1 shard_map.95
  182.3 1.6 shard_map.94.total_ref
  183.8 5.5 %collective-permute-done.12.part_ref.refs_6_ = bf16[784,128]{1,0:T(8,128)(2,1)S(1)} collective-permute-done((bf16[784,128]{1,0:T(8,128)(2,1)S(1)}, bf16[784,128]{1,0:T(8,128)(2,1)S(1)}, u32[]{:S(2)}, u32[]{:S(2)}) %collective-permute-start.12) | collective-permute-done | bytes 200736 | tf_op jit(solution)/shard_map/ppermute | solution.py:425
  189.4 1.2 shard_map.96.refs_2_
  190.5 0.3 collective-permute-done.14.refs_7_
  190.8 2.1 shard_map.97
  192.9 0.1 convert_element_type.70
  193.0 29.0 %all_to_all.46 = f16[64,8,768]{2,1,0:T(8,128)(2,1)S(1)} all-to-all(f16[64,8,768]{2,1,0:T(8,128)(2,1)S(1)} %convert_element_type.70), channel_id=1, replica_groups=mesh['freq'=64,'rec'=4] {'freq'}, dimensions={0} | all-to-all | bytes 1572864 | tf_op jit(solution)/shard_map/all_to_all | solution.py:422
  222.0 0.1 convert_element_type.71.refs_0_
  222.1 2.2 shard_map.98
  224.2 0.1 convert_element_type.72
  224.3 28.9 %all_to_all.47 = f16[64,8,768]{2,1,0:T(8,128)(2,1)S(1)} all-to-all(f16[64,8,768]{2,1,0:T(8,128)(2,1)S(1)} %convert_element_type.72), channel_id=1, replica_groups=mesh['freq'=64,'rec'=4] {'freq'}, dimensions={0} | all-to-all | bytes 1572864 | tf_op jit(solution)/shard_map/all_to_all | solution.py:422
  253.2 0.1 convert_element_type.73.x_ref
  253.3 2.1 shard_map.99
  (39 shorter events, 0.6 us)
Async XLA Ops:
  2.3 3.7 %copy-start = (bf16[2,4,768,768]{3,2,1,0:T(8,128)(2,1)S(1)}, bf16[2,4,768,768]{3,2,1,0:T(8,128)(2,1)}, u32[]{:S(2)}) copy-start(bf16[2,4,768,768]{3,2,1,0:T(8,128)(2,1)} %refs_1_.15) | copy-start | bytes 28311556
  6.0 5.4 %slice-start = ((s8[9437184]{0:T(1024)(128)(4,1)}), s8[4194304]{0:T(1024)(128)(4,1)S(1)}, s32[]{:S(2)}) async-start(s8[9437184]{0:T(1024)(128)(4,1)} %bitcast.22), calls=%async_computation.8 | async-start | bytes 8388608
  6.0 5.4 %slice-start.1 = ((s8[9437184]{0:T(1024)(128)(4,1)}), s8[4194304]{0:T(1024)(128)(4,1)S(1)}, s32[]{:S(2)}) async-start(s8[9437184]{0:T(1024)(128)(4,1)} %bitcast.22), calls=%async_computation.9 | async-start | bytes 8388608
  7.3 4.1 %slice-start.2 = ((s8[9437184]{0:T(1024)(128)(4,1)}), s8[1048576]{0:T(1024)(128)(4,1)S(1)}, s32[]{:S(2)}) async-start(s8[9437184]{0:T(1024)(128)(4,1)} %bitcast.22), calls=%async_computation.10 | async-start | bytes 2097152
  7.3 1.8 collective-permute-start
  9.2 5.3 %copy-start.3 = (s32[768,64]{0,1:T(8,128)S(1)}, s32[768,64]{0,1:T(8,128)}, u32[]{:S(2)}) copy-start(s32[768,64]{0,1:T(8,128)} %param.8) | copy-start | bytes 589828
  9.2 5.3 %copy-start.4 = (s32[768,64]{0,1:T(8,128)S(1)}, s32[768,64]{0,1:T(8,128)}, u32[]{:S(2)}) copy-start(s32[768,64]{0,1:T(8,128)} %param.9) | copy-start | bytes 589828
  9.2 8.5 %collective-permute-start.1 = (f16[4,192,128]{2,1,0:T(8,128)(2,1)S(1)}, f16[4,192,128]{2,1,0:T(8,128)(2,1)S(1)}, u32[]{:S(2)}, u32[]{:S(2)}) collective-permute-start(f16[4,192,128]{2,1,0:T(8,128)(2,1)S(1)} %multiply_convert_fusion.1), channel_id=1, source_target_pairs={{0,2},{2,0},{1,3},{3,1},{4,6},{6,4},{5,7},{7,5},{8,10},{10,8},{9,1... | collective-permute-start | bytes 589832 | tf_op jit(solution)/shard_map/ppermute | solution.py:425
  13.3 4.4 %collective-permute-start.5 = (f32[192,128]{1,0:T(8,128)S(1)}, f32[192,128]{1,0:T(8,128)S(1)}, u32[]{:S(2)}, u32[]{:S(2)}) collective-permute-start(f32[192,128]{1,0:T(8,128)S(1)} %get-tuple-element.66), channel_id=1, source_target_pairs={{0,1},{1,0},{2,3},{3,2},{4,5},{5,4},{6,7},{7,6},{8,9},{9,8},{10,11... | collective-permute-start | bytes 294920 | tf_op jit(solution)/shard_map/ppermute | solution.py:425
  13.4 4.4 %collective-permute-start.4 = (f32[192,128]{1,0:T(8,128)S(1)}, f32[192,128]{1,0:T(8,128)S(1)}, u32[]{:S(2)}, u32[]{:S(2)}) collective-permute-start(f32[192,128]{1,0:T(8,128)S(1)} %get-tuple-element.67), channel_id=1, source_target_pairs={{0,1},{1,0},{2,3},{3,2},{4,5},{5,4},{6,7},{7,6},{8,9},{9,8},{10,11... | collective-permute-start | bytes 294920 | tf_op jit(solution)/shard_map/ppermute | solution.py:425
  13.9 3.9 %collective-permute-start.3 = (f32[192,128]{1,0:T(8,128)S(1)}, f32[192,128]{1,0:T(8,128)S(1)}, u32[]{:S(2)}, u32[]{:S(2)}) collective-permute-start(f32[192,128]{1,0:T(8,128)S(1)} %get-tuple-element.68), channel_id=1, source_target_pairs={{0,1},{1,0},{2,3},{3,2},{4,5},{5,4},{6,7},{7,6},{8,9},{9,8},{10,11... | collective-permute-start | bytes 294920 | tf_op jit(solution)/shard_map/ppermute | solution.py:425
  14.0 3.8 %collective-permute-start.2 = (f32[192,128]{1,0:T(8,128)S(1)}, f32[192,128]{1,0:T(8,128)S(1)}, u32[]{:S(2)}, u32[]{:S(2)}) collective-permute-start(f32[192,128]{1,0:T(8,128)S(1)} %get-tuple-element.69), channel_id=1, source_target_pairs={{0,1},{1,0},{2,3},{3,2},{4,5},{5,4},{6,7},{7,6},{8,9},{9,8},{10,11... | collective-permute-start | bytes 294920 | tf_op jit(solution)/shard_map/ppermute | solution.py:425
  17.8 24.1 %copy-start.1 = (bf16[2,256,1008]{2,1,0:T(8,128)(2,1)S(1)}, bf16[2,256,1008]{2,1,0:T(8,128)(2,1)}, u32[]{:S(2)}) copy-start(bf16[2,256,1008]{2,1,0:T(8,128)(2,1)} %constant.45.clone.refs_2_) | copy-start | bytes 3096580
  17.8 24.1 %copy-start.2 = (bf16[2,336,768]{2,1,0:T(8,128)(2,1)S(1)}, bf16[2,336,768]{2,1,0:T(8,128)(2,1)}, u32[]{:S(2)}) copy-start(bf16[2,336,768]{2,1,0:T(8,128)(2,1)} %constant.46.clone.refs_3_) | copy-start | bytes 3096580
  59.8 1.5 collective-permute-start.7
  59.9 8.9 %collective-permute-start.6 = (bf16[784,128]{1,0:T(8,128)(2,1)S(1)}, bf16[784,128]{1,0:T(8,128)(2,1)S(1)}, u32[]{:S(2)}, u32[]{:S(2)}) collective-permute-start(bf16[784,128]{1,0:T(8,128)(2,1)S(1)} %shard_map.83.a_ref.refs_4_), channel_id=1, source_target_pairs={{0,2},{2,0},{1,3},{3,1},{4,6},{6,4},{5,7},{7,5},{8,10},{10,8},{9,1... | collective-permute-start | bytes 602120 | tf_op jit(solution)/shard_map/ppermute | solution.py:425
  68.8 1.4 collective-permute-start.8
  134.0 1.8 collective-permute-start.9
  135.9 8.9 %collective-permute-start.11 = (f32[4,192,128]{2,1,0:T(8,128)S(1)}, f32[4,192,128]{2,1,0:T(8,128)S(1)}, u32[]{:S(2)}, u32[]{:S(2)}) collective-permute-start(f32[4,192,128]{2,1,0:T(8,128)S(1)} %get-tuple-element.57), channel_id=1, source_target_pairs={{0,1},{1,0},{2,3},{3,2},{4,5},{5,4},{6,7},{7,6},{8,9},{9,8},{10,11... | collective-permute-start | bytes 1179656 | tf_op jit(solution)/shard_map/ppermute | solution.py:425
  136.1 8.7 %collective-permute-start.10 = (f16[4,192,128]{2,1,0:T(8,128)(2,1)S(1)}, f16[4,192,128]{2,1,0:T(8,128)(2,1)S(1)}, u32[]{:S(2)}, u32[]{:S(2)}) collective-permute-start(f16[4,192,128]{2,1,0:T(8,128)(2,1)S(1)} %multiply_convert_fusion), channel_id=1, source_target_pairs={{0,2},{2,0},{1,3},{3,1},{4,6},{6,4},{5,7},{7,5},{8,10},{10,8},{9,1... | collective-permute-start | bytes 589832 | tf_op jit(solution)/shard_map/ppermute | solution.py:425
  180.3 1.9 collective-permute-start.13
  180.4 8.9 %collective-permute-start.12 = (bf16[784,128]{1,0:T(8,128)(2,1)S(1)}, bf16[784,128]{1,0:T(8,128)(2,1)S(1)}, u32[]{:S(2)}, u32[]{:S(2)}) collective-permute-start(bf16[784,128]{1,0:T(8,128)(2,1)S(1)} %shard_map.93.a_ref.refs_4_), channel_id=1, source_target_pairs={{0,2},{2,0},{1,3},{3,1},{4,6},{6,4},{5,7},{7,5},{8,10},{10,8},{9,1... | collective-permute-start | bytes 602120 | tf_op jit(solution)/shard_map/ppermute | solution.py:425
  189.4 1.4 collective-permute-start.14

commit v7 on v6

--- a/solution.py
+++ b/solution.py
@@ -171,7 +171,8 @@
     starts = [pl.multiple_of(order_ref[pick] * block, HALF) for pick in picks]
     real = jnp.concatenate([r_ref[0, k, pl.ds(at, block), :] for at in starts], axis=0)
     imag = jnp.concatenate([r_ref[1, k, pl.ds(at, block), :] for at in starts], axis=0)
-    return jnp.dot(m, real, preferred_element_type=F32) + jnp.dot(n, imag, preferred_element_type=F32)
+    both = jnp.concatenate([real, imag], axis=0)
+    return jnp.dot(jnp.concatenate([m, n], axis=1), both, preferred_element_type=F32)
 
 
 def adjoint_first_kernel(order_ref, r_ref, a_ref, b_ref, o_ref):

time: 256 us -> 258 us (level)
  transfers between devices with their start and end apart: 15 -> 15, of which waited for: 9 -> 7; matrix products, arithmetic and copies ran while one was open for 0% -> 0% of each run, Pallas kernels for 5% -> 5%
where the time goes in v7:
time: 258 us; the launch traced here: 257 us
  blocking collectives  190 us (74%)
  Pallas kernels  31 us (12%)
  waiting for transfers between devices  22.7 us (9%)
  starting transfers between devices  5.93 us (2%)
  local copies, waits for them, and re-layouts  5.39 us (2%)
    all_to_all x8, blocking collectives, swap(): lax.all_to_all(values.astype(F16), 'freq', split_axis=0, concat_axis=0, t...  190 us
    ppermute x15, waiting for transfers between devices, step_to(): return lax.ppermute(values, 'rec', pairs)  22.7 us
    pallas_call x5, Pallas kernels, forward_call(): call(lambda *refs: forward_kernel(picks, *refs), [jax.ShapeDtypeStruct((b...  7.13 us
    pallas_call x4, Pallas kernels, window_call(): call(lambda *refs: window_kernel(from_source, *refs), jax.ShapeDtypeStruc...  6.58 us
    ppermute x15, starting transfers between devices, step_to(): return lax.ppermute(values, 'rec', pairs)  5.93 us
    unnamed x17, local copies, waits for them, and re-layouts  5.26 us
  transfers between devices with their start and end apart: 15, of which 7 were waited for; matrix products, arithmetic and copies ran while one was open for 0% of the time, Pallas kernels for 5%

profile of v7, /device:TPU:16, one launch (start us, length us, event | category | flops | bytes accessed | tf_op | source)
XLA Modules:
  0.0 257.5 jit_solution(7872846362986171033)
XLA Ops:
  0.7 1.5 copy.8
  2.2 0.1 stack.27.refs_0_.order_ref
  2.3 3.7 %copy-done = bf16[2,4,768,768]{3,2,1,0:T(8,128)(2,1)S(1)} copy-done((bf16[2,4,768,768]{3,2,1,0:T(8,128)(2,1)S(1)}, bf16[2,4,768,768]{3,2,1,0:T(8,128)(2,1)}, u32[]{:S(2)}) %copy-start) | copy-done | bytes 9437208
  6.0 1.3 shard_map.78
  7.3 0.1 collective-permute-start
  7.4 1.3 shard_map.77
  8.7 0.4 collective-permute-done
  9.2 2.2 collective-permute-start.1
  11.4 1.9 shard_map.79
  13.3 0.1 collective-permute-start.5
  13.4 0.5 collective-permute-start.4
  13.9 0.1 collective-permute-start.3
  14.0 0.4 collective-permute-start.2
  14.4 0.7 shard_map.80
  15.2 2.5 collective-permute-done.1
  17.9 0.3 shard_map.81
  18.1 0.1 convert_element_type.58
  18.2 23.7 %all_to_all.40 = f16[64,3,4,128]{3,2,1,0:T(4,128)(2,1)S(1)} all-to-all(f16[64,3,4,128]{3,2,1,0:T(4,128)(2,1)S(1)} %convert_element_type.58), channel_id=1, replica_groups=mesh['freq'=64,'rec'=4] {'freq'}, dimensions={0} | all-to-all | bytes 393216 | tf_op jit(solution)/shard_map/all_to_all | solution.py:423
  42.0 1.1 shard_map.82
  43.1 16.3 %all_to_all.41 = f16[64,8,256]{2,1,0:T(8,128)(2,1)S(1)} all-to-all(f16[64,8,256]{2,1,0:T(8,128)(2,1)S(1)} %convert_element_type.59), channel_id=1, replica_groups=mesh['freq'=64,'rec'=4] {'freq'}, dimensions={0} | all-to-all | bytes 524288 | tf_op jit(solution)/shard_map/all_to_all | solution.py:423
  59.5 0.2 shard_map.83.a_ref.refs_4_
  59.8 0.1 collective-permute-start.7
  59.9 0.7 collective-permute-start.6
  60.6 0.7 collective-permute-done.7.b_ref.refs_5_
  61.3 1.4 shard_map.84.total_ref
  62.7 6.1 %collective-permute-done.6.part_ref.refs_6_ = bf16[784,128]{1,0:T(8,128)(2,1)S(1)} collective-permute-done((bf16[784,128]{1,0:T(8,128)(2,1)S(1)}, bf16[784,128]{1,0:T(8,128)(2,1)S(1)}, u32[]{:S(2)}, u32[]{:S(2)}) %collective-permute-start.6) | collective-permute-done | bytes 200736 | tf_op jit(solution)/shard_map/ppermute | solution.py:426
  68.8 1.6 shard_map.85.refs_2_
  70.4 1.9 shard_map.86
  72.2 0.1 convert_element_type.61
  72.3 29.1 %all_to_all.42 = f16[64,8,768]{2,1,0:T(8,128)(2,1)S(1)} all-to-all(f16[64,8,768]{2,1,0:T(8,128)(2,1)S(1)} %convert_element_type.61), channel_id=1, replica_groups=mesh['freq'=64,'rec'=4] {'freq'}, dimensions={0} | all-to-all | bytes 1572864 | tf_op jit(solution)/shard_map/all_to_all | solution.py:423
  101.4 0.1 convert_element_type.62.refs_0_
  101.5 2.2 shard_map.87
  103.7 0.1 convert_element_type.63
  103.8 28.8 %all_to_all.43 = f16[64,8,768]{2,1,0:T(8,128)(2,1)S(1)} all-to-all(f16[64,8,768]{2,1,0:T(8,128)(2,1)S(1)} %convert_element_type.63), channel_id=1, replica_groups=mesh['freq'=64,'rec'=4] {'freq'}, dimensions={0} | all-to-all | bytes 1572864 | tf_op jit(solution)/shard_map/all_to_all | solution.py:423
  132.6 0.1 convert_element_type.64.refs_2_
  132.7 2.1 shard_map.88
  134.8 0.1 collective-permute-start.9
  134.9 1.3 shard_map.89
  136.2 0.4 collective-permute-done.9
  136.7 0.2 collective-permute-start.11
  136.9 0.7 collective-permute-start.10
  137.6 1.3 shard_map.90.kept_ref
  138.9 6.7 %collective-permute-done.10 = f16[4,192,128]{2,1,0:T(8,128)(2,1)S(1)} collective-permute-done((f16[4,192,128]{2,1,0:T(8,128)(2,1)S(1)}, f16[4,192,128]{2,1,0:T(8,128)(2,1)S(1)}, u32[]{:S(2)}, u32[]{:S(2)}) %collective-permute-start.10) | collective-permute-done | bytes 196640 | tf_op jit(solution)/shard_map/ppermute | solution.py:426
  145.7 0.3 shard_map.91
  146.0 0.1 convert_element_type.67
  146.1 16.8 %all_to_all.44 = f16[64,3,4,128]{3,2,1,0:T(4,128)(2,1)S(1)} all-to-all(f16[64,3,4,128]{3,2,1,0:T(4,128)(2,1)S(1)} %convert_element_type.67), channel_id=1, replica_groups=mesh['freq'=64,'rec'=4] {'freq'}, dimensions={0} | all-to-all | bytes 393216 | tf_op jit(solution)/shard_map/all_to_all | solution.py:423
  162.9 1.1 shard_map.92
  164.1 17.0 %all_to_all.45 = f16[64,8,256]{2,1,0:T(8,128)(2,1)S(1)} all-to-all(f16[64,8,256]{2,1,0:T(8,128)(2,1)S(1)} %convert_element_type.68), channel_id=1, replica_groups=mesh['freq'=64,'rec'=4] {'freq'}, dimensions={0} | all-to-all | bytes 524288 | tf_op jit(solution)/shard_map/all_to_all | solution.py:423
  181.1 0.2 shard_map.93.a_ref.refs_4_
  181.4 0.1 collective-permute-start.13
  181.5 0.7 collective-permute-start.12
  182.2 1.1 shard_map.95
  183.3 1.4 shard_map.94.total_ref
  184.6 5.8 %collective-permute-done.12.part_ref.refs_6_ = bf16[784,128]{1,0:T(8,128)(2,1)S(1)} collective-permute-done((bf16[784,128]{1,0:T(8,128)(2,1)S(1)}, bf16[784,128]{1,0:T(8,128)(2,1)S(1)}, u32[]{:S(2)}, u32[]{:S(2)}) %collective-permute-start.12) | collective-permute-done | bytes 200736 | tf_op jit(solution)/shard_map/ppermute | solution.py:426
  190.4 1.6 shard_map.96.refs_2_
  192.0 2.5 shard_map.97
  194.4 0.1 convert_element_type.70
  194.5 29.4 %all_to_all.46 = f16[64,8,768]{2,1,0:T(8,128)(2,1)S(1)} all-to-all(f16[64,8,768]{2,1,0:T(8,128)(2,1)S(1)} %convert_element_type.70), channel_id=1, replica_groups=mesh['freq'=64,'rec'=4] {'freq'}, dimensions={0} | all-to-all | bytes 1572864 | tf_op jit(solution)/shard_map/all_to_all | solution.py:423
  223.9 0.1 convert_element_type.71.refs_0_
  224.0 2.2 shard_map.98
  226.2 0.1 convert_element_type.72
  226.3 28.8 %all_to_all.47 = f16[64,8,768]{2,1,0:T(8,128)(2,1)S(1)} all-to-all(f16[64,8,768]{2,1,0:T(8,128)(2,1)S(1)} %convert_element_type.72), channel_id=1, replica_groups=mesh['freq'=64,'rec'=4] {'freq'}, dimensions={0} | all-to-all | bytes 1572864 | tf_op jit(solution)/shard_map/all_to_all | solution.py:423
  255.0 0.1 convert_element_type.73.x_ref
  255.2 2.1 shard_map.99
  (39 shorter events, 0.5 us)
Async XLA Ops:
  2.3 3.7 %copy-start = (bf16[2,4,768,768]{3,2,1,0:T(8,128)(2,1)S(1)}, bf16[2,4,768,768]{3,2,1,0:T(8,128)(2,1)}, u32[]{:S(2)}) copy-start(bf16[2,4,768,768]{3,2,1,0:T(8,128)(2,1)} %refs_1_.15) | copy-start | bytes 28311556
  6.0 5.4 %slice-start = ((s8[9437184]{0:T(1024)(128)(4,1)}), s8[4194304]{0:T(1024)(128)(4,1)S(1)}, s32[]{:S(2)}) async-start(s8[9437184]{0:T(1024)(128)(4,1)} %bitcast.22), calls=%async_computation.8 | async-start | bytes 8388608
  6.0 5.4 %slice-start.1 = ((s8[9437184]{0:T(1024)(128)(4,1)}), s8[4194304]{0:T(1024)(128)(4,1)S(1)}, s32[]{:S(2)}) async-start(s8[9437184]{0:T(1024)(128)(4,1)} %bitcast.22), calls=%async_computation.9 | async-start | bytes 8388608
  7.3 4.1 %slice-start.2 = ((s8[9437184]{0:T(1024)(128)(4,1)}), s8[1048576]{0:T(1024)(128)(4,1)S(1)}, s32[]{:S(2)}) async-start(s8[9437184]{0:T(1024)(128)(4,1)} %bitcast.22), calls=%async_computation.10 | async-start | bytes 2097152
  7.3 1.8 collective-permute-start
  9.2 5.3 %copy-start.3 = (s32[768,64]{0,1:T(8,128)S(1)}, s32[768,64]{0,1:T(8,128)}, u32[]{:S(2)}) copy-start(s32[768,64]{0,1:T(8,128)} %param.8) | copy-start | bytes 589828
  9.2 5.3 %copy-start.4 = (s32[768,64]{0,1:T(8,128)S(1)}, s32[768,64]{0,1:T(8,128)}, u32[]{:S(2)}) copy-start(s32[768,64]{0,1:T(8,128)} %param.9) | copy-start | bytes 589828
  9.2 8.5 %collective-permute-start.1 = (f16[4,192,128]{2,1,0:T(8,128)(2,1)S(1)}, f16[4,192,128]{2,1,0:T(8,128)(2,1)S(1)}, u32[]{:S(2)}, u32[]{:S(2)}) collective-permute-start(f16[4,192,128]{2,1,0:T(8,128)(2,1)S(1)} %multiply_convert_fusion.1), channel_id=1, source_target_pairs={{0,2},{2,0},{1,3},{3,1},{4,6},{6,4},{5,7},{7,5},{8,10},{10,8},{9,1... | collective-permute-start | bytes 589832 | tf_op jit(solution)/shard_map/ppermute | solution.py:426
  13.3 4.4 %collective-permute-start.5 = (f32[192,128]{1,0:T(8,128)S(1)}, f32[192,128]{1,0:T(8,128)S(1)}, u32[]{:S(2)}, u32[]{:S(2)}) collective-permute-start(f32[192,128]{1,0:T(8,128)S(1)} %get-tuple-element.66), channel_id=1, source_target_pairs={{0,1},{1,0},{2,3},{3,2},{4,5},{5,4},{6,7},{7,6},{8,9},{9,8},{10,11... | collective-permute-start | bytes 294920 | tf_op jit(solution)/shard_map/ppermute | solution.py:426
  13.4 4.4 %collective-permute-start.4 = (f32[192,128]{1,0:T(8,128)S(1)}, f32[192,128]{1,0:T(8,128)S(1)}, u32[]{:S(2)}, u32[]{:S(2)}) collective-permute-start(f32[192,128]{1,0:T(8,128)S(1)} %get-tuple-element.67), channel_id=1, source_target_pairs={{0,1},{1,0},{2,3},{3,2},{4,5},{5,4},{6,7},{7,6},{8,9},{9,8},{10,11... | collective-permute-start | bytes 294920 | tf_op jit(solution)/shard_map/ppermute | solution.py:426
  13.9 3.9 %collective-permute-start.3 = (f32[192,128]{1,0:T(8,128)S(1)}, f32[192,128]{1,0:T(8,128)S(1)}, u32[]{:S(2)}, u32[]{:S(2)}) collective-permute-start(f32[192,128]{1,0:T(8,128)S(1)} %get-tuple-element.68), channel_id=1, source_target_pairs={{0,1},{1,0},{2,3},{3,2},{4,5},{5,4},{6,7},{7,6},{8,9},{9,8},{10,11... | collective-permute-start | bytes 294920 | tf_op jit(solution)/shard_map/ppermute | solution.py:426
  14.0 3.8 %collective-permute-start.2 = (f32[192,128]{1,0:T(8,128)S(1)}, f32[192,128]{1,0:T(8,128)S(1)}, u32[]{:S(2)}, u32[]{:S(2)}) collective-permute-start(f32[192,128]{1,0:T(8,128)S(1)} %get-tuple-element.69), channel_id=1, source_target_pairs={{0,1},{1,0},{2,3},{3,2},{4,5},{5,4},{6,7},{7,6},{8,9},{9,8},{10,11... | collective-permute-start | bytes 294920 | tf_op jit(solution)/shard_map/ppermute | solution.py:426
  17.8 24.1 %copy-start.1 = (bf16[2,256,1008]{2,1,0:T(8,128)(2,1)S(1)}, bf16[2,256,1008]{2,1,0:T(8,128)(2,1)}, u32[]{:S(2)}) copy-start(bf16[2,256,1008]{2,1,0:T(8,128)(2,1)} %constant.45.clone.refs_2_) | copy-start | bytes 3096580
  17.8 24.1 %copy-start.2 = (bf16[2,336,768]{2,1,0:T(8,128)(2,1)S(1)}, bf16[2,336,768]{2,1,0:T(8,128)(2,1)}, u32[]{:S(2)}) copy-start(bf16[2,336,768]{2,1,0:T(8,128)(2,1)} %constant.46.clone.refs_3_) | copy-start | bytes 3096580
  59.8 1.5 collective-permute-start.7
  59.9 8.9 %collective-permute-start.6 = (bf16[784,128]{1,0:T(8,128)(2,1)S(1)}, bf16[784,128]{1,0:T(8,128)(2,1)S(1)}, u32[]{:S(2)}, u32[]{:S(2)}) collective-permute-start(bf16[784,128]{1,0:T(8,128)(2,1)S(1)} %shard_map.83.a_ref.refs_4_), channel_id=1, source_target_pairs={{0,2},{2,0},{1,3},{3,1},{4,6},{6,4},{5,7},{7,5},{8,10},{10,8},{9,1... | collective-permute-start | bytes 602120 | tf_op jit(solution)/shard_map/ppermute | solution.py:426
  68.8 1.6 collective-permute-start.8
  134.8 1.8 collective-permute-start.9
  136.7 8.9 %collective-permute-start.11 = (f32[4,192,128]{2,1,0:T(8,128)S(1)}, f32[4,192,128]{2,1,0:T(8,128)S(1)}, u32[]{:S(2)}, u32[]{:S(2)}) collective-permute-start(f32[4,192,128]{2,1,0:T(8,128)S(1)} %get-tuple-element.57), channel_id=1, source_target_pairs={{0,1},{1,0},{2,3},{3,2},{4,5},{5,4},{6,7},{7,6},{8,9},{9,8},{10,11... | collective-permute-start | bytes 1179656 | tf_op jit(solution)/shard_map/ppermute | solution.py:426
  136.9 8.7 %collective-permute-start.10 = (f16[4,192,128]{2,1,0:T(8,128)(2,1)S(1)}, f16[4,192,128]{2,1,0:T(8,128)(2,1)S(1)}, u32[]{:S(2)}, u32[]{:S(2)}) collective-permute-start(f16[4,192,128]{2,1,0:T(8,128)(2,1)S(1)} %multiply_convert_fusion), channel_id=1, source_target_pairs={{0,2},{2,0},{1,3},{3,1},{4,6},{6,4},{5,7},{7,5},{8,10},{10,8},{9,1... | collective-permute-start | bytes 589832 | tf_op jit(solution)/shard_map/ppermute | solution.py:426
  181.4 1.9 collective-permute-start.13
  181.5 8.9 %collective-permute-start.12 = (bf16[784,128]{1,0:T(8,128)(2,1)S(1)}, bf16[784,128]{1,0:T(8,128)(2,1)S(1)}, u32[]{:S(2)}, u32[]{:S(2)}) collective-permute-start(bf16[784,128]{1,0:T(8,128)(2,1)S(1)} %shard_map.93.a_ref.refs_4_), channel_id=1, source_target_pairs={{0,2},{2,0},{1,3},{3,1},{4,6},{6,4},{5,7},{7,5},{8,10},{10,8},{9,1... | collective-permute-start | bytes 602120 | tf_op jit(solution)/shard_map/ppermute | solution.py:426
  190.4 1.6 collective-permute-start.14
